TPU v7x, 128 devices: a whole 4x4x4 slice. The times are simulated.
128 devices in a mesh: walk: 4 (over x), chol: 32 (over y, z, core).
Axes of the slice: x: 4, y: 4, z: 4, core: 2. Of those that a mesh axis runs over, the one named last changes fastest.
Arguments:
- walkers: bfloat16 [16, 640, 200], P('walk'), as said below
- trial: bfloat16 [640, 200], replicated
- half_chol: bfloat16 [1792, 640, 200], P('chol', 'walk'), may hold values from -0.3984375 to 0.3984375
- chol_vectors: bfloat16 [1792, 640, 640], P('chol', 'walk'), may hold values from -0.001953125 to 0.001953125
- noise: float32 [16, 1792], P('walk', 'chol'), may hold values from -6 to 6
- copies: int32 [16], replicated, may hold values from 0 to 12, as said below
Outputs:
- new_walkers: bfloat16 [16, 640, 200], P('walk')
- energies: float32 [16], P('walk')
Inputs may be any that keep to these rules, and one draw needn't show every extreme that they name: copies sum to 16; exactly one walker, one of the first 4, has the most copies; every walker before it has one copy, every other walker one or none. trial^T walkers[w] is invertible for every walker.
All inputs are finite; a program needn't handle non-finite values.
Results may differ from a plain program's by a relative error of at most 0.0084.
Values may be sent and summed in bfloat16 or wider, within the bound.
No kernel may reach another device: no remote copies, remote signals or barrier semaphores. Data moves between devices by JAX's collectives and lax.ppermute only.
A program may use at most 256 MiB of HBM per device.

v0:
```python
import jax
import jax.numpy as jnp
from jax import lax
from jax.sharding import PartitionSpec as P

TERMS = 4


def make_theta(walkers, trial):
    correlation = jnp.einsum("rn,wrm->wnm", trial, walkers, preferred_element_type=jnp.float32)
    gram = jnp.einsum("wkn,wkm->wnm", correlation, correlation, precision=lax.Precision.HIGHEST)
    factor = jnp.linalg.cholesky(gram)
    inverse = jax.vmap(lambda f, o: jax.scipy.linalg.cho_solve((f, True), o.T))(factor, correlation)
    wide = walkers.astype(jnp.float32)
    return jnp.einsum("wrn,wnm->wrm", wide, inverse, precision=lax.Precision.HIGHEST).astype(
        jnp.bfloat16
    )


def shards(walkers, trial, half_chol, chol_vectors, noise, copies):
    groups = lax.axis_size("walk")
    slabs = lax.axis_size("chol")
    w_grp, n_orb, n_occ = walkers.shape
    ch_dev = half_chol.shape[0]
    theta = make_theta(walkers, trial)
    rows = theta
    pairs = lax.dot_general(
        lax.all_gather(half_chol, "walk", axis=1, tiled=True),
        rows,
        (((1,), (1,)), ((), ())),
        preferred_element_type=jnp.float32,
    )
    bias = jnp.einsum("giwi->wg", pairs)
    field = (noise - 0.5 * bias).astype(jnp.bfloat16)
    all_fields = lax.all_gather(field, "walk", axis=0, tiled=True)
    rows = chol_vectors.shape[1]
    partial_value = jnp.dot(
        all_fields, chol_vectors.reshape(ch_dev, rows * n_orb), preferred_element_type=jnp.float32
    )
    partial_value = partial_value.reshape(w_grp * groups, rows, n_orb)
    sent = lax.all_to_all(partial_value, "walk", split_axis=0, concat_axis=1, tiled=True)
    potential = lax.psum(sent, "chol").astype(jnp.bfloat16)
    cross = jnp.einsum("giwj,gjwi->wg", pairs, pairs)
    local = jnp.sum(0.5 * bias * bias - 0.5 * cross, axis=1)
    energies = lax.psum(local, "chol") / (ch_dev * slabs)
    term = walkers
    total = walkers.astype(jnp.float32)
    for k in range(1, TERMS + 1):
        term = (
            jnp.einsum("wrs,wsn->wrn", potential, term, preferred_element_type=jnp.float32) / k
        ).astype(jnp.bfloat16)
        total = total + term.astype(jnp.float32)
    propagated = total.astype(jnp.bfloat16)
    width = n_orb * n_occ // slabs
    flat = propagated.reshape(w_grp, n_orb * n_occ)
    mine = lax.dynamic_slice_in_dim(flat, lax.axis_index("chol") * width, width, 1)
    everyone = lax.all_gather(mine, "walk", axis=0, tiled=True)
    ends = jnp.cumsum(copies)
    starts = ends - copies
    slots = lax.axis_index("walk") * w_grp + jnp.arange(w_grp, dtype=jnp.int32)
    picker = ((starts[None, :] <= slots[:, None]) & (slots[:, None] < ends[None, :])).astype(
        jnp.bfloat16
    )
    chosen = jnp.dot(picker, everyone, preferred_element_type=jnp.float32).astype(jnp.bfloat16)
    rebuilt = lax.all_gather(chosen, "chol", axis=1, tiled=True)
    return (rebuilt.reshape(w_grp, n_orb, n_occ), energies)


def solution(mesh):
    placed = (
        P("walk", None, None),
        P(),
        P("chol", "walk", None),
        P("chol", "walk", None),
        P("walk", "chol"),
        P(),
    )
    return jax.shard_map(
        shards,
        mesh=mesh,
        in_specs=placed,
        out_specs=(P("walk", None, None), P("walk")),
        check_vma=False,
    )
```

profile of v0, /device:TPU:0, one launch (start us, length us, event | category | flops | bytes accessed | tf_op | source)
XLA Modules:
  0.0 652.7 jit_solution(12248328004704664661)
XLA Ops:
  7.2 0.0 copy-start
  7.2 0.0 all-gather.5.cloned.1.call-start
  7.2 0.7 all-gather.5.cloned.1.call-update
  7.9 0.2 copy-done
  8.1 0.4 copy-done.2
  8.5 0.5 fusion.18
  9.0 0.9 fusion.37
  10.0 1.2 copy.42
  11.2 1.3 fusion.12
  12.5 0.9 copy-done.4
  13.4 46.9 %custom-call.20 = f32[4,128,128]{2,1,0:T(8,128)S(1)} custom-call(f32[4,128,128]{2,1,0:T(8,128)S(1)} %cholesky.129), custom_call_target="Cholesky" | custom-call | tf_op jit(solution)/shard_map/jit(cholesky)/cholesky | solution.py:12
  60.3 0.1 cholesky.124
  60.4 0.1 select_reduce_fusion
  60.5 39.3 %custom-call.21 = f32[4,1,128,128]{2,3,1,0:T(8,128)S(1)} custom-call(f32[4,1,128,128]{3,2,1,0:T(8,128)S(1)} %get-tuple-element.31), custom_call_target="InvertDiagBlocksLowerTriangular" | custom-call | tf_op jit(solution)/shard_map/jit(cholesky)/cholesky | solution.py:12
  99.8 1.3 constant_dynamic-update-slice_fusion.1
  101.1 1.3 convolution_subtract_fusion.2
  102.4 26.4 %custom-call.22 = f32[4,72,72]{2,1,0:T(8,128)S(1)} custom-call(f32[4,72,72]{2,1,0:T(8,128)S(1)} %convolution_subtract_fusion.2), custom_call_target="Cholesky" | custom-call | tf_op jit(solution)/shard_map/jit(cholesky)/cholesky | solution.py:12
  128.9 0.1 compare_reduce_fusion.1
  129.0 0.1 compare_reduce_fusion
  129.2 0.2 select_select_fusion
  129.4 0.0 copy-start.3
  129.5 0.1 fusion.15
  129.6 0.7 copy-done.3
  130.3 0.8 pad_maximum_fusion
  131.1 79.6 %custom-call.23 = f32[4,2,128,128]{2,3,1,0:T(8,128)S(1)} custom-call(f32[4,2,128,128]{3,2,1,0:T(8,128)} %pad_maximum_fusion), custom_call_target="InvertDiagBlocksLowerTriangular" | custom-call | tf_op jit(solution)/shard_map/vmap(jit(_cho_solve))/triangular_solve | solution.py:13
  210.7 1.1 fusion.13
  211.9 1.8 convolution_subtract_fusion.1
  213.7 0.4 fusion.23
  214.2 0.4 fusion.22
  214.6 0.2 copy.49
  214.8 1.8 convolution_subtract_fusion
  216.6 0.8 fusion.20
  217.4 1.1 fusion.8
  218.5 0.0 all-gather.5.cloned.1.call-done
  218.6 29.3 %fusion.1 = (f32[56,4]{0,1:T(4,128)S(1)}, f32[4,200,56,200]{3,1,2,0:T(8,128)}) fusion(pred[200,200]{0,1:T(8,128)(4,1)S(1)} %iota_compare_fusion.2, bf16[4,640,200,1]{1,2,3,0:T(8,128)(2,1)S(1)} %fusion.8, bf16[56,640,200]{2,1,0:T(8,128)(2,1)} %all-gather.5.cloned.1.call-done), kind=kOutput, calls=%fused_computation.3 | convolution fusion | flops 11486720000 | bytes 51240896 | tf_op jit(solution)/shard_map/dot_general | solution.py:27
  247.9 47.4 %copy.67 = f32[4,56,200,200]{3,2,1,0:T(8,128)} copy(f32[4,56,200,200]{2,3,1,0:T(8,128)} %bitcast.107) | data formatting | bytes 71680000
  295.2 28.3 %fusion = f32[4,56]{1,0:T(4,128)S(1)} fusion(f32[4,56,200,200]{3,2,1,0:T(8,128)} %copy.67, f32[4,200,56,200]{3,1,2,0:T(8,128)} %get-tuple-element.39), kind=kLoop, calls=%fused_computation.1 | loop fusion | flops 17919776 | bytes 71680896 | tf_op jit(solution)/shard_map/giwj,gjwi->wg/dot_general | solution.py:43
  323.5 0.1 fusion.28
  323.7 9.8 %all-gather = bf16[4,4,56]{2,1,0:T(4,128)(2,1)S(1)} all-gather(bf16[1,4,56]{2,1,0:T(4,128)(2,1)S(1)} %get-tuple-element.35), channel_id=1, replica_groups=mesh['walk'=4,'chol'=32] {'walk'}, dimensions={0}, use_global_device_ids=true | all-gather | bytes 2240 | tf_op jit(solution)/shard_map/all_gather | solution.py:35
  333.4 13.0 %fusion.4 = f32[16,160,640]{2,0,1:T(8,128)S(1)} fusion(bf16[16,56,1]{1,0,2:T(8,128)(2,1)S(1)} %bitcast.111, bf16[7,8,160,640]{3,2,1,0:T(8,128)(2,1)} %bitcast.109), kind=kOutput, calls=%fused_computation.6 | convolution fusion | flops 183500800 | bytes 18024192 | tf_op jit(solution)/shard_map/dot_general | solution.py:37
  346.5 4.7 copy.51
  351.2 5.4 all-to-all-start
  356.6 0.0 copy-done.6
  356.6 0.1 copy.41
  356.8 0.1 reduce.13
  356.9 72.1 %all-to-all-done = f32[16,160,640]{2,1,0:T(8,128)} async-done(((f32[16,160,640]{2,1,0:T(8,128)}), f32[16,160,640]{2,1,0:T(8,128)}, u32[]{:S(2)}, u32[]{:S(2)}) %all-to-all-start) | async-done | bytes 6553632 | tf_op jit(solution)/shard_map/all_to_all | solution.py:41
  429.0 6.0 copy.52
  435.1 154.2 %all-reduce.5 = (bf16[4,640,640]{2,1,0:T(8,128)(2,1)}, f32[4]{0:T(128)S(1)}) all-reduce(f32[4,640,640]{2,1,0:T(8,128)} %bitcast.108, f32[4]{0:T(128)S(1)} %get-tuple-element.34), channel_id=1, replica_groups=mesh['walk'=4,'chol'=32] {'chol'}, use_global_device_ids=true, to_apply=%region_6.7 | all-reduce | flops 1638404 | bytes 9830432 | tf_op jit(solution)/shard_map/psum | solution.py:42
  589.3 3.5 convolution_convert_fusion.1
  592.7 0.0 copy-done.7
  592.7 1.4 multiply_convert_fusion.2
  594.1 1.4 multiply_convert_fusion.1
  595.5 2.5 add_convert_fusion
  598.0 1.5 copy.53
  599.6 3.5 reshape.83
  603.1 0.1 dynamic-slice_bitcast_fusion
  603.2 12.0 %all-gather.1 = bf16[4,4,4000]{2,1,0:T(4,128)(2,1)S(1)} all-gather(bf16[1,4,4000]{2,1,0:T(4,128)(2,1)S(1)} %dynamic-slice_bitcast_fusion), channel_id=1, replica_groups=mesh['walk'=4,'chol'=32] {'walk'}, dimensions={0}, use_global_device_ids=true | all-gather | bytes 160000 | tf_op jit(solution)/shard_map/all_gather | solution.py:57
  615.2 0.2 fusion.7
  615.4 22.2 %all-gather.2 = bf16[32,4000,4]{1,2,0:T(4,128)(2,1)S(1)} all-gather(bf16[1,4000,4]{1,2,0:T(4,128)(2,1)S(1)} %fusion.7), channel_id=1, replica_groups=mesh['walk'=4,'chol'=32] {'chol'}, dimensions={0}, use_global_device_ids=true | all-gather | bytes 1056000 | tf_op jit(solution)/shard_map/all_gather | solution.py:65
  637.6 0.6 copy.54
  638.2 1.6 reshape.123
  639.8 4.0 reshape.84
  643.8 1.4 copy.55
  645.1 0.5 broadcast_multiply_fusion
  (24 shorter events, 0.3 us)
Async XLA Ops:
  7.2 1.0 copy-start
  7.2 1.4 copy-start.2
  7.2 211.4 %all-gather.5.cloned.1.call-start = ((), (), s32[]{:S(2)}) async-start(), calls=%async_computation.1 | async-start | bytes 22937600 | tf_op jit(solution)/shard_map/all_gather | solution.py:28
  12.5 0.9 copy-start.4
  129.4 0.9 copy-start.3
  295.2 28.3 %copy-start.5 = (f32[4,56]{1,0:T(4,128)S(1)}, f32[4,56]{1,0:T(4,128)}, u32[]{:S(2)}) copy-start(f32[4,56]{1,0:T(4,128)} %param.10) | copy-start | bytes 2692
  351.2 5.5 copy-start.6
  351.2 77.8 %all-to-all-start = ((f32[16,160,640]{2,1,0:T(8,128)}), f32[16,160,640]{2,1,0:T(8,128)}, u32[]{:S(2)}, u32[]{:S(2)}) async-start(f32[16,160,640]{2,1,0:T(8,128)} %copy.51), calls=%async_computation | async-start | bytes 13107200 | tf_op jit(solution)/shard_map/all_to_all | solution.py:41
  589.3 3.5 copy-start.7
  637.6 8.0 %copy-start.1 = (bf16[640,200]{0,1:T(8,128)(2,1)S(1)}, bf16[640,200]{0,1:T(8,128)(2,1)}, u32[]{:S(2)}) copy-start(bf16[640,200]{0,1:T(8,128)(2,1)} %param.7) | copy-start | bytes 768004
Sparse Core Ops, SparseCore 0:
  9.7 170.6 all-gather.4
where the time goes:
time: 664 us; the launch traced here: 653 us
  other arithmetic  224 us (34%)
  blocking collectives  198 us (30%)
  local copies, waits for them, and re-layouts  74.6 us (11%)
  waiting for transfers between devices  72.8 us (11%)
  matrix products  62.9 us (9%)
  between operations  14.6 us (2%)
    psum x1, blocking collectives, shards(): potential = lax.psum(sent, 'chol').astype(jnp.bfloat16)  154 us
    another operation x10, other arithmetic, make_theta(): factor = jnp.linalg.cholesky(gram)  113 us
    another operation x7, other arithmetic, make_theta(): jax.scipy.linalg.cho_solve((f, True), o.T)  80.8 us
    all_to_all x1, waiting for transfers between devices, shards(): lax.all_to_all(partial_value, 'walk', split_axis=0, concat_axis=1, tiled=...  72.1 us
    unnamed x21, local copies, waits for them, and re-layouts  52.6 us
    dot_general x1, matrix products, shards(): lax.dot_general(lax.all_gather(half_chol, 'walk', axis=1, tiled=True), ro...  29.3 us
    dot_general x1, other arithmetic, shards(): cross = jnp.einsum('giwj,gjwi->wg', pairs, pairs)  28.3 us
    all_gather x1, blocking collectives, shards(): rebuilt = lax.all_gather(chosen, 'chol', axis=1, tiled=True)  22.2 us
  transfers between devices with their start and end apart: 2, of which 1 were waited for; matrix products, arithmetic and copies ran while one was open for 32% of the time, Pallas kernels for 0%

commit v1 on v0

v1 whole, which is shorter than its diff:
```python
import functools

import jax
import jax.numpy as jnp
from jax import lax
from jax.experimental import pallas as pl
from jax.experimental.pallas import tpu as pltpu
from jax.sharding import Mesh, PartitionSpec as P

TERMS = 4
BF = jnp.bfloat16
F32 = jnp.float32
HIGH = lax.Precision.HIGHEST
VMEM_LIMIT = 56 * 1024 * 1024
SMEM = pl.BlockSpec(memory_space=pltpu.SMEM)
VMEM = pl.BlockSpec(memory_space=pltpu.VMEM)


def params(**more):
    return pltpu.CompilerParams(vmem_limit_bytes=VMEM_LIMIT, **more)


def cost(flops, moved):
    return pl.CostEstimate(flops=int(flops), bytes_accessed=int(moved), transcendentals=0)


def mm(a, b, dims=((1,), (0,)), precision=None):
    return lax.dot_general(
        a, b, (dims, ((), ())), precision=precision, preferred_element_type=F32
    )


def shift(n, k):
    return [(q, (q + k) % n) for q in range(n)]


def theta_kernel(n, place, trial, walkers, *rest):
    own = rest[:n]
    others = rest[n : 2 * n - 1]
    c_ref, s_ref, x_ref = rest[2 * n - 1 :]
    x_at, core = place[0], place[3]
    pair = own[0].shape[0]
    rows = own[0].shape[1]
    n_occ = trial.shape[1]
    ids = [lax.broadcasted_iota(jnp.int32, (n_occ, n_occ), d) for d in (0, 1)]
    eye = (ids[0] == ids[1]).astype(F32)
    for i in range(pair):
        w = walkers[pair * core + i]
        c = mm(trial[...], w, ((0,), (0,)))
        ct = mm(w, trial[...], ((0,), (0,)))
        c_ref[i] = c
        g = jnp.abs(mm(c.astype(BF), ct.astype(BF)))
        side = jnp.max(jnp.sum(jnp.abs(c), axis=0)) * jnp.max(jnp.sum(jnp.abs(ct), axis=0))
        bound = jnp.max(jnp.sum(g, axis=0)) * 1.01 + side / 128.0
        start = ct * (1.9 / jnp.full(ct.shape, bound, F32))
        s_ref[i] = start
        x_ref[i] = start

    def coarse(state):
        step, _ = state
        xs = [x_ref[i] for i in range(pair)]
        rs = [eye - mm(c_ref[i].astype(BF), xs[i].astype(BF)) for i in range(pair)]
        for i in range(pair):
            x_ref[i] = xs[i] + mm(xs[i].astype(BF), rs[i].astype(BF))
        worst = sum(jnp.sum(r * r) for r in rs)
        return step + 1, worst

    def fine(state):
        step, _ = state
        xs = [x_ref[i] for i in range(pair)]
        rs = [eye - mm(c_ref[i], xs[i], precision=HIGH) for i in range(pair)]
        bs = [r.astype(BF) for r in rs]
        twos = [(rs[i] + mm(bs[i], bs[i])).astype(BF) for i in range(pair)]
        for i in range(pair):
            x_ref[i] = xs[i] + mm(xs[i].astype(BF), twos[i])
        worst = sum(jnp.sum(r * r) for r in rs)
        return step + 1, worst

    def far(limit, tolerance):
        return lambda state: (state[0] < limit) & jnp.logical_not(state[1] < tolerance)

    begin = (jnp.int32(0), jnp.float32(1e30))
    lax.while_loop(far(14, 0.3), coarse, begin)
    _, left = lax.while_loop(far(6, 0.005), fine, begin)

    @pl.when(jnp.logical_not(left < 0.005))
    def _():
        x_ref[...] = s_ref[...]
        lax.while_loop(far(60, 0.005), fine, begin)

    for i in range(pair):
        inv = x_ref[i]
        high = inv.astype(BF)
        low = (inv - high.astype(F32)).astype(BF)
        for j in range(n):
            block = lax.rem(x_at + j, n)
            w = walkers[pair * core + i, pl.ds(pl.multiple_of(block * rows, rows), rows), :]
            theta = (mm(w, high) + mm(w, low)).astype(BF)
            own[j][i] = theta
            for k in range(1, n):
                if j != k:
                    others[k - 1][j - (j > k), i] = theta


def make_theta(place, trial, walkers, n):
    _, n_orb, n_occ = walkers.shape
    rows = n_orb // n
    pair = walkers.shape[0] // 2
    small = jax.ShapeDtypeStruct((pair, rows, n_occ), BF)
    big = jax.ShapeDtypeStruct((n - 1, pair, rows, n_occ), BF)
    return pl.pallas_call(
        functools.partial(theta_kernel, n),
        out_shape=[small] * n + [big] * (n - 1),
        in_specs=[SMEM, VMEM, VMEM],
        out_specs=[VMEM] * (2 * n - 1),
        scratch_shapes=[pltpu.VMEM((pair, n_occ, n_occ), F32)] * 3,
        compiler_params=params(),
        cost_estimate=cost(1e10, 4e6),
        name="theta",
    )(place, trial, walkers)


def bias_kernel(n, place, half, noise, *rest):
    thetas = rest[: 2 * n]
    out, t_ref = rest[2 * n :]
    x_at, core = place[0], place[3]
    pair, rows, n_occ = thetas[0].shape
    lanes = 16
    walkers = 2 * n * pair
    chunks = rows // lanes
    step = pl.program_id(0)
    block = half.shape[0]
    n_vec = out.shape[1] // 2

    @pl.when(step == 0)
    def _():
        for l in range(walkers):
            t_ref[:, l * lanes : (l + 1) * lanes, :] = thetas[l // pair][l % pair].reshape(
                chunks, lanes, n_occ
            )
        out[...] = jnp.zeros(out.shape, F32)
        group = lax.broadcasted_iota(jnp.int32, (noise.shape[0], walkers), 0) + 2 * pair * x_at
        column = lax.broadcasted_iota(jnp.int32, (noise.shape[0], walkers), 1)
        out[1, pl.ds(pl.multiple_of(core * n_vec, 8), n_vec), :] = mm(
            noise[...], (group == column).astype(F32), ((0,), (0,)), HIGH
        )

    total = jnp.zeros((block * lanes, walkers * lanes), F32)
    for c in range(chunks):
        rows_c = half[:, c * lanes : (c + 1) * lanes, :].reshape(block * lanes, n_occ)
        total = total + mm(rows_c, t_ref[c], ((1,), (1,)))
    r0 = lax.broadcasted_iota(jnp.int32, total.shape, 0) % lanes
    r1 = lax.broadcasted_iota(jnp.int32, total.shape, 1) % lanes
    kept = jnp.where(r0 == r1, total, 0.0).reshape(block, lanes, walkers * lanes)
    per = jnp.sum(kept, axis=1)
    lane = lax.broadcasted_iota(jnp.int32, (walkers * lanes, walkers), 0) // lanes
    source = lane // pair
    k = source % n
    c = jnp.where(source < n, core, 1 - core)
    walker = 2 * pair * ((x_at - k + n) % n) + pair * c + lane % pair
    column = lax.broadcasted_iota(jnp.int32, (walkers * lanes, walkers), 1)
    picked = mm(per, (walker == column).astype(F32), precision=HIGH)
    out[0, pl.ds(pl.multiple_of(core * n_vec + step * block, 8), block), :] = picked


def make_bias(place, half, noise, thetas, n):
    n_vec, rows, n_occ = half.shape
    pair = thetas[0].shape[0]
    walkers = 2 * n * pair
    block = 8
    return pl.pallas_call(
        functools.partial(bias_kernel, n),
        out_shape=jax.ShapeDtypeStruct((2, 2 * n_vec, walkers), F32),
        grid=(n_vec // block,),
        in_specs=[SMEM, pl.BlockSpec((block, rows, n_occ), lambda s: (s, 0, 0)), VMEM]
        + [VMEM] * (2 * n),
        out_specs=VMEM,
        scratch_shapes=[pltpu.VMEM((rows // 16, walkers * 16, n_occ), BF)],
        compiler_params=params(),
        cost_estimate=cost(4e9, 8e6),
        name="bias",
    )(place, half, noise, *thetas)


def potential_kernel(n, place, summed, picker, mine, theirs, *rest):
    outs = rest[:n]
    (a_ref,) = rest[n:]
    core = place[3]
    n_vec, lanes, n_orb = mine.shape
    slots = picker.shape[0]

    @pl.when(pl.program_id(0) == 0)
    def _():
        field = (summed[1] - 0.5 * summed[0]).astype(BF)
        chosen = mm(picker[...], field, ((1,), (1,))).astype(BF)
        vec = lax.broadcasted_iota(jnp.int32, (n_vec, n_vec * lanes), 0)
        lane = lax.broadcasted_iota(jnp.int32, (n_vec, n_vec * lanes), 1)
        spread = (lane // lanes == vec).astype(F32).astype(BF)
        sub = lax.broadcasted_iota(jnp.int32, (lanes, n_vec * lanes), 0)
        along = lax.broadcasted_iota(jnp.int32, (lanes, n_vec * lanes), 1) % lanes
        same = (sub == along).astype(F32)
        for c in range(2):
            wide = mm(chosen[:, c * n_vec : (c + 1) * n_vec], spread)
            for s in range(slots):
                a_ref[c, s * lanes : (s + 1) * lanes, :] = (same * wide[s : s + 1, :]).astype(BF)

    got = mm(a_ref[core], mine[...].reshape(n_vec * lanes, n_orb)) + mm(
        a_ref[1 - core], theirs[...].reshape(n_vec * lanes, n_orb)
    )
    got = got.astype(BF).reshape(slots, lanes, n_orb)
    each = slots // n
    for k in range(n):
        outs[k][...] = got[k * each : (k + 1) * each]


def make_potential(place, summed, picker, mine, theirs, n):
    n_vec, rows, n_orb = mine.shape
    slots = picker.shape[0]
    half = rows // 2
    lanes = 16
    steps = half // lanes
    rows_of = pl.BlockSpec((n_vec, lanes, n_orb), lambda s, p: (0, p[3] * steps + s, 0))
    whole = pl.BlockSpec(memory_space=pltpu.VMEM)
    return pl.pallas_call(
        functools.partial(potential_kernel, n),
        out_shape=[jax.ShapeDtypeStruct((slots // n, half, n_orb), BF)] * n,
        grid_spec=pltpu.PrefetchScalarGridSpec(
            num_scalar_prefetch=1,
            grid=(steps,),
            in_specs=[whole, whole, rows_of, rows_of],
            out_specs=[pl.BlockSpec((slots // n, lanes, n_orb), lambda s, p: (0, s, 0))] * n,
            scratch_shapes=[pltpu.VMEM((2, slots * lanes, n_vec * lanes), BF)],
        ),
        compiler_params=params(),
        cost_estimate=cost(4e9, 1.5e7),
        name="potential",
    )(place, summed, picker, mine, theirs)


def cross_kernel(n, pieces, place, *rest):
    k = pieces[0]
    halves = rest[: 2 * n]
    n_theta = len(pieces[1])
    thetas = rest[2 * n : 2 * n + n_theta]
    out, h_ref, t_ref, acc = rest[2 * n + n_theta :]
    x_at = place[0]
    rows, n_occ = halves[0].shape[1:]
    pair = acc.shape[0]
    step = pl.program_id(0)

    def at(block):
        return pl.ds(pl.multiple_of(lax.rem(block, n) * rows, rows), rows)

    @pl.when(step == 0)
    def _():
        acc[...] = jnp.zeros(acc.shape, F32)
        for i in range(pair):
            for ref, part in zip(thetas, pieces[1]):
                for place_in, j in part:
                    block = ref[i] if place_in is None else ref[place_in, i]
                    h_ref[at(x_at - k + n + j), :] = block
            t_ref[i * n_occ : (i + 1) * n_occ, :] = h_ref[...].astype(F32).T.astype(BF)

    for side in range(2):
        for s in range(n):
            h_ref[at(x_at - s + n), :] = halves[side * n + s][0]
        got = mm(t_ref[...], h_ref[...])
        for i in range(pair):
            p = got[i * n_occ : (i + 1) * n_occ].astype(BF)
            acc[i] += mm(p, p)

    @pl.when(step == pl.num_programs(0) - 1)
    def _():
        ids = [lax.broadcasted_iota(jnp.int32, (n_occ, n_occ), d) for d in (0, 1)]
        for i in range(pair):
            out[i] = jnp.full(out.shape[1:], jnp.sum(jnp.where(ids[0] == ids[1], acc[i], 0.0)), F32)


def make_cross(k, place, halves, thetas, part, n):
    count, rows, n_occ = halves[0].shape
    pair = 2
    return pl.pallas_call(
        functools.partial(cross_kernel, n, (k, part)),
        out_shape=jax.ShapeDtypeStruct((pair, 8, 128), F32),
        grid=(count,),
        in_specs=[SMEM]
        + [pl.BlockSpec((1, rows, n_occ), lambda s: (s, 0, 0))] * (2 * n)
        + [VMEM] * len(thetas),
        out_specs=VMEM,
        scratch_shapes=[
            pltpu.VMEM((n * rows, n_occ), BF),
            pltpu.VMEM((pair * n_occ, n * rows), BF),
            pltpu.VMEM((pair, n_occ, n_occ), F32),
        ],
        compiler_params=params(),
        cost_estimate=cost(7e9, 1.2e7),
        name="cross",
    )(place, *halves, *thetas)


def taylor_kernel(n, place, walker, *rest):
    parts = rest[: 2 * n]
    mine, other, v_ref = rest[2 * n :]
    z_at, core = place[2], place[3]
    half = parts[0].shape[0]
    for k in range(n):
        block = lax.rem(z_at - k + n, n)
        v_ref[pl.ds(pl.multiple_of((2 * block + core) * half, half), half), :] = parts[k][...]
        v_ref[pl.ds(pl.multiple_of((2 * block + 1 - core) * half, half), half), :] = parts[n + k][...]
    term = walker[...]
    total = term.astype(F32)
    for k in range(1, TERMS + 1):
        term = (mm(v_ref[...], term) / k).astype(BF)
        total = total + term.astype(F32)
    done = total.astype(BF)
    rows = done.shape[0] // 2
    first = core == 0
    mine[...] = jnp.where(first, done[:rows].astype(F32), done[rows:].astype(F32)).astype(BF)
    other[...] = jnp.where(first, done[rows:].astype(F32), done[:rows].astype(F32)).astype(BF)


def make_taylor(place, walker, parts, n):
    n_orb, n_occ = walker.shape
    half = jax.ShapeDtypeStruct((n_orb // 2, n_occ), BF)
    return pl.pallas_call(
        functools.partial(taylor_kernel, n),
        out_shape=[half, half],
        in_specs=[SMEM] + [VMEM] * (1 + 2 * n),
        out_specs=[VMEM] * 2,
        scratch_shapes=[pltpu.VMEM((n_orb, n_orb), BF)],
        compiler_params=params(),
        cost_estimate=cost(1.3e9, 2e6),
        name="taylor",
    )(place, walker, *parts)


def join_kernel(n, place, *rest):
    parts, out = rest[:-1], rest[-1]
    y_at, core = place[1], place[3]
    rows = parts[0].shape[0]
    for k in range(n):
        slot = lax.rem(y_at - k + n, n)
        out[slot, pl.ds(pl.multiple_of(core * rows, rows), rows), :] = parts[k][...]
        out[slot, pl.ds(pl.multiple_of((1 - core) * rows, rows), rows), :] = parts[n + k][...]


def join(place, parts, n):
    rows, n_occ = parts[0].shape
    return pl.pallas_call(
        functools.partial(join_kernel, n),
        out_shape=jax.ShapeDtypeStruct((n, 2 * rows, n_occ), BF),
        in_specs=[SMEM] + [VMEM] * (2 * n),
        out_specs=VMEM,
        compiler_params=params(),
        cost_estimate=cost(1e6, 2e6),
        name="join",
    )(place, *parts)


def shards(walkers, trial, half_chol, chol_vectors, noise, copies):
    n = lax.axis_size("x")
    x, y, z, core = (lax.axis_index(a) for a in ("x", "y", "z", "core"))
    place = jnp.stack([x, y, z, core]).astype(jnp.int32)
    w_grp, n_orb, n_occ = walkers.shape
    n_vec = half_chol.shape[0]
    slots = w_grp * n
    other_core = functools.partial(lax.ppermute, axis_name="core", perm=[(0, 1), (1, 0)])

    def along(v, axis, k):
        return lax.ppermute(v, axis, shift(n, k)) if k else v

    parent = jnp.sum(
        (jnp.cumsum(copies)[None, :] <= jnp.arange(slots, dtype=jnp.int32)[:, None]).astype(jnp.int32),
        axis=1,
    )

    per = n_vec // n
    halves = [
        along(lax.dynamic_slice_in_dim(half_chol, (x + k) % n * per, per, 0), "x", k) for k in range(n)
    ]
    halves = halves + [other_core(h) for h in halves]
    chol_theirs = other_core(chol_vectors)

    def offered(k):
        wanted = parent[(x + k) % n * w_grp + y] - w_grp * x
        return along(
            lax.dynamic_index_in_dim(walkers, jnp.clip(wanted, 0, w_grp - 1), 0, keepdims=False), "x", k
        )

    home = parent[x * w_grp + y] // w_grp
    offers = [offered(k) for k in range(n)]
    walker = offers[0]
    for k in range(1, n):
        walker = jnp.where((x - k) % n == home, offers[k], walker)

    made = make_theta(place, trial, walkers, n)
    own, rest = made[:n], made[n:]
    rows_here = [along(own[k], "x", k) for k in range(n)]
    thetas = rows_here + [other_core(t) for t in rows_here]
    partial_bias = make_bias(place, half_chol, noise, thetas, n)
    summed = lax.psum(partial_bias, ("x", "core"))

    order = jnp.array([[k, m] for k in range(n) for m in range(n)], jnp.int32)
    slot = w_grp * ((z + order[:, 1]) % n) + (y + order[:, 0]) % n
    picker = (parent[slot][:, None] == jnp.arange(slots, dtype=jnp.int32)[None, :]).astype(BF)
    partials = make_potential(place, summed, picker, chol_vectors, chol_theirs, n)

    def added(parts):
        total = parts[0].astype(F32)
        for p in parts[1:]:
            total = total + p.astype(F32)
        return total.astype(BF)

    over_y = added([along(partials[k], "y", k) for k in range(n)])
    piece = added([along(over_y[m], "z", m) for m in range(n)])
    cross_plane = [
        lax.ppermute(
            piece, ("x", "z"), [(n * a + b, n * b + (a + k) % n) for a in range(n) for b in range(n)]
        )
        for k in range(n)
    ]
    parts = cross_plane + [other_core(p) for p in cross_plane]
    mine, other = make_taylor(place, walker, parts, n)
    spread = [along(mine, "y", k) for k in range(n)]
    new_walkers = join(place, spread + [other] + [other_core(s) for s in spread[1:]], n)

    crosses = []
    for k in range(n):
        if k == 0:
            arrays, part = own, [[(None, j)] for j in range(n)]
        else:
            arrays = [rows_here[k], along(rest[k - 1], "x", k)]
            part = [[(None, k)], [(j - (j > k), j) for j in range(n) if j != k]]
        crosses.append(make_cross(k, place, halves, arrays, part, n))
    local = 0.5 / (2 * n) * jnp.sum(summed[0] * summed[0], axis=0)
    for k in range(n):
        first = w_grp * ((x - k) % n) + 2 * core
        local = lax.dynamic_update_slice(
            local, lax.dynamic_slice(local, (first,), (2,)) - 0.5 * crosses[k][:, 0, 0], (first,)
        )
    every = lax.all_gather(local.reshape(1, slots), ("x", "y", "z", "core"), axis=0, tiled=True)
    n_all = n_vec * 2 * n * n
    energies = lax.dynamic_slice_in_dim(jnp.sum(every, axis=0), w_grp * x, w_grp) / n_all
    return new_walkers, energies


def solution(mesh):
    finer = Mesh(mesh.devices.reshape(4, 4, 4, 2), ("x", "y", "z", "core"))
    chol = ("y", "z", "core")
    placed = (
        P("x", None, None),
        P(),
        P(chol, "x", None),
        P(chol, "x", None),
        P("x", chol),
        P(),
    )
    return jax.shard_map(
        shards,
        mesh=finer,
        in_specs=placed,
        out_specs=(P("x", None, None), P("x")),
        check_vma=False,
    )
```

time: 664 us -> 341 us (0.51); the launches traced: 653 us -> 338 us
  other arithmetic: 224 us -> 7.22 us
  blocking collectives: 198 us -> 59.2 us
  Pallas kernels: 0 us -> 113 us
  matrix products: 62.9 us -> 0 us
  local copies, waits for them, and re-layouts: 74.6 us -> 18.9 us
  starting transfers between devices: 5.47 us -> 44.7 us
  waiting for transfers between devices: 72.8 us -> 88.8 us
  between operations: 14.6 us -> 6.21 us
    another operation x19 -> x3, other arithmetic: 194 us -> 0.82 us  [the longest x1 0.66 us: shards(): place = jnp.stack([x, y, z, core]).astype(jnp.int32)]
    psum x1, blocking collectives: 154 us -> 26.6 us  [shards(): summed = lax.psum(partial_bias, ('x', 'core'))]
    pallas_call x0 -> x9, Pallas kernels: none -> 113 us  [the longest x4 78 us: make_cross(): pl.pallas_call(functools.partial(cross_kernel, n, (k, part)), out_shape=j...]
    ppermute x0 -> x41, waiting for transfers between devices: none -> 88.8 us  [the longest x21 80.5 us: along(): return lax.ppermute(v, axis, shift(n, k)) if k else v]
    all_to_all x1 -> x0, waiting for transfers between devices: 72.1 us -> none  [shards(): lax.all_to_all(partial_value, 'walk', split_axis=0, concat_axis=1, tiled=...]
    dot_general x10 -> x0, matrix products: 53.8 us -> none  [the longest x1 29.3 us: shards(): lax.dot_general(lax.all_gather(half_chol, 'walk', axis=1, tiled=True), ro...]
    ppermute x0 -> x41, starting transfers between devices: none -> 44.7 us  [the longest x21 30.4 us: along(): return lax.ppermute(v, axis, shift(n, k)) if k else v]
    unnamed x21 -> x71, local copies, waits for them, and re-layouts: 52.6 us -> 11.6 us
  transfers between devices with their start and end apart: 2 -> 41, of which waited for: 1 -> 12; matrix products, arithmetic and copies ran while one was open for 32% -> 5% of each run, Pallas kernels for 0% -> 31%
where the time goes in v1:
time: 341 us; the launch traced here: 338 us
  Pallas kernels  113 us (33%)
  waiting for transfers between devices  88.8 us (26%)
  blocking collectives  59.2 us (17%)
  starting transfers between devices  44.7 us (13%)
  local copies, waits for them, and re-layouts  18.9 us (6%)
  other arithmetic  7.22 us (2%)
  between operations  6.21 us (2%)
    ppermute x21, waiting for transfers between devices, along(): return lax.ppermute(v, axis, shift(n, k)) if k else v  80.5 us
    pallas_call x4, Pallas kernels, make_cross(): pl.pallas_call(functools.partial(cross_kernel, n, (k, part)), out_shape=j...  78 us
    all_gather x1, blocking collectives, shards(): lax.all_gather(local.reshape(1, slots), ('x', 'y', 'z', 'core'), axis=0,...  32.6 us
    ppermute x21, starting transfers between devices, along(): return lax.ppermute(v, axis, shift(n, k)) if k else v  30.4 us
    psum x1, blocking collectives, shards(): summed = lax.psum(partial_bias, ('x', 'core'))  26.6 us
    unnamed x71, local copies, waits for them, and re-layouts  11.6 us
    ppermute x4, starting transfers between devices, shards(): lax.ppermute(piece, ('x', 'z'), [(n * a + b, n * b + (a + k) % n) for a i...  10.9 us
    pallas_call x1, Pallas kernels, make_potential(): pl.pallas_call(functools.partial(potential_kernel, n), out_shape=[jax.Sha...  9.93 us
  transfers between devices with their start and end apart: 41, of which 12 were waited for; matrix products, arithmetic and copies ran while one was open for 5% of the time, Pallas kernels for 31%

profile of v1, /device:TPU:0, one launch (start us, length us, event | category | flops | bytes accessed | tf_op | source)
XLA Modules:
  0.0 338.0 jit_solution(2417191934186174482)
XLA Ops:
  0.7 2.5 copy.39.walkers
  3.2 0.9 copy.38.trial
  4.1 0.7 pad_add_fusion.place
  4.8 8.8 %theta.1 = (bf16[2,160,200]{2,1,0:T(8,128)(2,1)}, bf16[2,160,200]{2,1,0:T(8,128)(2,1)}, bf16[2,160,200]{2,1,0:T(8,128)(2,1)}, bf16[2,160,200]{2,1,0:T(8,128)(2,1...) custom-call(s32[4]{0:T(128)} %pad_add_fusion.place, ...), custom_call_target="tpu_custom_call" | custom-call | flops 10000000000 | bytes 4000000 | tf_op jit(solution)/shard_map/theta/pallas_call | solution.py:111
  13.6 1.6 collective-permute-start.3
  15.2 2.2 collective-permute-start.4
  17.4 1.4 collective-permute-start.5
  19.4 0.7 fusion.16
  23.1 3.0 collective-permute-done.4.rest_2_.rest_8_
  26.3 4.1 %constant_dynamic-slice_fusion = (bf16[14,160,200]{2,1,0:T(8,128)(2,1)S(1)}, bf16[14,160,200]{2,1,0:T(8,128)(2,1)}, bf16[14,160,200]{2,1,0:T(8,128)(2,1)S(1)}, bf16[14,160,200]{2,1,0:T(8,128)(2,1)}) fusion(bf16[56,160,200]{2,1,0:T(8,128)(2,1)} %half.1, s32[]{:T(128)S(6)} %select_n.164, s32[]{:T(128)S(6)} %select_n.162, s32[]{:T(128)S(6)} %select_n.161, ...), kind=kLoop, calls=%fused_computation.25 | loop fusion | bytes 7168016 | tf_op jit(solution)/shard_map/dynamic_slice | solution.py:379
  30.5 1.3 collective-permute-start.32
  31.8 2.5 collective-permute-start.33
  35.0 0.9 copy.34
  36.7 55.1 %collective-permute-done = bf16[640,200]{1,0:T(8,128)(2,1)} collective-permute-done((bf16[640,200]{1,0:T(8,128)(2,1)}, bf16[640,200]{1,0:T(8,128)(2,1)}, u32[]{:S(2)}, u32[]{:S(2)}) %collective-permute-start) | collective-permute-done | bytes 256032 | tf_op jit(solution)/shard_map/ppermute | solution.py:370
  91.8 1.1 collective-permute-start.1
  93.1 9.2 %collective-permute-done.1 = bf16[640,200]{1,0:T(8,128)(2,1)} collective-permute-done((bf16[640,200]{1,0:T(8,128)(2,1)S(1)}, bf16[640,200]{1,0:T(8,128)(2,1)}, u32[]{:S(2)}, u32[]{:S(2)}) %collective-permute-start.1) | collective-permute-done | bytes 256032 | tf_op jit(solution)/shard_map/ppermute | solution.py:370
  102.2 1.2 collective-permute-start.2
  105.9 0.7 gather_fusion
  106.8 0.7 fusion.6.picker
  107.4 4.2 %collective-permute-done.2 = bf16[640,200]{1,0:T(8,128)(2,1)S(1)} collective-permute-done((bf16[640,200]{1,0:T(8,128)(2,1)S(1)}, bf16[640,200]{1,0:T(8,128)(2,1)S(1)}, u32[]{:S(2)}, u32[]{:S(2)}) %collective-permute-start.2) | collective-permute-done | bytes 256032 | tf_op jit(solution)/shard_map/ppermute | solution.py:370
  111.6 0.5 collective-permute-start.35
  112.7 9.3 %bias.1 = f32[2,112,16]{2,1,0:T(8,128)} custom-call(s32[4]{0:T(128)} %pad_add_fusion.place, bf16[56,160,200]{2,1,0:T(8,128)(2,1)} %half.1, f32[4,56]{1,0:T(4,128)} %noise.1, bf16[2,160,200]{2,1,0:T(8,128)(2,1)} %get-tuple-element.15.rest_0_.rest_8_, bf16[2,160,200]{2,1,0:T(8,128)(2,1)} %copy-done.21, bf16[2,160,200]{2,1,0:T(8,128)(2,1)} %copy-done.22, ...), custom_call_target="tpu_custom_call" | custom-call | flops 4000000000 | bytes 8000000 | tf_op jit(solution)/shard_map/bias/pallas_call | solution.py:171
  121.9 26.6 %psum.7.summed = f32[2,112,16]{2,1,0:T(8,128)S(1)} all-reduce(f32[2,112,16]{2,1,0:T(8,128)} %bias.1), channel_id=1, replica_groups=mesh['x'=4,'y'=4,'z'=4,'core'=2] {'x','core'}, use_global_device_ids=true, to_apply=%region_2.3 | all-reduce | flops 3584 | bytes 28672 | tf_op jit(solution)/shard_map/psum | solution.py:401
  148.7 0.8 fusion.1.walker
  149.7 0.6 collective-permute-start.40
  150.3 1.5 collective-permute-start.38
  151.8 1.0 copy-done.14
  152.8 19.6 %cross.4 = f32[2,8,128]{2,1,0:T(8,128)} custom-call(s32[4]{0:T(128)} %pad_add_fusion.place, bf16[14,160,200]{2,1,0:T(8,128)(2,1)} %copy-done.1, bf16[14,160,200]{2,1,0:T(8,128)(2,1)} %collective-permute-done.31.rest_1_, bf16[14,160,200]{2,1,0:T(8,128)(2,1)} %collective-permute-done.32.rest_2_, bf16[14,160,200]{2,1,0:T(8,128)(2,1)} %collective-permute-done.33.rest_3_, ...), custom_call_target="tpu_custom_call" | custom-call | flops 7000000000 | bytes 12000000 | tf_op jit(solution)/shard_map/cross/pallas_call | solution.py:282
  172.4 0.8 copy-done.19
  173.2 19.5 %cross.7 = f32[2,8,128]{2,1,0:T(8,128)} custom-call(s32[4]{0:T(128)} %pad_add_fusion.place, bf16[14,160,200]{2,1,0:T(8,128)(2,1)} %copy-done.1, bf16[14,160,200]{2,1,0:T(8,128)(2,1)} %collective-permute-done.31.rest_1_, bf16[14,160,200]{2,1,0:T(8,128)(2,1)} %collective-permute-done.32.rest_2_, bf16[14,160,200]{2,1,0:T(8,128)(2,1)} %collective-permute-done.33.rest_3_, ...), custom_call_target="tpu_custom_call" | custom-call | flops 7000000000 | bytes 12000000 | tf_op jit(solution)/shard_map/cross/pallas_call | solution.py:282
  192.7 0.8 copy-done.20
  193.5 19.5 %cross.6 = f32[2,8,128]{2,1,0:T(8,128)} custom-call(s32[4]{0:T(128)} %pad_add_fusion.place, bf16[14,160,200]{2,1,0:T(8,128)(2,1)} %copy-done.1, bf16[14,160,200]{2,1,0:T(8,128)(2,1)} %collective-permute-done.31.rest_1_, bf16[14,160,200]{2,1,0:T(8,128)(2,1)} %collective-permute-done.32.rest_2_, bf16[14,160,200]{2,1,0:T(8,128)(2,1)} %collective-permute-done.33.rest_3_, ...), custom_call_target="tpu_custom_call" | custom-call | flops 7000000000 | bytes 12000000 | tf_op jit(solution)/shard_map/cross/pallas_call | solution.py:282
  212.9 9.9 %potential.1 = (bf16[4,80,640]{2,1,0:T(8,128)(2,1)}, bf16[4,80,640]{2,1,0:T(8,128)(2,1)}, bf16[4,80,640]{2,1,0:T(8,128)(2,1)}, bf16[4,80,640]{2,1,0:T(8,128)(2,1)}) custom-call(s32[4]{0:T(128)} %pad_add_fusion.place, f32[2,112,16]{2,1,0:T(8,128)} %copy-done.2, bf16[16,16]{1,0:T(8,128)(2,1)} %fusion.6.picker, bf16[56,160,640]{2,1,0:T(8,128)(2,1)} %mine.1, ...), custom_call_target="tpu_custom_call" | custom-call | flops 4000000000 | bytes 15000000 | tf_op jit(solution)/shard_map/potential/pallas_call | solution.py:224
  222.9 1.6 collective-permute-start.11
  224.4 2.9 collective-permute-start.12
  227.4 1.3 collective-permute-start.13
  228.7 0.8 copy-done.18
  229.5 19.5 %cross.5 = f32[2,8,128]{2,1,0:T(8,128)} custom-call(s32[4]{0:T(128)} %pad_add_fusion.place, bf16[14,160,200]{2,1,0:T(8,128)(2,1)} %copy-done.1, bf16[14,160,200]{2,1,0:T(8,128)(2,1)} %collective-permute-done.31.rest_1_, bf16[14,160,200]{2,1,0:T(8,128)(2,1)} %collective-permute-done.32.rest_2_, bf16[14,160,200]{2,1,0:T(8,128)(2,1)} %collective-permute-done.33.rest_3_, ...), custom_call_target="tpu_custom_call" | custom-call | flops 7000000000 | bytes 12000000 | tf_op jit(solution)/shard_map/cross/pallas_call | solution.py:282
  249.0 0.8 fusion.7
  250.2 2.0 collective-permute-start.14
  252.2 3.6 %collective-permute-start.15 = (bf16[80,640]{1,0:T(8,128)(2,1)S(1)}, bf16[80,640]{1,0:T(8,128)(2,1)S(1)}, u32[]{:S(2)}, u32[]{:S(2)}) collective-permute-start(bf16[80,640]{1,0:T(8,128)(2,1)S(1)} %get-tuple-element.46), channel_id=1, source_target_pairs={{0,4},{2,6},{4,0},{6,2},{1,5},{3,7},{5,1},{7,3},{8,12},{10,14},{12... | collective-permute-start | bytes 307208 | tf_op jit(solution)/shard_map/ppermute | solution.py:370
  255.8 1.0 collective-permute-start.16
  256.8 0.8 fusion.8
  257.6 1.9 collective-permute-done.15
  259.5 0.9 collective-permute-done.16
  260.5 0.7 collective-permute-start.17
  261.2 4.4 %collective-permute-start.18 = (bf16[80,640]{1,0:T(8,128)(2,1)S(1)}, bf16[80,640]{1,0:T(8,128)(2,1)S(1)}, u32[]{:S(2)}, u32[]{:S(2)}) collective-permute-start(bf16[80,640]{1,0:T(8,128)(2,1)S(1)} %fusion.4), channel_id=1, source_target_pairs={{0,2},{2,34},{4,66},{6,98},{32,4},{34,36},{36,68},{38,100},{64,6},... | collective-permute-start | bytes 307208 | tf_op jit(solution)/shard_map/ppermute | solution.py:417
  265.6 4.0 %collective-permute-start.19 = (bf16[80,640]{1,0:T(8,128)(2,1)S(1)}, bf16[80,640]{1,0:T(8,128)(2,1)S(1)}, u32[]{:S(2)}, u32[]{:S(2)}) collective-permute-start(bf16[80,640]{1,0:T(8,128)(2,1)S(1)} %fusion.4), channel_id=1, source_target_pairs={{0,4},{2,36},{4,68},{6,100},{32,6},{34,38},{36,70},{38,102},{64,0}... | collective-permute-start | bytes 307208 | tf_op jit(solution)/shard_map/ppermute | solution.py:417
  269.6 1.9 collective-permute-start.20
  271.7 7.8 %collective-permute-done.18.rest_1_ = bf16[80,640]{1,0:T(8,128)(2,1)S(1)} collective-permute-done((bf16[80,640]{1,0:T(8,128)(2,1)S(1)}, bf16[80,640]{1,0:T(8,128)(2,1)S(1)}, u32[]{:S(2)}, u32[]{:S(2)}) %collective-permute-start.18) | collective-permute-done | bytes 102432 | tf_op jit(solution)/shard_map/ppermute | solution.py:417
  279.5 0.5 collective-permute-start.23
  280.4 0.8 fusion.9
  281.9 0.6 copy-done.33
  282.5 4.3 %taylor.1 = (bf16[320,200]{1,0:T(8,128)(2,1)}, bf16[320,200]{1,0:T(8,128)(2,1)}) custom-call(s32[4]{0:T(128)} %pad_add_fusion.place, bf16[640,200]{1,0:T(8,128)(2,1)} %fusion.1.walker, bf16[80,640]{1,0:T(8,128)(2,1)} %copy-done.26, bf16[80,640]{1,0:T(8,128)(2,1)} %copy-done.27, bf16[80,640]{1,0:T(8,128)(2,1)} %copy-done.28, bf16[80,640]{1,0:T(8,128)(2,1)} %copy-done.29, ...), custom_call_target="tpu_custom_call" | custom-call | flops 1300000000 | bytes 2000000 | tf_op jit(solution)/shard_map/taylor/pallas_call | solution.py:325
  286.8 0.7 collective-permute-start.25
  287.5 1.2 collective-permute-start.26
  288.7 2.3 collective-permute-start.27
  291.1 0.8 fusion.10
  291.9 6.1 %collective-permute-done.25.rest_1_ = bf16[320,200]{1,0:T(8,128)(2,1)S(1)} collective-permute-done((bf16[320,200]{1,0:T(8,128)(2,1)}, bf16[320,200]{1,0:T(8,128)(2,1)S(1)}, u32[]{:S(2)}, u32[]{:S(2)}) %collective-permute-start.25) | collective-permute-done | bytes 128032 | tf_op jit(solution)/shard_map/ppermute | solution.py:370
  299.0 32.6 %all-gather = f32[128,1,16]{2,1,0:T(1,128)S(1)} all-gather(f32[1,1,16]{2,1,0:T(1,128)S(1)} %dynamic_update_slice.17), channel_id=1, replica_groups=mesh['x'=4,'y'=4,'z'=4,'core'=2] {'x','y','z','core'}, dimensions={0}, use_global_device_ids=true | all-gather | bytes 8256 | tf_op jit(solution)/shard_map/all_gather | solution.py:441
  331.7 0.6 dynamic-slice_multiply_fusion
  332.3 0.6 copy-done.8
  333.0 2.6 join.1
  335.6 2.3 copy.40
  (133 shorter events, 7.0 us)
Async XLA Ops:
  0.6 212.3 %collective-permute-start.10 = (bf16[56,160,640]{2,1,0:T(8,128)(2,1)}, bf16[56,160,640]{2,1,0:T(8,128)(2,1)}, u32[]{:S(2)}, u32[]{:S(2)}) collective-permute-start(bf16[56,160,640]{2,1,0:T(8,128)(2,1)} %mine.1), channel_id=1, source_target_pairs={{0,1},{1,0},{2,3},{3,2},{4,5},{5,4},{6,7},{7,6},{8,9},{9,8},{10,11... | collective-permute-start | bytes 34406408 | tf_op jit(solution)/shard_map/ppermute | solution.py:382
  0.7 2.5 copy-start.4
  4.8 14.2 %copy-start.11 = (s32[16]{0:T(128)S(1)}, s32[16]{0:T(128)}, u32[]{:S(2)}) copy-start(s32[16]{0:T(128)} %param.12) | copy-start | bytes 196
  13.6 9.1 %collective-permute-start.3 = (bf16[2,160,200]{2,1,0:T(8,128)(2,1)}, bf16[2,160,200]{2,1,0:T(8,128)(2,1)S(1)}, u32[]{:S(2)}, u32[]{:S(2)}) collective-permute-start(bf16[2,160,200]{2,1,0:T(8,128)(2,1)} %get-tuple-element.16.rest_9_), channel_id=1, source_target_pairs={{0,32},{32,64},{64,96},{96,0},{1,33},{33,65},{65,97},{97,1},{2,34}... | collective-permute-start | bytes 384008 | tf_op jit(solution)/shard_map/ppermute | solution.py:370
  15.2 11.0 %collective-permute-start.4 = (bf16[2,160,200]{2,1,0:T(8,128)(2,1)}, bf16[2,160,200]{2,1,0:T(8,128)(2,1)S(1)}, u32[]{:S(2)}, u32[]{:S(2)}) collective-permute-start(bf16[2,160,200]{2,1,0:T(8,128)(2,1)} %get-tuple-element.17.rest_10_), channel_id=1, source_target_pairs={{0,64},{32,96},{64,0},{96,32},{1,65},{33,97},{65,1},{97,33},{2,66}... | collective-permute-start | bytes 384008 | tf_op jit(solution)/shard_map/ppermute | solution.py:370
  17.4 12.9 %collective-permute-start.5 = (bf16[2,160,200]{2,1,0:T(8,128)(2,1)}, bf16[2,160,200]{2,1,0:T(8,128)(2,1)}, u32[]{:S(2)}, u32[]{:S(2)}) collective-permute-start(bf16[2,160,200]{2,1,0:T(8,128)(2,1)} %get-tuple-element.18.rest_11_), channel_id=1, source_target_pairs={{0,96},{32,0},{64,32},{96,64},{1,97},{33,1},{65,33},{97,65},{2,98}... | collective-permute-start | bytes 384008 | tf_op jit(solution)/shard_map/ppermute | solution.py:370
  18.8 11.6 %collective-permute-start.6 = (bf16[2,160,200]{2,1,0:T(8,128)(2,1)}, bf16[2,160,200]{2,1,0:T(8,128)(2,1)S(1)}, u32[]{:S(2)}, u32[]{:S(2)}) collective-permute-start(bf16[2,160,200]{2,1,0:T(8,128)(2,1)} %get-tuple-element.15.rest_0_.rest_8_), channel_id=1, source_target_pairs={{0,1},{1,0},{2,3},{3,2},{4,5},{5,4},{6,7},{7,6},{8,9},{9,8},{10,11... | collective-permute-start | bytes 384008 | tf_op jit(solution)/shard_map/ppermute | solution.py:399
  22.7 11.7 %copy-start = (bf16[4,640,200]{1,2,0:T(8,128)(2,1)S(1)}, bf16[4,640,200]{1,2,0:T(8,128)(2,1)}, u32[]{:S(2)}) copy-start(bf16[4,640,200]{1,2,0:T(8,128)(2,1)} %param.7) | copy-start | bytes 3072004
  22.7 7.7 %copy-start.21 = (bf16[2,160,200]{2,1,0:T(8,128)(2,1)}, bf16[2,160,200]{2,1,0:T(8,128)(2,1)S(1)}, u32[]{:S(2)}) copy-start(bf16[2,160,200]{2,1,0:T(8,128)(2,1)S(1)} %collective-permute-done.3.rest_1_.rest_8_) | copy-start | bytes 384004
  22.7 9.1 %collective-permute-start.7 = (bf16[2,160,200]{2,1,0:T(8,128)(2,1)S(1)}, bf16[2,160,200]{2,1,0:T(8,128)(2,1)S(1)}, u32[]{:S(2)}, u32[]{:S(2)}) collective-permute-start(bf16[2,160,200]{2,1,0:T(8,128)(2,1)S(1)} %collective-permute-done.3.rest_1_.rest_8_), channel_id=1, source_target_pairs={{0,1},{1,0},{2,3},{3,2},{4,5},{5,4},{6,7},{7,6},{8,9},{9,8},{10,11... | collective-permute-start | bytes 384008 | tf_op jit(solution)/shard_map/ppermute | solution.py:399
  26.2 4.2 %copy-start.22 = (bf16[2,160,200]{2,1,0:T(8,128)(2,1)}, bf16[2,160,200]{2,1,0:T(8,128)(2,1)S(1)}, u32[]{:S(2)}) copy-start(bf16[2,160,200]{2,1,0:T(8,128)(2,1)S(1)} %collective-permute-done.4.rest_2_.rest_8_) | copy-start | bytes 384004
  26.2 8.2 %collective-permute-start.8 = (bf16[2,160,200]{2,1,0:T(8,128)(2,1)S(1)}, bf16[2,160,200]{2,1,0:T(8,128)(2,1)S(1)}, u32[]{:S(2)}, u32[]{:S(2)}) collective-permute-start(bf16[2,160,200]{2,1,0:T(8,128)(2,1)S(1)} %collective-permute-done.4.rest_2_.rest_8_), channel_id=1, source_target_pairs={{0,1},{1,0},{2,3},{3,2},{4,5},{5,4},{6,7},{7,6},{8,9},{9,8},{10,11... | collective-permute-start | bytes 384008 | tf_op jit(solution)/shard_map/ppermute | solution.py:399
  30.4 81.3 %copy-start.1 = (bf16[14,160,200]{2,1,0:T(8,128)(2,1)}, bf16[14,160,200]{2,1,0:T(8,128)(2,1)S(1)}, u32[]{:S(2)}) copy-start(bf16[14,160,200]{2,1,0:T(8,128)(2,1)S(1)} %get-tuple-element.38.rest_0_) | copy-start | bytes 2688004
  30.4 81.3 %collective-permute-start.31 = (bf16[14,160,200]{2,1,0:T(8,128)(2,1)}, bf16[14,160,200]{2,1,0:T(8,128)(2,1)}, u32[]{:S(2)}, u32[]{:S(2)}) collective-permute-start(bf16[14,160,200]{2,1,0:T(8,128)(2,1)} %get-tuple-element.37), channel_id=1, source_target_pairs={{0,32},{32,64},{64,96},{96,0},{1,33},{33,65},{65,97},{97,1},{2,34}... | collective-permute-start | bytes 2688008 | tf_op jit(solution)/shard_map/ppermute | solution.py:370
  30.5 3.9 %copy-start.23 = (bf16[2,160,200]{2,1,0:T(8,128)(2,1)}, bf16[2,160,200]{2,1,0:T(8,128)(2,1)S(1)}, u32[]{:S(2)}) copy-start(bf16[2,160,200]{2,1,0:T(8,128)(2,1)S(1)} %collective-permute-done.6.rest_4_) | copy-start | bytes 384004
  30.5 81.7 %collective-permute-start.32 = (bf16[14,160,200]{2,1,0:T(8,128)(2,1)}, bf16[14,160,200]{2,1,0:T(8,128)(2,1)}, u32[]{:S(2)}, u32[]{:S(2)}) collective-permute-start(bf16[14,160,200]{2,1,0:T(8,128)(2,1)} %get-tuple-element.39), channel_id=1, source_target_pairs={{0,64},{32,96},{64,0},{96,32},{1,65},{33,97},{65,1},{97,33},{2,66}... | collective-permute-start | bytes 2688008 | tf_op jit(solution)/shard_map/ppermute | solution.py:370
  31.8 2.7 copy-start.24
  31.8 80.4 %collective-permute-start.33 = (bf16[14,160,200]{2,1,0:T(8,128)(2,1)S(1)}, bf16[14,160,200]{2,1,0:T(8,128)(2,1)}, u32[]{:S(2)}, u32[]{:S(2)}) collective-permute-start(bf16[14,160,200]{2,1,0:T(8,128)(2,1)S(1)} %get-tuple-element.36), channel_id=1, source_target_pairs={{0,96},{32,0},{64,32},{96,64},{1,97},{33,1},{65,33},{97,65},{2,98}... | collective-permute-start | bytes 2688008 | tf_op jit(solution)/shard_map/ppermute | solution.py:370
  34.3 1.8 collective-permute-start.9
  35.0 58.0 %copy-start.12 = (s32[16,1]{0,1:T(1,128)S(1)}, s32[16,1]{0,1:T(1,128)}, u32[]{:S(2)}) copy-start(s32[16,1]{0,1:T(1,128)} %constant.145) | copy-start | bytes 196
  35.0 58.1 %copy-start.13 = (s32[16,1]{0,1:T(1,128)S(1)}, s32[16,1]{0,1:T(1,128)}, u32[]{:S(2)}) copy-start(s32[16,1]{0,1:T(1,128)} %constant.146) | copy-start | bytes 196
  36.1 55.6 %collective-permute-start = (bf16[640,200]{1,0:T(8,128)(2,1)}, bf16[640,200]{1,0:T(8,128)(2,1)}, u32[]{:S(2)}, u32[]{:S(2)}) collective-permute-start(bf16[640,200]{1,0:T(8,128)(2,1)} %bitcast.37), channel_id=1, source_target_pairs={{0,96},{32,0},{64,32},{96,64},{1,97},{33,1},{65,33},{97,65},{2,98}... | collective-permute-start | bytes 768008 | tf_op jit(solution)/shard_map/ppermute | solution.py:370
  91.8 10.5 %collective-permute-start.1 = (bf16[640,200]{1,0:T(8,128)(2,1)S(1)}, bf16[640,200]{1,0:T(8,128)(2,1)}, u32[]{:S(2)}, u32[]{:S(2)}) collective-permute-start(bf16[640,200]{1,0:T(8,128)(2,1)S(1)} %bitcast.36), channel_id=1, source_target_pairs={{0,64},{32,96},{64,0},{96,32},{1,65},{33,97},{65,1},{97,33},{2,66}... | collective-permute-start | bytes 768008 | tf_op jit(solution)/shard_map/ppermute | solution.py:370
  102.2 9.4 %collective-permute-start.2 = (bf16[640,200]{1,0:T(8,128)(2,1)S(1)}, bf16[640,200]{1,0:T(8,128)(2,1)S(1)}, u32[]{:S(2)}, u32[]{:S(2)}) collective-permute-start(bf16[640,200]{1,0:T(8,128)(2,1)S(1)} %bitcast.35), channel_id=1, source_target_pairs={{0,32},{32,64},{64,96},{96,0},{1,33},{33,65},{65,97},{97,1},{2,34}... | collective-permute-start | bytes 768008 | tf_op jit(solution)/shard_map/ppermute | solution.py:370
  111.6 37.9 %collective-permute-start.34 = (bf16[14,160,200]{2,1,0:T(8,128)(2,1)S(1)}, bf16[14,160,200]{2,1,0:T(8,128)(2,1)}, u32[]{:S(2)}, u32[]{:S(2)}) collective-permute-start(bf16[14,160,200]{2,1,0:T(8,128)(2,1)S(1)} %get-tuple-element.38.rest_0_), channel_id=1, source_target_pairs={{0,1},{1,0},{2,3},{3,2},{4,5},{5,4},{6,7},{7,6},{8,9},{9,8},{10,11... | collective-permute-start | bytes 2688008 | tf_op jit(solution)/shard_map/ppermute | solution.py:381
  111.6 38.7 %collective-permute-start.35 = (bf16[14,160,200]{2,1,0:T(8,128)(2,1)}, bf16[14,160,200]{2,1,0:T(8,128)(2,1)}, u32[]{:S(2)}, u32[]{:S(2)}) collective-permute-start(bf16[14,160,200]{2,1,0:T(8,128)(2,1)} %collective-permute-done.31.rest_1_), channel_id=1, source_target_pairs={{0,1},{1,0},{2,3},{3,2},{4,5},{5,4},{6,7},{7,6},{8,9},{9,8},{10,11... | collective-permute-start | bytes 2688008 | tf_op jit(solution)/shard_map/ppermute | solution.py:381
  112.1 38.2 %collective-permute-start.36 = (bf16[14,160,200]{2,1,0:T(8,128)(2,1)}, bf16[14,160,200]{2,1,0:T(8,128)(2,1)}, u32[]{:S(2)}, u32[]{:S(2)}) collective-permute-start(bf16[14,160,200]{2,1,0:T(8,128)(2,1)} %collective-permute-done.32.rest_2_), channel_id=1, source_target_pairs={{0,1},{1,0},{2,3},{3,2},{4,5},{5,4},{6,7},{7,6},{8,9},{9,8},{10,11... | collective-permute-start | bytes 2688008 | tf_op jit(solution)/shard_map/ppermute | solution.py:381
  112.2 39.6 %collective-permute-start.37 = (bf16[14,160,200]{2,1,0:T(8,128)(2,1)}, bf16[14,160,200]{2,1,0:T(8,128)(2,1)S(1)}, u32[]{:S(2)}, u32[]{:S(2)}) collective-permute-start(bf16[14,160,200]{2,1,0:T(8,128)(2,1)} %collective-permute-done.33.rest_3_), channel_id=1, source_target_pairs={{0,1},{1,0},{2,3},{3,2},{4,5},{5,4},{6,7},{7,6},{8,9},{9,8},{10,11... | collective-permute-start | bytes 2688008 | tf_op jit(solution)/shard_map/ppermute | solution.py:381
  148.6 23.8 %copy-start.2 = (f32[2,112,16]{2,1,0:T(8,128)}, f32[2,112,16]{2,1,0:T(8,128)S(1)}, u32[]{:S(2)}) copy-start(f32[2,112,16]{2,1,0:T(8,128)S(1)} %psum.7.summed) | copy-start | bytes 43012
  148.6 1.1 copy-start.17
  148.6 1.7 copy-start.16
  148.6 1.7 copy-start.15
  149.7 22.7 %collective-permute-start.40 = (bf16[3,2,160,200]{3,2,1,0:T(8,128)(2,1)S(1)}, bf16[3,2,160,200]{3,2,1,0:T(8,128)(2,1)S(1)}, u32[]{:S(2)}, u32[]{:S(2)}) collective-permute-start(bf16[3,2,160,200]{3,2,1,0:T(8,128)(2,1)S(1)} %copy-done.17), channel_id=1, source_target_pairs={{0,96},{32,0},{64,32},{96,64},{1,97},{33,1},{65,33},{97,65},{2,98}... | collective-permute-start | bytes 1152008 | tf_op jit(solution)/shard_map/ppermute | solution.py:370
  150.3 42.4 %collective-permute-start.39 = (bf16[3,2,160,200]{3,2,1,0:T(8,128)(2,1)S(1)}, bf16[3,2,160,200]{3,2,1,0:T(8,128)(2,1)S(1)}, u32[]{:S(2)}, u32[]{:S(2)}) collective-permute-start(bf16[3,2,160,200]{3,2,1,0:T(8,128)(2,1)S(1)} %copy-done.16), channel_id=1, source_target_pairs={{0,64},{32,96},{64,0},{96,32},{1,65},{33,97},{65,1},{97,33},{2,66}... | collective-permute-start | bytes 1152008 | tf_op jit(solution)/shard_map/ppermute | solution.py:370
  150.3 78.4 %collective-permute-start.38 = (bf16[3,2,160,200]{3,2,1,0:T(8,128)(2,1)S(1)}, bf16[3,2,160,200]{3,2,1,0:T(8,128)(2,1)S(1)}, u32[]{:S(2)}, u32[]{:S(2)}) collective-permute-start(bf16[3,2,160,200]{3,2,1,0:T(8,128)(2,1)S(1)} %copy-done.15), channel_id=1, source_target_pairs={{0,32},{32,64},{64,96},{96,0},{1,33},{33,65},{65,97},{97,1},{2,34}... | collective-permute-start | bytes 1152008 | tf_op jit(solution)/shard_map/ppermute | solution.py:370
  151.8 1.0 copy-start.14
  222.9 27.1 %collective-permute-start.11 = (bf16[4,80,640]{2,1,0:T(8,128)(2,1)}, bf16[4,80,640]{2,1,0:T(8,128)(2,1)S(1)}, u32[]{:S(2)}, u32[]{:S(2)}) collective-permute-start(bf16[4,80,640]{2,1,0:T(8,128)(2,1)} %get-tuple-element.20), channel_id=1, source_target_pairs={{0,8},{8,16},{16,24},{24,0},{1,9},{9,17},{17,25},{25,1},{2,10},{10... | collective-permute-start | bytes 1228808 | tf_op jit(solution)/shard_map/ppermute | solution.py:370
  224.4 25.5 %collective-permute-start.12 = (bf16[4,80,640]{2,1,0:T(8,128)(2,1)}, bf16[4,80,640]{2,1,0:T(8,128)(2,1)S(1)}, u32[]{:S(2)}, u32[]{:S(2)}) collective-permute-start(bf16[4,80,640]{2,1,0:T(8,128)(2,1)} %get-tuple-element.21), channel_id=1, source_target_pairs={{0,16},{8,24},{16,0},{24,8},{1,17},{9,25},{17,1},{25,9},{2,18},{10... | collective-permute-start | bytes 1228808 | tf_op jit(solution)/shard_map/ppermute | solution.py:370
  227.4 22.6 %copy-start.3 = (bf16[4,80,640]{2,1,0:T(8,128)(2,1)S(1)}, bf16[4,80,640]{2,1,0:T(8,128)(2,1)}, u32[]{:S(2)}) copy-start(bf16[4,80,640]{2,1,0:T(8,128)(2,1)} %get-tuple-element.19) | copy-start | bytes 1228804
  227.4 22.6 %collective-permute-start.13 = (bf16[4,80,640]{2,1,0:T(8,128)(2,1)}, bf16[4,80,640]{2,1,0:T(8,128)(2,1)S(1)}, u32[]{:S(2)}, u32[]{:S(2)}) collective-permute-start(bf16[4,80,640]{2,1,0:T(8,128)(2,1)} %get-tuple-element.22), channel_id=1, source_target_pairs={{0,24},{8,0},{16,8},{24,16},{1,25},{9,1},{17,9},{25,17},{2,26},{10... | collective-permute-start | bytes 1228808 | tf_op jit(solution)/shard_map/ppermute | solution.py:370
  250.2 7.4 %collective-permute-start.14 = (bf16[80,640]{1,0:T(8,128)(2,1)S(1)}, bf16[80,640]{1,0:T(8,128)(2,1)S(1)}, u32[]{:S(2)}, u32[]{:S(2)}) collective-permute-start(bf16[80,640]{1,0:T(8,128)(2,1)S(1)} %get-tuple-element.44), channel_id=1, source_target_pairs={{0,2},{2,4},{4,6},{6,0},{1,3},{3,5},{5,7},{7,1},{8,10},{10,12},{12... | collective-permute-start | bytes 307208 | tf_op jit(solution)/shard_map/ppermute | solution.py:370
  252.2 7.3 %collective-permute-start.15 = (bf16[80,640]{1,0:T(8,128)(2,1)S(1)}, bf16[80,640]{1,0:T(8,128)(2,1)S(1)}, u32[]{:S(2)}, u32[]{:S(2)}) collective-permute-start(bf16[80,640]{1,0:T(8,128)(2,1)S(1)} %get-tuple-element.46), channel_id=1, source_target_pairs={{0,4},{2,6},{4,0},{6,2},{1,5},{3,7},{5,1},{7,3},{8,12},{10,14},{12... | collective-permute-start | bytes 307208 | tf_op jit(solution)/shard_map/ppermute | solution.py:370
  255.8 4.7 %collective-permute-start.16 = (bf16[80,640]{1,0:T(8,128)(2,1)S(1)}, bf16[80,640]{1,0:T(8,128)(2,1)S(1)}, u32[]{:S(2)}, u32[]{:S(2)}) collective-permute-start(bf16[80,640]{1,0:T(8,128)(2,1)S(1)} %get-tuple-element.45), channel_id=1, source_target_pairs={{0,6},{2,0},{4,2},{6,4},{1,7},{3,1},{5,3},{7,5},{8,14},{10,8},{12,... | collective-permute-start | bytes 307208 | tf_op jit(solution)/shard_map/ppermute | solution.py:370
  260.5 11.1 %collective-permute-start.17 = (bf16[80,640]{1,0:T(8,128)(2,1)S(1)}, bf16[80,640]{1,0:T(8,128)(2,1)S(1)}, u32[]{:S(2)}, u32[]{:S(2)}) collective-permute-start(bf16[80,640]{1,0:T(8,128)(2,1)S(1)} %fusion.4), channel_id=1, source_target_pairs={{0,0},{2,32},{4,64},{6,96},{32,2},{34,34},{36,66},{38,98},{64,4},{... | collective-permute-start | bytes 307208 | tf_op jit(solution)/shard_map/ppermute | solution.py:417
  261.2 18.4 %collective-permute-start.18 = (bf16[80,640]{1,0:T(8,128)(2,1)S(1)}, bf16[80,640]{1,0:T(8,128)(2,1)S(1)}, u32[]{:S(2)}, u32[]{:S(2)}) collective-permute-start(bf16[80,640]{1,0:T(8,128)(2,1)S(1)} %fusion.4), channel_id=1, source_target_pairs={{0,2},{2,34},{4,66},{6,98},{32,4},{34,36},{36,68},{38,100},{64,6},... | collective-permute-start | bytes 307208 | tf_op jit(solution)/shard_map/ppermute | solution.py:417
  265.6 13.9 %collective-permute-start.19 = (bf16[80,640]{1,0:T(8,128)(2,1)S(1)}, bf16[80,640]{1,0:T(8,128)(2,1)S(1)}, u32[]{:S(2)}, u32[]{:S(2)}) collective-permute-start(bf16[80,640]{1,0:T(8,128)(2,1)S(1)} %fusion.4), channel_id=1, source_target_pairs={{0,4},{2,36},{4,68},{6,100},{32,6},{34,38},{36,70},{38,102},{64,0}... | collective-permute-start | bytes 307208 | tf_op jit(solution)/shard_map/ppermute | solution.py:417
  269.6 10.5 %collective-permute-start.20 = (bf16[80,640]{1,0:T(8,128)(2,1)S(1)}, bf16[80,640]{1,0:T(8,128)(2,1)S(1)}, u32[]{:S(2)}, u32[]{:S(2)}) collective-permute-start(bf16[80,640]{1,0:T(8,128)(2,1)S(1)} %fusion.4), channel_id=1, source_target_pairs={{0,6},{2,38},{4,70},{6,102},{32,0},{34,32},{36,64},{38,96},{64,2},... | collective-permute-start | bytes 307208 | tf_op jit(solution)/shard_map/ppermute | solution.py:417
  271.6 9.8 %copy-start.26 = (bf16[80,640]{1,0:T(8,128)(2,1)}, bf16[80,640]{1,0:T(8,128)(2,1)S(1)}, u32[]{:S(2)}) copy-start(bf16[80,640]{1,0:T(8,128)(2,1)S(1)} %collective-permute-done.17.rest_0_) | copy-start | bytes 307204
  271.6 9.6 %collective-permute-start.21 = (bf16[80,640]{1,0:T(8,128)(2,1)S(1)}, bf16[80,640]{1,0:T(8,128)(2,1)S(1)}, u32[]{:S(2)}, u32[]{:S(2)}) collective-permute-start(bf16[80,640]{1,0:T(8,128)(2,1)S(1)} %collective-permute-done.17.rest_0_), channel_id=1, source_target_pairs={{0,1},{1,0},{2,3},{3,2},{4,5},{5,4},{6,7},{7,6},{8,9},{9,8},{10,11... | collective-permute-start | bytes 307208 | tf_op jit(solution)/shard_map/ppermute | solution.py:422
  279.5 1.8 copy-start.27
  279.5 1.6 collective-permute-start.22
  279.5 1.8 copy-start.28
  279.5 1.6 collective-permute-start.23
  280.0 1.3 copy-start.29
  280.0 1.3 collective-permute-start.24
  286.8 11.2 %collective-permute-start.25 = (bf16[320,200]{1,0:T(8,128)(2,1)}, bf16[320,200]{1,0:T(8,128)(2,1)S(1)}, u32[]{:S(2)}, u32[]{:S(2)}) collective-permute-start(bf16[320,200]{1,0:T(8,128)(2,1)} %get-tuple-element.23.rest_0_), channel_id=1, source_target_pairs={{0,8},{8,16},{16,24},{24,0},{1,9},{9,17},{17,25},{25,1},{2,10},{10... | collective-permute-start | bytes 384008 | tf_op jit(solution)/shard_map/ppermute | solution.py:370
  287.5 10.6 %collective-permute-start.26 = (bf16[320,200]{1,0:T(8,128)(2,1)}, bf16[320,200]{1,0:T(8,128)(2,1)S(1)}, u32[]{:S(2)}, u32[]{:S(2)}) collective-permute-start(bf16[320,200]{1,0:T(8,128)(2,1)} %get-tuple-element.23.rest_0_), channel_id=1, source_target_pairs={{0,16},{8,24},{16,0},{24,8},{1,17},{9,25},{17,1},{25,9},{2,18},{10... | collective-permute-start | bytes 384008 | tf_op jit(solution)/shard_map/ppermute | solution.py:370
  288.7 10.0 %collective-permute-start.27 = (bf16[320,200]{1,0:T(8,128)(2,1)}, bf16[320,200]{1,0:T(8,128)(2,1)S(1)}, u32[]{:S(2)}, u32[]{:S(2)}) collective-permute-start(bf16[320,200]{1,0:T(8,128)(2,1)} %get-tuple-element.23.rest_0_), channel_id=1, source_target_pairs={{0,24},{8,0},{16,8},{24,16},{1,25},{9,1},{17,9},{25,17},{2,26},{10... | collective-permute-start | bytes 384008 | tf_op jit(solution)/shard_map/ppermute | solution.py:370
  298.1 34.2 %copy-start.5 = (bf16[320,200]{1,0:T(8,128)(2,1)}, bf16[320,200]{1,0:T(8,128)(2,1)S(1)}, u32[]{:S(2)}) copy-start(bf16[320,200]{1,0:T(8,128)(2,1)S(1)} %collective-permute-done.25.rest_1_) | copy-start | bytes 384004
  298.1 34.2 %collective-permute-start.28 = (bf16[320,200]{1,0:T(8,128)(2,1)S(1)}, bf16[320,200]{1,0:T(8,128)(2,1)S(1)}, u32[]{:S(2)}, u32[]{:S(2)}) collective-permute-start(bf16[320,200]{1,0:T(8,128)(2,1)S(1)} %collective-permute-done.25.rest_1_), channel_id=1, source_target_pairs={{0,1},{1,0},{2,3},{3,2},{4,5},{5,4},{6,7},{7,6},{8,9},{9,8},{10,11... | collective-permute-start | bytes 384008 | tf_op jit(solution)/shard_map/ppermute | solution.py:425
  298.1 34.2 %copy-start.6 = (bf16[320,200]{1,0:T(8,128)(2,1)}, bf16[320,200]{1,0:T(8,128)(2,1)S(1)}, u32[]{:S(2)}) copy-start(bf16[320,200]{1,0:T(8,128)(2,1)S(1)} %collective-permute-done.26.rest_2_) | copy-start | bytes 384004
  298.1 34.2 %collective-permute-start.29 = (bf16[320,200]{1,0:T(8,128)(2,1)S(1)}, bf16[320,200]{1,0:T(8,128)(2,1)S(1)}, u32[]{:S(2)}, u32[]{:S(2)}) collective-permute-start(bf16[320,200]{1,0:T(8,128)(2,1)S(1)} %collective-permute-done.26.rest_2_), channel_id=1, source_target_pairs={{0,1},{1,0},{2,3},{3,2},{4,5},{5,4},{6,7},{7,6},{8,9},{9,8},{10,11... | collective-permute-start | bytes 384008 | tf_op jit(solution)/shard_map/ppermute | solution.py:425
  298.7 33.6 %copy-start.7 = (bf16[320,200]{1,0:T(8,128)(2,1)}, bf16[320,200]{1,0:T(8,128)(2,1)S(1)}, u32[]{:S(2)}) copy-start(bf16[320,200]{1,0:T(8,128)(2,1)S(1)} %collective-permute-done.27.rest_3_) | copy-start | bytes 384004
  298.7 33.6 %collective-permute-start.30 = (bf16[320,200]{1,0:T(8,128)(2,1)S(1)}, bf16[320,200]{1,0:T(8,128)(2,1)S(1)}, u32[]{:S(2)}, u32[]{:S(2)}) collective-permute-start(bf16[320,200]{1,0:T(8,128)(2,1)S(1)} %collective-permute-done.27.rest_3_), channel_id=1, source_target_pairs={{0,1},{1,0},{2,3},{3,2},{4,5},{5,4},{6,7},{7,6},{8,9},{9,8},{10,11... | collective-permute-start | bytes 384008 | tf_op jit(solution)/shard_map/ppermute | solution.py:425
  (11 other events, 7.9 us)

commit v2 on v0

v2 whole, which is shorter than its diff:
```python
import functools

import jax
import jax.numpy as jnp
from jax import lax
from jax.experimental import pallas as pl
from jax.experimental.pallas import tpu as pltpu
from jax.sharding import Mesh, PartitionSpec as P

TERMS = 4
BF = jnp.bfloat16
F32 = jnp.float32
HIGH = lax.Precision.HIGHEST
VMEM_LIMIT = 56 * 1024 * 1024
SMEM = pl.BlockSpec(memory_space=pltpu.SMEM)
VMEM = pl.BlockSpec(memory_space=pltpu.VMEM)


def params(**more):
    return pltpu.CompilerParams(vmem_limit_bytes=VMEM_LIMIT, **more)


def taking(us):
    return pl.CostEstimate(flops=int(us * 1.15e9), bytes_accessed=1, transcendentals=0)


def mm(a, b, dims=((1,), (0,)), precision=None):
    return lax.dot_general(
        a, b, (dims, ((), ())), precision=precision, preferred_element_type=F32
    )


def shift(n, k):
    return [(q, (q + k) % n) for q in range(n)]


def theta_kernel(n, quarter, place, wanted, trial, walkers, *rest):
    own, (sent, c_ref, s_ref, y_ref, w_ref, h_ref, whole) = rest[:n], rest[n:]
    x_at, z_at, core = place[0], place[2], place[3]
    pair, rows = own[0].shape[:2]
    n_occ = trial.shape[0]
    ids = [lax.broadcasted_iota(jnp.int32, (n_occ, n_occ), d) for d in (0, 1)]
    eye = (ids[0] == ids[1]).astype(F32)
    for i in range(pair):
        w = walkers[pair * core + i]
        c = mm(trial[...], w, ((1,), (1,)))
        ct = mm(w, trial[...], ((1,), (1,)))
        c_ref[i] = ct
        g = jnp.abs(mm(c.astype(BF), ct.astype(BF)))
        side = jnp.max(jnp.sum(jnp.abs(c), axis=0)) * jnp.max(jnp.sum(jnp.abs(ct), axis=0))
        bound = jnp.max(jnp.sum(g, axis=0)) * 1.01 + side / 128.0
        start = c * (1.9 / jnp.full(ct.shape, bound, F32))
        s_ref[i] = start
        y_ref[i] = start

    def coarse(state):
        step, _ = state
        ys = [y_ref[i] for i in range(pair)]
        rs = [eye - mm(c_ref[i].astype(BF), ys[i].astype(BF)) for i in range(pair)]
        for i in range(pair):
            y_ref[i] = ys[i] + mm(ys[i].astype(BF), rs[i].astype(BF))
        return step + 1, sum(jnp.sum(r * r) for r in rs)

    def fine(state):
        step, _ = state
        ys = [y_ref[i] for i in range(pair)]
        rs = [eye - mm(c_ref[i], ys[i], precision=HIGH) for i in range(pair)]
        bs = [r.astype(BF) for r in rs]
        twos = [(rs[i] + mm(bs[i], bs[i])).astype(BF) for i in range(pair)]
        for i in range(pair):
            y_ref[i] = ys[i] + mm(ys[i].astype(BF), twos[i])
        return step + 1, sum(jnp.sum(r * r) for r in rs)

    def far(limit, tolerance):
        return lambda state: (state[0] < limit) & jnp.logical_not(state[1] < tolerance)

    begin = (jnp.int32(0), jnp.float32(1e30))
    lax.while_loop(far(14, 0.3), coarse, begin)
    _, left = lax.while_loop(far(6, 0.005), fine, begin)

    @pl.when(jnp.logical_not(left < 0.005))
    def _():
        y_ref[...] = s_ref[...]
        lax.while_loop(far(60, 0.005), fine, begin)

    for i in range(pair):
        inv = y_ref[i]
        high = inv.astype(BF)
        low = (inv - high.astype(F32)).astype(BF)
        w = walkers[pair * core + i]
        turned = mm(high, w) + mm(low, w)
        w_ref[i * n_occ : (i + 1) * n_occ, :] = turned
        h_ref[...] = turned.T.astype(BF)
        for j in range(n):
            block = lax.rem(x_at + j, n)
            own[j][i] = h_ref[pl.ds(pl.multiple_of(block * rows, rows), rows), :]
    whole[...] = w_ref[...].astype(BF)
    stride = (whole.shape[0] - quarter) // (n - 1)
    count = sent.shape[1] - quarter
    far = n_occ - count
    for j in range(n):
        sent[j, :quarter, :] = whole[pl.ds(pl.multiple_of(z_at * stride, stride), quarter), :]
        sent[j, quarter:, :] = walkers[wanted[j], pl.ds(pl.multiple_of(core * far, far), count), :]


def make_theta(place, wanted, trial, walkers, n, quarter, count):
    _, n_occ, n_orb = walkers.shape
    pair = walkers.shape[0] // 2
    return pl.pallas_call(
        functools.partial(theta_kernel, n, quarter),
        out_shape=[jax.ShapeDtypeStruct((pair, n_orb // n, n_occ), BF)] * n
        + [
            jax.ShapeDtypeStruct((n, quarter + count, n_orb), BF),
        ],
        in_specs=[SMEM, SMEM, VMEM, VMEM],
        out_specs=[VMEM] * (n + 1),
        scratch_shapes=[pltpu.VMEM((pair, n_occ, n_occ), F32)] * 3
        + [
            pltpu.VMEM((pair * n_occ, n_orb), F32),
            pltpu.VMEM((n_orb, n_occ), BF),
            pltpu.VMEM((pair * n_occ, n_orb), BF),
        ],
        compiler_params=params(),
        cost_estimate=taking(7.6),
        name="theta",
    )(place, wanted, trial, walkers)


def bias_kernel(n, place, mine, theirs, noise_mine, noise_theirs, *rest):
    thetas, (out, t_ref, acc) = rest[:n], rest[n:]
    x_at, core = place[0], place[3]
    pair, rows, n_occ = thetas[0].shape
    lanes = 32
    chunks = rows // lanes
    block = mine.shape[0]
    n_vec = acc.shape[1]
    walkers = out.shape[0]
    width = n * pair * lanes
    step = pl.program_id(0)
    sub = 8

    @pl.when(step == 0)
    def _():
        for k in range(n):
            for i in range(pair):
                at = (k * pair + i) * lanes
                t_ref[:, at : at + lanes, :] = thetas[k][i].reshape(chunks, lanes, n_occ)

    along = lax.broadcasted_iota(jnp.int32, (1, lanes // sub, sub, width), 3) % lanes
    row = sub * lax.broadcasted_iota(jnp.int32, along.shape, 1) + lax.broadcasted_iota(
        jnp.int32, along.shape, 2
    )
    for side, ref in enumerate((mine, theirs)):
        got = jnp.zeros((block * lanes, width), F32)
        for c in range(chunks):
            left = ref[:, c * lanes : (c + 1) * lanes, :].reshape(block * lanes, n_occ)
            got = got + mm(left, t_ref[c], ((1,), (1,)))
        got = got.reshape(block, lanes // sub, sub, width)
        kept = jnp.sum(jnp.where(along == row, got, 0.0), axis=1)
        acc[core if side == 0 else 1 - core, pl.ds(step * block, block)] = kept

    @pl.when(step == pl.num_programs(0) - 1)
    def _():
        lane = lax.broadcasted_iota(jnp.int32, (width, walkers), 0) // lanes
        column = lax.broadcasted_iota(jnp.int32, (width, walkers), 1)
        spot = pair * ((x_at - lane // pair + n) % n) + lane % pair
        sums = jnp.sum(acc[...].reshape(2 * n_vec, sub, width), axis=1)
        out[...] = -0.5 * mm((spot == column).astype(F32), sums, ((0,), (1,)), HIGH)
        own = pair_noise(place, noise_mine, noise_theirs, pair)
        row = lax.broadcasted_iota(jnp.int32, (walkers, pair), 0)
        which = lax.broadcasted_iota(jnp.int32, (walkers, pair), 1) + pair * x_at
        out[...] += mm((row == which).astype(F32), own, precision=HIGH)


def pair_noise(place, mine, theirs, pair):
    core = place[3]
    count, n_vec = mine.shape
    walker = lax.broadcasted_iota(jnp.int32, (pair, count), 1) - pair * core
    pick = (walker == lax.broadcasted_iota(jnp.int32, (pair, count), 0)).astype(F32)
    vec = lax.broadcasted_iota(jnp.int32, (n_vec, 2 * n_vec), 0)
    spot = lax.broadcasted_iota(jnp.int32, (n_vec, 2 * n_vec), 1)
    near = mm(mine[...], (vec + core * n_vec == spot).astype(F32), precision=HIGH)
    far = mm(theirs[...], (vec + (1 - core) * n_vec == spot).astype(F32), precision=HIGH)
    return mm(pick, near + far, precision=HIGH)


def make_bias(place, mine, theirs, noise_mine, noise_theirs, thetas, n):
    n_vec, rows, n_occ = mine.shape
    pair = thetas[0].shape[0]
    walkers = n * pair
    lanes = 32
    block = 14
    return pl.pallas_call(
        functools.partial(bias_kernel, n),
        out_shape=jax.ShapeDtypeStruct((walkers, 2 * n_vec), F32),
        grid=(n_vec // block,),
        in_specs=[SMEM]
        + [pl.BlockSpec((block, rows, n_occ), lambda s: (s, 0, 0))] * 2
        + [VMEM] * (2 + n),
        out_specs=VMEM,
        scratch_shapes=[
            pltpu.VMEM((rows // lanes, n * pair * lanes, n_occ), BF),
            pltpu.VMEM((2, n_vec, 8, n * pair * lanes), F32),
        ],
        compiler_params=params(),
        cost_estimate=taking(0.01),
        name="bias",
    )(place, mine, theirs, noise_mine, noise_theirs, *thetas)


def potential_kernel(n, place, near, far, noise_mine, noise_theirs, pick_near, pick_far, mine, theirs, *rest):
    outs = rest[:n]
    squares, a_ref = rest[n:]
    core = place[3]
    n_vec, lanes, n_orb = mine.shape
    x_at = place[0]
    slots = pick_near.shape[0]

    @pl.when(pl.program_id(0) == 0)
    def _():
        chosen = (
            mm(pick_near[...], near[...].astype(BF)) + mm(pick_far[...], far[...].astype(BF))
        ).astype(BF)
        pair = near.shape[0] // n
        row = lax.broadcasted_iota(jnp.int32, (pair, n * pair), 0) + pair * x_at
        which = lax.broadcasted_iota(jnp.int32, (pair, n * pair), 1)
        field = mm((row == which).astype(F32), near[...], precision=HIGH)
        bias = 2.0 * (pair_noise(place, noise_mine, noise_theirs, pair) - field)
        total = jnp.sum(bias * bias, axis=1, keepdims=True)
        lane = lax.broadcasted_iota(jnp.int32, (pair, slots), 1)
        walker = 2 * pair * x_at + pair * core + lax.broadcasted_iota(jnp.int32, (pair, slots), 0)
        spread = jnp.sum(jnp.where(lane == walker, 0.5 * total, 0.0), axis=0, keepdims=True)
        squares[...] = jnp.broadcast_to(spread, squares.shape)
        vec = lax.broadcasted_iota(jnp.int32, (n_vec, n_vec * lanes), 0)
        lane = lax.broadcasted_iota(jnp.int32, (n_vec, n_vec * lanes), 1)
        repeat = (lane // lanes == vec).astype(F32).astype(BF)
        sub = lax.broadcasted_iota(jnp.int32, (lanes, n_vec * lanes), 0)
        along = lax.broadcasted_iota(jnp.int32, (lanes, n_vec * lanes), 1) % lanes
        same = (sub == along).astype(F32)
        for c in range(2):
            wide = mm(chosen[:, c * n_vec : (c + 1) * n_vec], repeat)
            for s in range(slots):
                a_ref[c, s * lanes : (s + 1) * lanes, :] = (same * wide[s : s + 1, :]).astype(BF)

    got = mm(a_ref[core], mine[...].reshape(n_vec * lanes, n_orb)) + mm(
        a_ref[1 - core], theirs[...].reshape(n_vec * lanes, n_orb)
    )
    got = got.astype(BF).reshape(slots, lanes, n_orb)
    each = slots // n
    for k in range(n):
        outs[k][...] = got[k * each : (k + 1) * each]


def make_potential(place, small, mine, theirs, n):
    n_vec, rows, n_orb = mine.shape
    slots = small[-1].shape[0]
    half = rows // 2
    lanes = 16
    steps = half // lanes
    rows_of = pl.BlockSpec((n_vec, lanes, n_orb), lambda s, p: (0, p[3] * steps + s, 0))
    return pl.pallas_call(
        functools.partial(potential_kernel, n),
        out_shape=[jax.ShapeDtypeStruct((slots // n, half, n_orb), BF)] * n
        + [jax.ShapeDtypeStruct((8, slots), F32)],
        grid_spec=pltpu.PrefetchScalarGridSpec(
            num_scalar_prefetch=1,
            grid=(steps,),
            in_specs=[VMEM] * len(small) + [rows_of, rows_of],
            out_specs=[pl.BlockSpec((slots // n, lanes, n_orb), lambda s, p: (0, s, 0))] * n + [VMEM],
            scratch_shapes=[pltpu.VMEM((2, slots * lanes, n_vec * lanes), BF)],
        ),
        compiler_params=params(),
        cost_estimate=taking(0.01),
        name="potential",
    )(place, *small, mine, theirs)


def cross_kernel(n, pair, place, before, *rest):
    mine, theirs, halves = rest[:n], rest[n : 2 * n], rest[2 * n]
    out, t_ref, h_ref, p_ref, acc = rest[2 * n + 1 :]
    rows, n_occ = halves.shape[2:]
    z_at, core = place[2], place[3]
    block, count = pair * n_occ, mine[0].shape[1]
    stride = (block - count) // (n - 1)
    walkers = 2 * n * pair
    step = pl.program_id(0)

    @pl.when(step == 0)
    def _():
        acc[...] = jnp.zeros(acc.shape, F32)
        p_ref[...] = jnp.zeros(p_ref.shape, BF)
        for c, tables in enumerate((mine, theirs)):
            for j in range(n):
                start = stride * lax.rem(z_at - j + n, n)
                for k in range(n):
                    at = pl.multiple_of((c * n + k) * block + start, 16)
                    t_ref[pl.ds(at, count), :] = tables[j][k]

    def square():
        for w in range(walkers):
            p = p_ref[w]
            acc[w] += mm(p, p)

    for s in range(n):
        h_ref[s * rows : (s + 1) * rows, :] = halves[s, 0]
    square()
    for q in range(2 * n):
        got = mm(t_ref[q * block : (q + 1) * block, :], h_ref[...])
        for i in range(pair):
            p_ref[q * pair + i] = got[i * n_occ : (i + 1) * n_occ].astype(BF)

    @pl.when(step == pl.num_programs(0) - 1)
    def _():
        square()
        ids = [lax.broadcasted_iota(jnp.int32, (n_occ, n_occ), d) for d in (0, 1)]
        lane = lax.broadcasted_iota(jnp.int32, out.shape, 1)
        total = before[...]
        for c in range(2):
            for k in range(n):
                for i in range(pair):
                    got = acc[(c * n + k) * pair + i]
                    value = jnp.sum(jnp.where(ids[0] == ids[1], got, 0.0))
                    parity = core if c == 0 else 1 - core
                    walker = 2 * pair * k + pair * parity + i
                    total = total + jnp.where(lane == walker, -0.5 * value, 0.0)
        out[...] = total


def make_cross(place, before, tables, halves, n):
    _, steps, rows, n_occ = halves.shape
    n_orb = tables[0].shape[2]
    pair = 2
    walkers = 2 * n * pair
    return pl.pallas_call(
        functools.partial(cross_kernel, n, pair),
        out_shape=jax.ShapeDtypeStruct(before.shape, F32),
        grid=(steps,),
        in_specs=[SMEM]
        + [VMEM] * (2 * n + 1)
        + [pl.BlockSpec((n, 1, rows, n_occ), lambda s: (0, s, 0, 0))],
        out_specs=VMEM,
        scratch_shapes=[
            pltpu.VMEM((walkers * n_occ, n_orb), BF),
            pltpu.VMEM((n_orb, n_occ), BF),
            pltpu.VMEM((walkers, n_occ, n_occ), BF),
            pltpu.VMEM((walkers, n_occ, n_occ), F32),
        ],
        compiler_params=params(),
        cost_estimate=taking(0.5),
        name="cross",
    )(place, before, *tables, halves)


def taylor_kernel(n, place, chosen, walker, mine, theirs, out, v_ref):
    x_at, z_at, core = place[0], place[2], place[3]
    half = mine.shape[1]
    for k in range(n):
        block = lax.rem(z_at - k - x_at + 2 * n, n)
        v_ref[pl.ds(pl.multiple_of((2 * block + core) * half, half), half), :] = mine[k]
        v_ref[pl.ds(pl.multiple_of((2 * block + 1 - core) * half, half), half), :] = theirs[k]

    term = walker[0, walker.shape[1] - out.shape[0] :, :]
    total = term.astype(F32)
    for k in range(1, TERMS + 1):
        term = (mm(term, v_ref[...], ((1,), (1,))) / k).astype(BF)
        total = total + term.astype(F32)
    out[...] = total.astype(BF)


def make_taylor(place, chosen, walkers, mine, theirs, n, count):
    _, rows, n_orb = walkers.shape
    return pl.pallas_call(
        functools.partial(taylor_kernel, n),
        out_shape=jax.ShapeDtypeStruct((count, n_orb), BF),
        grid_spec=pltpu.PrefetchScalarGridSpec(
            num_scalar_prefetch=2,
            grid=(1,),
            in_specs=[pl.BlockSpec((1, rows, n_orb), lambda s, p, c: (c[0], 0, 0)), VMEM, VMEM],
            out_specs=VMEM,
            scratch_shapes=[pltpu.VMEM((n_orb, n_orb), BF)],
        ),
        compiler_params=params(),
        cost_estimate=taking(0.01),
        name="taylor",
    )(place, chosen, walkers, mine, theirs)


def join_kernel(n, place, mine, theirs, out):
    y_at, core = place[1], place[3]
    count = mine.shape[1]
    far = out.shape[1] - count
    for k in range(n):
        slot = lax.rem(y_at - k + n, n)
        out[slot, pl.ds(pl.multiple_of(core * far, far), count), :] = mine[k]
        out[slot, pl.ds(pl.multiple_of((1 - core) * far, far), count), :] = theirs[k]


def join(place, mine, theirs, n, n_occ):
    n_orb = mine.shape[2]
    return pl.pallas_call(
        functools.partial(join_kernel, n),
        out_shape=jax.ShapeDtypeStruct((n, n_occ, n_orb), BF),
        in_specs=[SMEM, VMEM, VMEM],
        out_specs=VMEM,
        compiler_params=params(),
        cost_estimate=taking(0.01),
        name="join",
    )(place, mine, theirs)


def after(value, *earlier):
    return lax.optimization_barrier((value, *earlier))[0]


def shards(walkers, trial, half_chol, chol_vectors, noise, copies):
    n = lax.axis_size("x")
    x, y, z, core = (lax.axis_index(a) for a in ("x", "y", "z", "core"))
    place = jnp.stack([x, y, z, core]).astype(jnp.int32)
    w_grp, n_orb, n_occ = walkers.shape
    n_vec = half_chol.shape[0]
    slots = w_grp * n
    walkers = walkers.transpose(0, 2, 1)
    trial = trial.T
    other_core = functools.partial(lax.ppermute, axis_name="core", perm=[(0, 1), (1, 0)])

    def along(v, axis, k):
        return lax.ppermute(v, axis, shift(n, k)) if k else v

    parent = jnp.sum(
        (jnp.cumsum(copies)[None, :] <= jnp.arange(slots, dtype=jnp.int32)[:, None]).astype(jnp.int32),
        axis=1,
    )

    noise_theirs = other_core(noise)
    half_theirs = other_core(half_chol)
    quarter, count = 112, 104
    wanted = jnp.clip(parent.reshape(n, w_grp)[:, y] - w_grp * x, 0, w_grp - 1)
    *own, sent = make_theta(place, wanted, trial, walkers, n, quarter, count)
    own = [own[0]] + [after(t, half_theirs, noise_theirs) for t in own[1:]]
    thetas = [along(own[k], "x", k) for k in range(n)]
    got = lax.all_to_all(after(sent, *thetas[1:]), "x", 0, 0, tiled=True)
    chol_theirs = other_core(after(chol_vectors, own[0], half_theirs, noise_theirs))

    share = make_bias(place, half_chol, half_theirs, noise, noise_theirs, thetas, n)
    near = lax.psum(share, "x")
    got = after(got, near)
    distant = other_core(near)
    by_x = half_chol.reshape((n, n_vec // n) + half_chol.shape[1:])
    halves = lax.all_to_all(after(by_x, near), "x", 0, 0, tiled=True)

    pieces = got[:, :quarter]
    after_one, before_one = along(pieces, "z", 1), along(pieces, "z", 3)
    opposite = jnp.concatenate(
        [along(after_one[: n // 2], "z", 1), along(before_one[n // 2 :], "z", 3)], axis=0
    )
    tables = [pieces, after_one, opposite, before_one]
    order = jnp.array([[k, m] for k in range(n) for m in range(n)], jnp.int32)
    slot = w_grp * ((z + order[:, 1] - x) % n) + (y + order[:, 0]) % n
    pairs = jnp.array([w_grp * a + i for a in range(n) for i in range(w_grp // 2)], jnp.int32)
    pick_near, pick_far = [
        (parent[slot][:, None] == (pairs + w_grp // 2 * c)[None, :]).astype(BF) for c in (core, 1 - core)
    ]
    small = (near, distant, noise, noise_theirs, pick_near, pick_far)
    *partials, running = make_potential(place, small, chol_vectors, chol_theirs, n)

    def added(parts):
        total = parts[0].astype(F32)
        for p in parts[1:]:
            total = total + p.astype(F32)
        return total.astype(BF)

    moved = [along(partials[k], "y", k) for k in range(n)]
    over_y = added([after(moved[0], *tables)] + moved[1:])
    piece = added([along(over_y[m], "z", m) for m in range(n)])
    plane = jnp.stack(
        [
            lax.ppermute(
                piece,
                ("x", "z"),
                [(n * a + b, n * ((b - a) % n) + (b + k) % n) for a in range(n) for b in range(n)],
            )
            for k in range(n)
        ]
    )
    plane_theirs = other_core(plane)
    tables = tables + [other_core(t) for t in tables]
    running = make_cross(place, after(running, plane), tables, halves, n)
    plane = after(plane, running)
    chosen = parent[x * w_grp + y].reshape(1) // w_grp
    mine = make_taylor(place, chosen, got, plane, plane_theirs, n, count)
    spread = jnp.stack([along(mine, "y", k) for k in range(n)])
    new_walkers = join(place, spread, other_core(spread), n, n_occ)

    energy = running[:1]
    for axis in ("x", "z", "y"):
        energy = sum([along(energy, axis, k) for k in range(n)])
        if axis == "x":
            energy = energy + other_core(energy)
    n_all = n_vec * 2 * n * n
    energies = lax.dynamic_slice_in_dim(energy[0], w_grp * x, w_grp) / n_all
    return new_walkers.transpose(0, 2, 1), energies


def solution(mesh):
    finer = Mesh(mesh.devices.reshape(4, 4, 4, 2), ("x", "y", "z", "core"))
    chol = ("y", "z", "core")
    placed = (
        P("x", None, None),
        P(),
        P(chol, "x", None),
        P(chol, "x", None),
        P("x", chol),
        P(),
    )
    return jax.shard_map(
        shards,
        mesh=finer,
        in_specs=placed,
        out_specs=(P("x", None, None), P("x")),
        check_vma=False,
    )
```

time: 664 us -> 191 us (0.29); the launches traced: 653 us -> 190 us
  other arithmetic: 224 us -> 5.97 us
  blocking collectives: 198 us -> 10.9 us
  local copies, waits for them, and re-layouts: 74.6 us -> 5.1 us
  Pallas kernels: 0 us -> 63.5 us
  matrix products: 62.9 us -> 0 us
  starting transfers between devices: 5.47 us -> 56.5 us
  waiting for transfers between devices: 72.8 us -> 44.5 us
  between operations: 14.6 us -> 3.59 us
    another operation x19 -> x5, other arithmetic: 194 us -> 1.8 us  [the longest x1 0.99 us: shards(): spread = jnp.stack([along(mine, 'y', k) for k in range(n)])]
    psum x1, blocking collectives: 154 us -> 10.9 us  [shards(): near = lax.psum(share, 'x')]
    all_to_all x1 -> x2, waiting for transfers between devices: 72.1 us -> 0.01 us  [the longest x1 0.01 us: shards(): halves = lax.all_to_all(after(by_x, near), 'x', 0, 0, tiled=True)]
    pallas_call x0 -> x6, Pallas kernels: none -> 63.5 us  [the longest x1 31.5 us: make_cross(): pl.pallas_call(functools.partial(cross_kernel, n, pair), out_shape=jax.Sh...]
    dot_general x10 -> x0, matrix products: 53.8 us -> none  [the longest x1 29.3 us: shards(): lax.dot_general(lax.all_gather(half_chol, 'walk', axis=1, tiled=True), ro...]
    unnamed x21 -> x37, local copies, waits for them, and re-layouts: 52.6 us -> 2.21 us
    ppermute x0 -> x40, starting transfers between devices: none -> 47.3 us  [the longest x25 40 us: along(): return lax.ppermute(v, axis, shift(n, k)) if k else v]
    ppermute x0 -> x40, waiting for transfers between devices: none -> 44.5 us  [the longest x25 35.6 us: along(): return lax.ppermute(v, axis, shift(n, k)) if k else v]
  transfers between devices with their start and end apart: 2 -> 42, of which waited for: 1 -> 17; matrix products, arithmetic and copies ran while one was open for 32% -> 5% of each run, Pallas kernels for 0% -> 32%
where the time goes in v2:
time: 191 us; the launch traced here: 190 us
  Pallas kernels  63.5 us (33%)
  starting transfers between devices  56.5 us (30%)
  waiting for transfers between devices  44.5 us (23%)
  blocking collectives  10.9 us (6%)
  other arithmetic  5.97 us (3%)
  local copies, waits for them, and re-layouts  5.1 us (3%)
  between operations  3.59 us (2%)
    ppermute x25, starting transfers between devices, along(): return lax.ppermute(v, axis, shift(n, k)) if k else v  40 us
    ppermute x25, waiting for transfers between devices, along(): return lax.ppermute(v, axis, shift(n, k)) if k else v  35.6 us
    pallas_call x1, Pallas kernels, make_cross(): pl.pallas_call(functools.partial(cross_kernel, n, pair), out_shape=jax.Sh...  31.5 us
    psum x1, blocking collectives, shards(): near = lax.psum(share, 'x')  10.9 us
    pallas_call x1, Pallas kernels, make_potential(): pl.pallas_call(functools.partial(potential_kernel, n), out_shape=[jax.Sha...  10 us
    pallas_call x1, Pallas kernels, make_theta(): pl.pallas_call(functools.partial(theta_kernel, n, quarter), out_shape=[ja...  8.41 us
    ppermute x4, waiting for transfers between devices, shards(): lax.ppermute(piece, ('x', 'z'), [(n * a + b, n * ((b - a) % n) + (b + k)...  7.76 us
    pallas_call x1, Pallas kernels, make_bias(): pl.pallas_call(functools.partial(bias_kernel, n), out_shape=jax.ShapeDtyp...  7.49 us
  transfers between devices with their start and end apart: 42, of which 17 were waited for; matrix products, arithmetic and copies ran while one was open for 5% of the time, Pallas kernels for 32%

profile of v2, /device:TPU:0, one launch (start us, length us, event | category | flops | bytes accessed | tf_op | source)
XLA Modules:
  0.0 190.1 jit_solution(12107121539030326106)
XLA Ops:
  0.7 0.5 collective-permute-start.1
  1.2 0.7 copy.13
  2.3 0.8 clamp_reduce_fusion.wanted
  3.1 0.6 pad_add_fusion.place
  3.7 8.4 %theta.1 = (bf16[2,160,200]{2,1,0:T(8,128)(2,1)}, bf16[2,160,200]{2,1,0:T(8,128)(2,1)}, bf16[2,160,200]{2,1,0:T(8,128)(2,1)}, bf16[2,160,200]{2,1,0:T(8,128)(2,1)}, bf16[4,216,640]{2,1,0:T(8,128)(2,1)}) custom-call(s32[4]{0:T(128)} %pad_add_fusion.place, s32[4]{0:T(128)} %clamp_reduce_fusion.wanted, bf16[200,640]{1,0:T(8,128)(2,1)} %bitcast.44, ...), custom_call_target="tpu_custom_call" | custom-call | flops 8739999744 | bytes 1 | tf_op jit(solution)/shard_map/theta/pallas_call | solution.py:109
  12.3 2.1 %collective-permute-start.2 = (bf16[2,160,200]{2,1,0:T(8,128)(2,1)}, bf16[2,160,200]{2,1,0:T(8,128)(2,1)S(1)}, u32[]{:S(2)}, u32[]{:S(2)}) collective-permute-start(bf16[2,160,200]{2,1,0:T(8,128)(2,1)} %get-tuple-element.24), channel_id=1, source_target_pairs={{0,32},{32,64},{64,96},{96,0},{1,33},{33,65},{65,97},{97,1},{2,34}... | collective-permute-start | bytes 384008 | tf_op jit(solution)/shard_map/ppermute | solution.py:427
  14.4 2.2 %collective-permute-start.3 = (bf16[2,160,200]{2,1,0:T(8,128)(2,1)}, bf16[2,160,200]{2,1,0:T(8,128)(2,1)S(1)}, u32[]{:S(2)}, u32[]{:S(2)}) collective-permute-start(bf16[2,160,200]{2,1,0:T(8,128)(2,1)} %get-tuple-element.26), channel_id=1, source_target_pairs={{0,64},{32,96},{64,0},{96,32},{1,65},{33,97},{65,1},{97,33},{2,66}... | collective-permute-start | bytes 384008 | tf_op jit(solution)/shard_map/ppermute | solution.py:427
  16.6 2.0 %collective-permute-start.4 = (bf16[2,160,200]{2,1,0:T(8,128)(2,1)}, bf16[2,160,200]{2,1,0:T(8,128)(2,1)S(1)}, u32[]{:S(2)}, u32[]{:S(2)}) collective-permute-start(bf16[2,160,200]{2,1,0:T(8,128)(2,1)} %get-tuple-element.28), channel_id=1, source_target_pairs={{0,96},{32,0},{64,32},{96,64},{1,97},{33,1},{65,33},{97,65},{2,98}... | collective-permute-start | bytes 384008 | tf_op jit(solution)/shard_map/ppermute | solution.py:427
  18.6 1.7 collective-permute-done.2.rest_1_
  20.3 4.6 %collective-permute-done.3.rest_2_ = bf16[2,160,200]{2,1,0:T(8,128)(2,1)S(1)} collective-permute-done((bf16[2,160,200]{2,1,0:T(8,128)(2,1)}, bf16[2,160,200]{2,1,0:T(8,128)(2,1)S(1)}, u32[]{:S(2)}, u32[]{:S(2)}) %collective-permute-start.3) | collective-permute-done | bytes 128032 | tf_op jit(solution)/shard_map/ppermute | solution.py:427
  24.8 4.1 %all-to-all-start = ((bf16[4,216,640]{2,1,0:T(8,128)(2,1)}), bf16[4,216,640]{2,1,0:T(8,128)(2,1)S(1)}, u32[]{:S(2)}, u32[]{:S(2)}) async-start(bf16[4,216,640]{2,1,0:T(8,128)(2,1)} %get-tuple-element.29), calls=%async_computation | async-start | bytes 2211840 | tf_op jit(solution)/shard_map/all_to_all | solution.py:441
  29.0 7.5 %bias.1 = f32[8,112]{1,0:T(8,128)} custom-call(s32[4]{0:T(128)} %pad_add_fusion.place, bf16[56,160,200]{2,1,0:T(8,128)(2,1)} %mine.2, bf16[56,160,200]{2,1,0:T(8,128)(2,1)} %collective-permute-done.theirs, f32[4,56]{1,0:T(4,128)} %noise_mine.3, f32[4,56]{1,0:T(4,128)} %copy-done.13, bf16[2,160,200]{2,1,0:T(8,128)(2,1)} %get-tuple-element.30.rest_0_, ...), custom_call_target="tpu_custom_call" | custom-call | flops 11500000 | bytes 1 | tf_op jit(solution)/shard_map/bias/pallas_call | solution.py:193
  36.5 10.9 %psum.7.near = f32[8,112]{1,0:T(8,128)S(1)} all-reduce(f32[8,112]{1,0:T(8,128)} %bias.1), channel_id=1, replica_groups=mesh['x'=4,'y'=4,'z'=4,'core'=2] {'x'}, use_global_device_ids=true, to_apply=%region_2.3 | all-reduce | flops 896 | bytes 7168 | tf_op jit(solution)/shard_map/psum | solution.py:445
  47.5 2.0 %collective-permute-start.7 = (bf16[4,112,640]{2,1,0:T(8,128)(2,1)S(1)}, bf16[4,112,640]{2,1,0:T(8,128)(2,1)S(1)}, u32[]{:S(2)}, u32[]{:S(2)}) collective-permute-start(bf16[4,112,640]{2,1,0:T(8,128)(2,1)S(1)} %slice.32.rest_0_), channel_id=1, source_target_pairs={{0,2},{2,4},{4,6},{6,0},{1,3},{3,5},{5,7},{7,1},{8,10},{10,12},{12... | collective-permute-start | bytes 1720328 | tf_op jit(solution)/shard_map/ppermute | solution.py:427
  49.5 5.1 %all-to-all-start.1 = ((bf16[4,14,160,200]{3,2,1,0:T(8,128)(2,1)}), bf16[4,14,160,200]{3,2,1,0:T(8,128)(2,1)}, u32[]{:S(2)}, u32[]{:S(2)}) async-start(bf16[4,14,160,200]{3,2,1,0:T(8,128)(2,1)} %bitcast.32), calls=%async_computation.1 | async-start | bytes 9175040 | tf_op jit(solution)/shard_map/all_to_all | solution.py:449
  54.6 2.9 %collective-permute-start.9 = (bf16[4,112,640]{2,1,0:T(8,128)(2,1)S(1)}, bf16[4,112,640]{2,1,0:T(8,128)(2,1)S(1)}, u32[]{:S(2)}, u32[]{:S(2)}) collective-permute-start(bf16[4,112,640]{2,1,0:T(8,128)(2,1)S(1)} %slice.32.rest_0_), channel_id=1, source_target_pairs={{0,6},{2,0},{4,2},{6,4},{1,7},{3,1},{5,3},{7,5},{8,14},{10,8},{12,... | collective-permute-start | bytes 1720328 | tf_op jit(solution)/shard_map/ppermute | solution.py:427
  57.5 0.7 gather_fusion
  58.3 3.9 %collective-permute-done.7.rest_1_ = bf16[4,112,640]{2,1,0:T(8,128)(2,1)S(1)} collective-permute-done((bf16[4,112,640]{2,1,0:T(8,128)(2,1)S(1)}, bf16[4,112,640]{2,1,0:T(8,128)(2,1)S(1)}, u32[]{:S(2)}, u32[]{:S(2)}) %collective-permute-start.7) | collective-permute-done | bytes 573472 | tf_op jit(solution)/shard_map/ppermute | solution.py:427
  62.3 0.7 compare_convert_fusion
  63.0 0.6 copy-done.14
  63.6 10.0 %potential.1 = (bf16[4,80,640]{2,1,0:T(8,128)(2,1)}, bf16[4,80,640]{2,1,0:T(8,128)(2,1)}, bf16[4,80,640]{2,1,0:T(8,128)(2,1)}, bf16[4,80,640]{2,1,0:T(8,128)(2,1)}, f32[8,16]{1,0:T(8,128)}) custom-call(s32[4]{0:T(128)} %pad_add_fusion.place, f32[8,112]{1,0:T(8,128)} %copy-done.12, f32[8,112]{1,0:T(8,128)} %copy-done.14, f32[4,56]{1,0:T(4,128)} %noise_mine.3, ...), custom_call_target="tpu_custom_call" | custom-call | flops 11500000 | bytes 1 | tf_op jit(solution)/shard_map/potential/pallas_call | solution.py:261
  73.6 3.1 %collective-permute-start.13 = (bf16[4,80,640]{2,1,0:T(8,128)(2,1)}, bf16[4,80,640]{2,1,0:T(8,128)(2,1)S(1)}, u32[]{:S(2)}, u32[]{:S(2)}) collective-permute-start(bf16[4,80,640]{2,1,0:T(8,128)(2,1)} %get-tuple-element.37), channel_id=1, source_target_pairs={{0,24},{8,0},{16,8},{24,16},{1,25},{9,1},{17,9},{25,17},{2,26},{10... | collective-permute-start | bytes 1228808 | tf_op jit(solution)/shard_map/ppermute | solution.py:427
  76.7 0.6 collective-permute-start.12
  77.4 1.0 collective-permute-start.11
  78.4 3.3 %collective-permute-start.10 = (bf16[2,112,640]{2,1,0:T(8,128)(2,1)S(1)}, bf16[2,112,640]{2,1,0:T(8,128)(2,1)S(1)}, u32[]{:S(2)}, u32[]{:S(2)}) collective-permute-start(bf16[2,112,640]{2,1,0:T(8,128)(2,1)S(1)} %slice.43), channel_id=1, source_target_pairs={{0,6},{2,0},{4,2},{6,4},{1,7},{3,1},{5,3},{7,5},{8,14},{10,8},{12,... | collective-permute-start | bytes 860168 | tf_op jit(solution)/shard_map/ppermute | solution.py:427
  81.6 4.1 %collective-permute-done.10 = bf16[2,112,640]{2,1,0:T(8,128)(2,1)S(1)} collective-permute-done((bf16[2,112,640]{2,1,0:T(8,128)(2,1)S(1)}, bf16[2,112,640]{2,1,0:T(8,128)(2,1)S(1)}, u32[]{:S(2)}, u32[]{:S(2)}) %collective-permute-start.10) | collective-permute-done | bytes 286752 | tf_op jit(solution)/shard_map/ppermute | solution.py:427
  85.8 5.7 %collective-permute-done.13 = bf16[4,80,640]{2,1,0:T(8,128)(2,1)S(1)} collective-permute-done((bf16[4,80,640]{2,1,0:T(8,128)(2,1)}, bf16[4,80,640]{2,1,0:T(8,128)(2,1)S(1)}, u32[]{:S(2)}, u32[]{:S(2)}) %collective-permute-start.13) | collective-permute-done | bytes 409632 | tf_op jit(solution)/shard_map/ppermute | solution.py:427
  91.5 3.6 %collective-permute-done.11 = bf16[4,80,640]{2,1,0:T(8,128)(2,1)S(1)} collective-permute-done((bf16[4,80,640]{2,1,0:T(8,128)(2,1)}, bf16[4,80,640]{2,1,0:T(8,128)(2,1)S(1)}, u32[]{:S(2)}, u32[]{:S(2)}) %collective-permute-start.11) | collective-permute-done | bytes 409632 | tf_op jit(solution)/shard_map/ppermute | solution.py:427
  95.1 1.2 add_convert_fusion
  96.3 3.0 %collective-permute-start.16 = (bf16[80,640]{1,0:T(8,128)(2,1)S(1)}, bf16[80,640]{1,0:T(8,128)(2,1)S(1)}, u32[]{:S(2)}, u32[]{:S(2)}) collective-permute-start(bf16[80,640]{1,0:T(8,128)(2,1)S(1)} %get-tuple-element.43), channel_id=1, source_target_pairs={{0,6},{2,0},{4,2},{6,4},{1,7},{3,1},{5,3},{7,5},{8,14},{10,8},{12,... | collective-permute-start | bytes 307208 | tf_op jit(solution)/shard_map/ppermute | solution.py:427
  99.4 1.0 collective-permute-start.14
  100.4 3.0 %collective-permute-done.16 = bf16[80,640]{1,0:T(8,128)(2,1)S(1)} collective-permute-done((bf16[80,640]{1,0:T(8,128)(2,1)S(1)}, bf16[80,640]{1,0:T(8,128)(2,1)S(1)}, u32[]{:S(2)}, u32[]{:S(2)}) %collective-permute-start.16) | collective-permute-done | bytes 102432 | tf_op jit(solution)/shard_map/ppermute | solution.py:427
  103.4 2.7 %collective-permute-done.15 = bf16[80,640]{1,0:T(8,128)(2,1)S(1)} collective-permute-done((bf16[80,640]{1,0:T(8,128)(2,1)S(1)}, bf16[80,640]{1,0:T(8,128)(2,1)S(1)}, u32[]{:S(2)}, u32[]{:S(2)}) %collective-permute-start.15) | collective-permute-done | bytes 102432 | tf_op jit(solution)/shard_map/ppermute | solution.py:427
  106.1 0.7 collective-permute-done.14
  106.9 1.0 collective-permute-start.20
  107.9 3.4 %collective-permute-start.19 = (bf16[80,640]{1,0:T(8,128)(2,1)S(1)}, bf16[80,640]{1,0:T(8,128)(2,1)S(1)}, u32[]{:S(2)}, u32[]{:S(2)}) collective-permute-start(bf16[80,640]{1,0:T(8,128)(2,1)S(1)} %fusion.2), channel_id=1, source_target_pairs={{0,4},{2,38},{4,64},{6,98},{32,100},{34,6},{36,32},{38,66},{64,68}... | collective-permute-start | bytes 307208 | tf_op jit(solution)/shard_map/ppermute | solution.py:477
  111.6 0.7 collective-permute-start.17
  112.9 3.6 %collective-permute-done.19 = bf16[80,640]{1,0:T(8,128)(2,1)S(1)} collective-permute-done((bf16[80,640]{1,0:T(8,128)(2,1)S(1)}, bf16[80,640]{1,0:T(8,128)(2,1)S(1)}, u32[]{:S(2)}, u32[]{:S(2)}) %collective-permute-start.19) | collective-permute-done | bytes 102432 | tf_op jit(solution)/shard_map/ppermute | solution.py:477
  116.4 4.0 %collective-permute-done.18 = bf16[80,640]{1,0:T(8,128)(2,1)S(1)} collective-permute-done((bf16[80,640]{1,0:T(8,128)(2,1)S(1)}, bf16[80,640]{1,0:T(8,128)(2,1)S(1)}, u32[]{:S(2)}, u32[]{:S(2)}) %collective-permute-start.18) | collective-permute-done | bytes 102432 | tf_op jit(solution)/shard_map/ppermute | solution.py:477
  120.5 0.6 collective-permute-start.25
  121.1 0.6 dynamic_slice.9
  124.4 0.7 copy-done.7
  125.1 31.5 %cross.1 = f32[8,16]{1,0:T(8,128)} custom-call(s32[4]{0:T(128)} %pad_add_fusion.place, f32[8,16]{1,0:T(8,128)} %get-tuple-element.39.before, bf16[4,112,640]{2,1,0:T(8,128)(2,1)} %copy-done.1, bf16[4,112,640]{2,1,0:T(8,128)(2,1)} %copy-done.4, bf16[4,112,640]{2,1,0:T(8,128)(2,1)} %copy-done.6, bf16[4,112,640]{2,1,0:T(8,128)(2,1)} %copy-done.5, ...), custom_call_target="tpu_custom_call" | custom-call | flops 575000000 | bytes 1 | tf_op jit(solution)/shard_map/cross/pallas_call | solution.py:334
  156.6 0.7 slice.39
  157.3 2.7 %collective-permute-start.32 = (f32[1,16]{1,0:T(1,128)S(1)}, f32[1,16]{1,0:T(1,128)S(1)}, u32[]{:S(2)}, u32[]{:S(2)}) collective-permute-start(f32[1,16]{1,0:T(1,128)S(1)} %slice.39), channel_id=1, source_target_pairs={{0,96},{32,0},{64,32},{96,64},{1,97},{33,1},{65,33},{97,65},{2,98}... | collective-permute-start | bytes 200 | tf_op jit(solution)/shard_map/ppermute | solution.py:427
  160.0 0.9 collective-permute-start.30
  160.8 3.7 %taylor.1 = bf16[104,640]{1,0:T(8,128)(2,1)} custom-call(s32[4]{0:T(128)} %pad_add_fusion.place, s32[1]{0:T(128)S(6)} %select_n.33.chosen, bf16[4,216,640]{2,1,0:T(8,128)(2,1)} %copy-done, bf16[4,80,640]{2,1,0:T(8,128)(2,1)} %copy-done.3, bf16[4,80,640]{2,1,0:T(8,128)(2,1)} %collective-permute-done.25.theirs), custom_call_target="tpu_custom_call" | custom-call | flops 11500000 | bytes 1 | tf_op jit(solution)/shard_map/taylor/pallas_call | solution.py:372
  164.7 0.6 collective-permute-start.27
  165.3 1.3 collective-permute-start.26
  166.6 0.7 add_add_fusion.2
  167.3 1.1 collective-permute-done.33
  168.4 1.4 collective-permute-start.36
  169.8 2.9 %collective-permute-start.35 = (f32[1,16]{1,0:T(1,128)S(1)}, f32[1,16]{1,0:T(1,128)S(1)}, u32[]{:S(2)}, u32[]{:S(2)}) collective-permute-start(f32[1,16]{1,0:T(1,128)S(1)} %add.134), channel_id=1, source_target_pairs={{0,4},{2,6},{4,0},{6,2},{1,5},{3,7},{5,1},{7,3},{8,12},{10,14},{12... | collective-permute-start | bytes 200 | tf_op jit(solution)/shard_map/ppermute | solution.py:427
  172.8 1.4 collective-permute-start.34
  174.5 1.0 pad_maximum_fusion.mine
  175.6 1.9 %collective-permute-done.34 = f32[1,16]{1,0:T(1,128)S(1)} collective-permute-done((f32[1,16]{1,0:T(1,128)S(1)}, f32[1,16]{1,0:T(1,128)S(1)}, u32[]{:S(2)}, u32[]{:S(2)}) %collective-permute-start.34) | collective-permute-done | bytes 96 | tf_op jit(solution)/shard_map/ppermute | solution.py:427
  177.6 2.6 %collective-permute-start.39 = (f32[1,16]{1,0:T(1,128)S(1)}, f32[1,16]{1,0:T(1,128)S(1)}, u32[]{:S(2)}, u32[]{:S(2)}) collective-permute-start(f32[1,16]{1,0:T(1,128)S(1)} %add_add_fusion.1), channel_id=1, source_target_pairs={{0,24},{8,0},{16,8},{24,16},{1,25},{9,1},{17,9},{25,17},{2,26},{10... | collective-permute-start | bytes 200 | tf_op jit(solution)/shard_map/ppermute | solution.py:427
  180.1 1.5 collective-permute-start.38
  181.7 1.3 collective-permute-start.37
  183.0 2.2 %collective-permute-done.38 = f32[1,16]{1,0:T(1,128)S(1)} collective-permute-done((f32[1,16]{1,0:T(1,128)S(1)}, f32[1,16]{1,0:T(1,128)S(1)}, u32[]{:S(2)}, u32[]{:S(2)}) %collective-permute-start.38) | collective-permute-done | bytes 96 | tf_op jit(solution)/shard_map/ppermute | solution.py:427
  185.2 1.2 collective-permute-done.37
  186.4 0.6 multiply_bitcast_fusion
  187.0 0.8 copy-done.8
  187.8 2.3 %join.1 = bf16[4,200,640]{2,1,0:T(8,128)(2,1)} custom-call(s32[4]{0:T(128)} %pad_add_fusion.place, bf16[4,104,640]{2,1,0:T(8,128)(2,1)} %copy-done.2, bf16[4,104,640]{2,1,0:T(8,128)(2,1)} %copy-done.8), custom_call_target="tpu_custom_call" | custom-call | flops 11500000 | bytes 1 | tf_op jit(solution)/shard_map/join/pallas_call | solution.py:400
  (92 shorter events, 2.8 us)
Async XLA Ops:
  0.6 11.5 %collective-permute-start = (bf16[56,160,200]{2,1,0:T(8,128)(2,1)}, bf16[56,160,200]{2,1,0:T(8,128)(2,1)}, u32[]{:S(2)}, u32[]{:S(2)}) collective-permute-start(bf16[56,160,200]{2,1,0:T(8,128)(2,1)} %mine.2), channel_id=1, source_target_pairs={{0,1},{1,0},{2,3},{3,2},{4,5},{5,4},{6,7},{7,6},{8,9},{9,8},{10,11... | collective-permute-start | bytes 10752008 | tf_op jit(solution)/shard_map/ppermute | solution.py:435
  0.7 11.4 %collective-permute-start.1 = (f32[4,56]{1,0:T(4,128)}, f32[4,56]{1,0:T(4,128)S(1)}, u32[]{:S(2)}, u32[]{:S(2)}) collective-permute-start(f32[4,56]{1,0:T(4,128)} %noise_mine.3), channel_id=1, source_target_pairs={{0,1},{1,0},{2,3},{3,2},{4,5},{5,4},{6,7},{7,6},{8,9},{9,8},{10,11... | collective-permute-start | bytes 2696 | tf_op jit(solution)/shard_map/ppermute | solution.py:434
  12.1 16.8 %copy-start.13 = (f32[4,56]{1,0:T(4,128)}, f32[4,56]{1,0:T(4,128)S(1)}, u32[]{:S(2)}) copy-start(f32[4,56]{1,0:T(4,128)S(1)} %collective-permute-done.1.noise_theirs) | copy-start | bytes 2692
  12.1 50.9 %collective-permute-start.6 = (bf16[56,160,640]{2,1,0:T(8,128)(2,1)}, bf16[56,160,640]{2,1,0:T(8,128)(2,1)}, u32[]{:S(2)}, u32[]{:S(2)}) collective-permute-start(bf16[56,160,640]{2,1,0:T(8,128)(2,1)} %mine.3), channel_id=1, source_target_pairs={{0,1},{1,0},{2,3},{3,2},{4,5},{5,4},{6,7},{7,6},{8,9},{9,8},{10,11... | collective-permute-start | bytes 34406408 | tf_op jit(solution)/shard_map/ppermute | solution.py:442
  12.3 8.0 %collective-permute-start.2 = (bf16[2,160,200]{2,1,0:T(8,128)(2,1)}, bf16[2,160,200]{2,1,0:T(8,128)(2,1)S(1)}, u32[]{:S(2)}, u32[]{:S(2)}) collective-permute-start(bf16[2,160,200]{2,1,0:T(8,128)(2,1)} %get-tuple-element.24), channel_id=1, source_target_pairs={{0,32},{32,64},{64,96},{96,0},{1,33},{33,65},{65,97},{97,1},{2,34}... | collective-permute-start | bytes 384008 | tf_op jit(solution)/shard_map/ppermute | solution.py:427
  14.4 10.4 %collective-permute-start.3 = (bf16[2,160,200]{2,1,0:T(8,128)(2,1)}, bf16[2,160,200]{2,1,0:T(8,128)(2,1)S(1)}, u32[]{:S(2)}, u32[]{:S(2)}) collective-permute-start(bf16[2,160,200]{2,1,0:T(8,128)(2,1)} %get-tuple-element.26), channel_id=1, source_target_pairs={{0,64},{32,96},{64,0},{96,32},{1,65},{33,97},{65,1},{97,33},{2,66}... | collective-permute-start | bytes 384008 | tf_op jit(solution)/shard_map/ppermute | solution.py:427
  16.6 8.2 %collective-permute-start.4 = (bf16[2,160,200]{2,1,0:T(8,128)(2,1)}, bf16[2,160,200]{2,1,0:T(8,128)(2,1)S(1)}, u32[]{:S(2)}, u32[]{:S(2)}) collective-permute-start(bf16[2,160,200]{2,1,0:T(8,128)(2,1)} %get-tuple-element.28), channel_id=1, source_target_pairs={{0,96},{32,0},{64,32},{96,64},{1,97},{33,1},{65,33},{97,65},{2,98}... | collective-permute-start | bytes 384008 | tf_op jit(solution)/shard_map/ppermute | solution.py:427
  20.2 8.7 %copy-start.9 = (bf16[2,160,200]{2,1,0:T(8,128)(2,1)}, bf16[2,160,200]{2,1,0:T(8,128)(2,1)S(1)}, u32[]{:S(2)}) copy-start(bf16[2,160,200]{2,1,0:T(8,128)(2,1)S(1)} %collective-permute-done.2.rest_1_) | copy-start | bytes 384004
  24.8 4.1 %copy-start.10 = (bf16[2,160,200]{2,1,0:T(8,128)(2,1)}, bf16[2,160,200]{2,1,0:T(8,128)(2,1)S(1)}, u32[]{:S(2)}) copy-start(bf16[2,160,200]{2,1,0:T(8,128)(2,1)S(1)} %collective-permute-done.3.rest_2_) | copy-start | bytes 384004
  24.8 4.1 %copy-start.11 = (bf16[2,160,200]{2,1,0:T(8,128)(2,1)}, bf16[2,160,200]{2,1,0:T(8,128)(2,1)S(1)}, u32[]{:S(2)}) copy-start(bf16[2,160,200]{2,1,0:T(8,128)(2,1)S(1)} %collective-permute-done.4.rest_3_) | copy-start | bytes 384004
  24.8 22.6 %all-to-all-start = ((bf16[4,216,640]{2,1,0:T(8,128)(2,1)}), bf16[4,216,640]{2,1,0:T(8,128)(2,1)S(1)}, u32[]{:S(2)}, u32[]{:S(2)}) async-start(bf16[4,216,640]{2,1,0:T(8,128)(2,1)} %get-tuple-element.29), calls=%async_computation | async-start | bytes 2211840 | tf_op jit(solution)/shard_map/all_to_all | solution.py:441
  47.4 10.8 %copy-start.12 = (f32[8,112]{1,0:T(8,128)}, f32[8,112]{1,0:T(8,128)S(1)}, u32[]{:S(2)}) copy-start(f32[8,112]{1,0:T(8,128)S(1)} %psum.7.near) | copy-start | bytes 10756
  47.4 2.1 %copy-start = (bf16[4,216,640]{2,1,0:T(8,128)(2,1)}, bf16[4,216,640]{2,1,0:T(8,128)(2,1)S(1)}, u32[]{:S(2)}) copy-start(bf16[4,216,640]{2,1,0:T(8,128)(2,1)S(1)} %all-to-all-done.walker) | copy-start | bytes 3317764
  47.5 64.8 %copy-start.1 = (bf16[4,112,640]{2,1,0:T(8,128)(2,1)}, bf16[4,112,640]{2,1,0:T(8,128)(2,1)S(1)}, u32[]{:S(2)}) copy-start(bf16[4,112,640]{2,1,0:T(8,128)(2,1)S(1)} %slice.32.rest_0_) | copy-start | bytes 1720324
  47.5 14.7 %collective-permute-start.7 = (bf16[4,112,640]{2,1,0:T(8,128)(2,1)S(1)}, bf16[4,112,640]{2,1,0:T(8,128)(2,1)S(1)}, u32[]{:S(2)}, u32[]{:S(2)}) collective-permute-start(bf16[4,112,640]{2,1,0:T(8,128)(2,1)S(1)} %slice.32.rest_0_), channel_id=1, source_target_pairs={{0,2},{2,4},{4,6},{6,0},{1,3},{3,5},{5,7},{7,1},{8,10},{10,12},{12... | collective-permute-start | bytes 1720328 | tf_op jit(solution)/shard_map/ppermute | solution.py:427
  49.5 8.0 %copy-start.16 = (s32[16,1]{0,1:T(1,128)S(1)}, s32[16,1]{0,1:T(1,128)}, u32[]{:S(2)}) copy-start(s32[16,1]{0,1:T(1,128)} %constant.84) | copy-start | bytes 196
  49.5 8.0 %copy-start.17 = (s32[16,1]{0,1:T(1,128)S(1)}, s32[16,1]{0,1:T(1,128)}, u32[]{:S(2)}) copy-start(s32[16,1]{0,1:T(1,128)} %constant.83) | copy-start | bytes 196
  49.5 8.7 %copy-start.15 = (s32[8]{0:T(128)S(1)}, s32[8]{0:T(128)}, u32[]{:S(2)}) copy-start(s32[8]{0:T(128)} %constant.79.clone) | copy-start | bytes 100
  49.5 74.8 %all-to-all-start.1 = ((bf16[4,14,160,200]{3,2,1,0:T(8,128)(2,1)}), bf16[4,14,160,200]{3,2,1,0:T(8,128)(2,1)}, u32[]{:S(2)}, u32[]{:S(2)}) async-start(bf16[4,14,160,200]{3,2,1,0:T(8,128)(2,1)} %bitcast.32), calls=%async_computation.1 | async-start | bytes 9175040 | tf_op jit(solution)/shard_map/all_to_all | solution.py:449
  54.6 23.7 %collective-permute-start.9 = (bf16[4,112,640]{2,1,0:T(8,128)(2,1)S(1)}, bf16[4,112,640]{2,1,0:T(8,128)(2,1)S(1)}, u32[]{:S(2)}, u32[]{:S(2)}) collective-permute-start(bf16[4,112,640]{2,1,0:T(8,128)(2,1)S(1)} %slice.32.rest_0_), channel_id=1, source_target_pairs={{0,6},{2,0},{4,2},{6,4},{1,7},{3,1},{5,3},{7,5},{8,14},{10,8},{12,... | collective-permute-start | bytes 1720328 | tf_op jit(solution)/shard_map/ppermute | solution.py:427
  58.2 4.8 %collective-permute-start.5 = (f32[8,112]{1,0:T(8,128)S(1)}, f32[8,112]{1,0:T(8,128)S(1)}, u32[]{:S(2)}, u32[]{:S(2)}) collective-permute-start(f32[8,112]{1,0:T(8,128)S(1)} %psum.7.near), channel_id=1, source_target_pairs={{0,1},{1,0},{2,3},{3,2},{4,5},{5,4},{6,7},{7,6},{8,9},{9,8},{10,11... | collective-permute-start | bytes 10760 | tf_op jit(solution)/shard_map/ppermute | solution.py:447
  62.2 50.4 %copy-start.4 = (bf16[4,112,640]{2,1,0:T(8,128)(2,1)}, bf16[4,112,640]{2,1,0:T(8,128)(2,1)S(1)}, u32[]{:S(2)}) copy-start(bf16[4,112,640]{2,1,0:T(8,128)(2,1)S(1)} %collective-permute-done.7.rest_1_) | copy-start | bytes 1720324
  62.2 19.4 %collective-permute-start.8 = (bf16[2,112,640]{2,1,0:T(8,128)(2,1)S(1)}, bf16[2,112,640]{2,1,0:T(8,128)(2,1)S(1)}, u32[]{:S(2)}, u32[]{:S(2)}) collective-permute-start(bf16[2,112,640]{2,1,0:T(8,128)(2,1)S(1)} %slice.42), channel_id=1, source_target_pairs={{0,2},{2,4},{4,6},{6,0},{1,3},{3,5},{5,7},{7,1},{8,10},{10,12},{12... | collective-permute-start | bytes 860168 | tf_op jit(solution)/shard_map/ppermute | solution.py:427
  63.0 0.6 copy-start.14
  73.6 17.8 %collective-permute-start.13 = (bf16[4,80,640]{2,1,0:T(8,128)(2,1)}, bf16[4,80,640]{2,1,0:T(8,128)(2,1)S(1)}, u32[]{:S(2)}, u32[]{:S(2)}) collective-permute-start(bf16[4,80,640]{2,1,0:T(8,128)(2,1)} %get-tuple-element.37), channel_id=1, source_target_pairs={{0,24},{8,0},{16,8},{24,16},{1,25},{9,1},{17,9},{25,17},{2,26},{10... | collective-permute-start | bytes 1228808 | tf_op jit(solution)/shard_map/ppermute | solution.py:427
  76.7 14.8 %collective-permute-start.12 = (bf16[4,80,640]{2,1,0:T(8,128)(2,1)}, bf16[4,80,640]{2,1,0:T(8,128)(2,1)S(1)}, u32[]{:S(2)}, u32[]{:S(2)}) collective-permute-start(bf16[4,80,640]{2,1,0:T(8,128)(2,1)} %get-tuple-element.36), channel_id=1, source_target_pairs={{0,16},{8,24},{16,0},{24,8},{1,17},{9,25},{17,1},{25,9},{2,18},{10... | collective-permute-start | bytes 1228808 | tf_op jit(solution)/shard_map/ppermute | solution.py:427
  77.4 17.7 %collective-permute-start.11 = (bf16[4,80,640]{2,1,0:T(8,128)(2,1)}, bf16[4,80,640]{2,1,0:T(8,128)(2,1)S(1)}, u32[]{:S(2)}, u32[]{:S(2)}) collective-permute-start(bf16[4,80,640]{2,1,0:T(8,128)(2,1)} %get-tuple-element.35), channel_id=1, source_target_pairs={{0,8},{8,16},{16,24},{24,0},{1,9},{9,17},{17,25},{25,1},{2,10},{10... | collective-permute-start | bytes 1228808 | tf_op jit(solution)/shard_map/ppermute | solution.py:427
  78.3 46.0 %copy-start.5 = (bf16[4,112,640]{2,1,0:T(8,128)(2,1)}, bf16[4,112,640]{2,1,0:T(8,128)(2,1)S(1)}, u32[]{:S(2)}) copy-start(bf16[4,112,640]{2,1,0:T(8,128)(2,1)S(1)} %collective-permute-done.9.rest_3_) | copy-start | bytes 1720324
  78.4 7.4 %collective-permute-start.10 = (bf16[2,112,640]{2,1,0:T(8,128)(2,1)S(1)}, bf16[2,112,640]{2,1,0:T(8,128)(2,1)S(1)}, u32[]{:S(2)}, u32[]{:S(2)}) collective-permute-start(bf16[2,112,640]{2,1,0:T(8,128)(2,1)S(1)} %slice.43), channel_id=1, source_target_pairs={{0,6},{2,0},{4,2},{6,4},{1,7},{3,1},{5,3},{7,5},{8,14},{10,8},{12,... | collective-permute-start | bytes 860168 | tf_op jit(solution)/shard_map/ppermute | solution.py:427
  85.8 38.5 %copy-start.6 = (bf16[4,112,640]{2,1,0:T(8,128)(2,1)}, bf16[4,112,640]{2,1,0:T(8,128)(2,1)S(1)}, u32[]{:S(2)}) copy-start(bf16[4,112,640]{2,1,0:T(8,128)(2,1)S(1)} %constant_dynamic-update-slice_fusion.rest_2_) | copy-start | bytes 1720324
  96.3 7.1 %collective-permute-start.16 = (bf16[80,640]{1,0:T(8,128)(2,1)S(1)}, bf16[80,640]{1,0:T(8,128)(2,1)S(1)}, u32[]{:S(2)}, u32[]{:S(2)}) collective-permute-start(bf16[80,640]{1,0:T(8,128)(2,1)S(1)} %get-tuple-element.43), channel_id=1, source_target_pairs={{0,6},{2,0},{4,2},{6,4},{1,7},{3,1},{5,3},{7,5},{8,14},{10,8},{12,... | collective-permute-start | bytes 307208 | tf_op jit(solution)/shard_map/ppermute | solution.py:427
  99.3 6.8 %collective-permute-start.15 = (bf16[80,640]{1,0:T(8,128)(2,1)S(1)}, bf16[80,640]{1,0:T(8,128)(2,1)S(1)}, u32[]{:S(2)}, u32[]{:S(2)}) collective-permute-start(bf16[80,640]{1,0:T(8,128)(2,1)S(1)} %get-tuple-element.44), channel_id=1, source_target_pairs={{0,4},{2,6},{4,0},{6,2},{1,5},{3,7},{5,1},{7,3},{8,12},{10,14},{12... | collective-permute-start | bytes 307208 | tf_op jit(solution)/shard_map/ppermute | solution.py:427
  99.4 7.4 %collective-permute-start.14 = (bf16[80,640]{1,0:T(8,128)(2,1)S(1)}, bf16[80,640]{1,0:T(8,128)(2,1)S(1)}, u32[]{:S(2)}, u32[]{:S(2)}) collective-permute-start(bf16[80,640]{1,0:T(8,128)(2,1)S(1)} %get-tuple-element.42), channel_id=1, source_target_pairs={{0,2},{2,4},{4,6},{6,0},{1,3},{3,5},{5,7},{7,1},{8,10},{10,12},{12... | collective-permute-start | bytes 307208 | tf_op jit(solution)/shard_map/ppermute | solution.py:427
  106.9 5.7 %collective-permute-start.20 = (bf16[80,640]{1,0:T(8,128)(2,1)S(1)}, bf16[80,640]{1,0:T(8,128)(2,1)S(1)}, u32[]{:S(2)}, u32[]{:S(2)}) collective-permute-start(bf16[80,640]{1,0:T(8,128)(2,1)S(1)} %fusion.2), channel_id=1, source_target_pairs={{0,6},{2,32},{4,66},{6,100},{32,102},{34,0},{36,34},{38,68},{64,70... | collective-permute-start | bytes 307208 | tf_op jit(solution)/shard_map/ppermute | solution.py:477
  107.9 8.6 %collective-permute-start.19 = (bf16[80,640]{1,0:T(8,128)(2,1)S(1)}, bf16[80,640]{1,0:T(8,128)(2,1)S(1)}, u32[]{:S(2)}, u32[]{:S(2)}) collective-permute-start(bf16[80,640]{1,0:T(8,128)(2,1)S(1)} %fusion.2), channel_id=1, source_target_pairs={{0,4},{2,38},{4,64},{6,98},{32,100},{34,6},{36,32},{38,66},{64,68}... | collective-permute-start | bytes 307208 | tf_op jit(solution)/shard_map/ppermute | solution.py:477
  111.2 9.2 %collective-permute-start.18 = (bf16[80,640]{1,0:T(8,128)(2,1)S(1)}, bf16[80,640]{1,0:T(8,128)(2,1)S(1)}, u32[]{:S(2)}, u32[]{:S(2)}) collective-permute-start(bf16[80,640]{1,0:T(8,128)(2,1)S(1)} %fusion.2), channel_id=1, source_target_pairs={{0,2},{2,36},{4,70},{6,96},{32,98},{34,4},{36,38},{38,64},{64,66},... | collective-permute-start | bytes 307208 | tf_op jit(solution)/shard_map/ppermute | solution.py:477
  111.6 8.8 %collective-permute-start.17 = (bf16[80,640]{1,0:T(8,128)(2,1)S(1)}, bf16[80,640]{1,0:T(8,128)(2,1)S(1)}, u32[]{:S(2)}, u32[]{:S(2)}) collective-permute-start(bf16[80,640]{1,0:T(8,128)(2,1)S(1)} %fusion.2), channel_id=1, source_target_pairs={{0,0},{2,34},{4,68},{6,102},{32,96},{34,2},{36,36},{38,70},{64,64}... | collective-permute-start | bytes 307208 | tf_op jit(solution)/shard_map/ppermute | solution.py:477
  112.3 12.0 %collective-permute-start.21 = (bf16[4,112,640]{2,1,0:T(8,128)(2,1)S(1)}, bf16[4,112,640]{2,1,0:T(8,128)(2,1)S(1)}, u32[]{:S(2)}, u32[]{:S(2)}) collective-permute-start(bf16[4,112,640]{2,1,0:T(8,128)(2,1)S(1)} %slice.32.rest_0_), channel_id=1, source_target_pairs={{0,1},{1,0},{2,3},{3,2},{4,5},{5,4},{6,7},{7,6},{8,9},{9,8},{10,11... | collective-permute-start | bytes 1720328 | tf_op jit(solution)/shard_map/ppermute | solution.py:486
  112.6 11.7 %collective-permute-start.22 = (bf16[4,112,640]{2,1,0:T(8,128)(2,1)S(1)}, bf16[4,112,640]{2,1,0:T(8,128)(2,1)}, u32[]{:S(2)}, u32[]{:S(2)}) collective-permute-start(bf16[4,112,640]{2,1,0:T(8,128)(2,1)S(1)} %collective-permute-done.7.rest_1_), channel_id=1, source_target_pairs={{0,1},{1,0},{2,3},{3,2},{4,5},{5,4},{6,7},{7,6},{8,9},{9,8},{10,11... | collective-permute-start | bytes 1720328 | tf_op jit(solution)/shard_map/ppermute | solution.py:486
  116.4 7.9 %collective-permute-start.24 = (bf16[4,112,640]{2,1,0:T(8,128)(2,1)S(1)}, bf16[4,112,640]{2,1,0:T(8,128)(2,1)}, u32[]{:S(2)}, u32[]{:S(2)}) collective-permute-start(bf16[4,112,640]{2,1,0:T(8,128)(2,1)S(1)} %collective-permute-done.9.rest_3_), channel_id=1, source_target_pairs={{0,1},{1,0},{2,3},{3,2},{4,5},{5,4},{6,7},{7,6},{8,9},{9,8},{10,11... | collective-permute-start | bytes 1720328 | tf_op jit(solution)/shard_map/ppermute | solution.py:486
  120.4 3.9 %collective-permute-start.23 = (bf16[4,112,640]{2,1,0:T(8,128)(2,1)S(1)}, bf16[4,112,640]{2,1,0:T(8,128)(2,1)}, u32[]{:S(2)}, u32[]{:S(2)}) collective-permute-start(bf16[4,112,640]{2,1,0:T(8,128)(2,1)S(1)} %constant_dynamic-update-slice_fusion.rest_2_), channel_id=1, source_target_pairs={{0,1},{1,0},{2,3},{3,2},{4,5},{5,4},{6,7},{7,6},{8,9},{9,8},{10,11... | collective-permute-start | bytes 1720328 | tf_op jit(solution)/shard_map/ppermute | solution.py:486
  120.5 36.1 %copy-start.3 = (bf16[4,80,640]{2,1,0:T(8,128)(2,1)}, bf16[4,80,640]{2,1,0:T(8,128)(2,1)S(1)}, u32[]{:S(2)}) copy-start(bf16[4,80,640]{2,1,0:T(8,128)(2,1)S(1)} %pad_maximum_fusion.1.mine) | copy-start | bytes 1228804
  120.5 40.3 %collective-permute-start.25 = (bf16[4,80,640]{2,1,0:T(8,128)(2,1)S(1)}, bf16[4,80,640]{2,1,0:T(8,128)(2,1)}, u32[]{:S(2)}, u32[]{:S(2)}) collective-permute-start(bf16[4,80,640]{2,1,0:T(8,128)(2,1)S(1)} %pad_maximum_fusion.1.mine), channel_id=1, source_target_pairs={{0,1},{1,0},{2,3},{3,2},{4,5},{5,4},{6,7},{7,6},{8,9},{9,8},{10,11... | collective-permute-start | bytes 1228808 | tf_op jit(solution)/shard_map/ppermute | solution.py:485
  124.3 0.8 copy-start.7
  157.3 8.0 %collective-permute-start.32 = (f32[1,16]{1,0:T(1,128)S(1)}, f32[1,16]{1,0:T(1,128)S(1)}, u32[]{:S(2)}, u32[]{:S(2)}) collective-permute-start(f32[1,16]{1,0:T(1,128)S(1)} %slice.39), channel_id=1, source_target_pairs={{0,96},{32,0},{64,32},{96,64},{1,97},{33,1},{65,33},{97,65},{2,98}... | collective-permute-start | bytes 200 | tf_op jit(solution)/shard_map/ppermute | solution.py:427
  160.0 6.7 %collective-permute-start.31 = (f32[1,16]{1,0:T(1,128)S(1)}, f32[1,16]{1,0:T(1,128)S(1)}, u32[]{:S(2)}, u32[]{:S(2)}) collective-permute-start(f32[1,16]{1,0:T(1,128)S(1)} %slice.39), channel_id=1, source_target_pairs={{0,64},{32,96},{64,0},{96,32},{1,65},{33,97},{65,1},{97,33},{2,66}... | collective-permute-start | bytes 200 | tf_op jit(solution)/shard_map/ppermute | solution.py:427
  160.0 6.7 %collective-permute-start.30 = (f32[1,16]{1,0:T(1,128)S(1)}, f32[1,16]{1,0:T(1,128)S(1)}, u32[]{:S(2)}, u32[]{:S(2)}) collective-permute-start(f32[1,16]{1,0:T(1,128)S(1)} %slice.39), channel_id=1, source_target_pairs={{0,32},{32,64},{64,96},{96,0},{1,33},{33,65},{65,97},{97,1},{2,34}... | collective-permute-start | bytes 200 | tf_op jit(solution)/shard_map/ppermute | solution.py:427
  164.6 8.2 %collective-permute-start.28 = (bf16[104,640]{1,0:T(8,128)(2,1)}, bf16[104,640]{1,0:T(8,128)(2,1)S(1)}, u32[]{:S(2)}, u32[]{:S(2)}) collective-permute-start(bf16[104,640]{1,0:T(8,128)(2,1)} %taylor.1), channel_id=1, source_target_pairs={{0,24},{8,0},{16,8},{24,16},{1,25},{9,1},{17,9},{25,17},{2,26},{10... | collective-permute-start | bytes 399368 | tf_op jit(solution)/shard_map/ppermute | solution.py:427
  164.7 9.5 %collective-permute-start.27 = (bf16[104,640]{1,0:T(8,128)(2,1)}, bf16[104,640]{1,0:T(8,128)(2,1)S(1)}, u32[]{:S(2)}, u32[]{:S(2)}) collective-permute-start(bf16[104,640]{1,0:T(8,128)(2,1)} %taylor.1), channel_id=1, source_target_pairs={{0,16},{8,24},{16,0},{24,8},{1,17},{9,25},{17,1},{25,9},{2,18},{10... | collective-permute-start | bytes 399368 | tf_op jit(solution)/shard_map/ppermute | solution.py:427
  165.3 9.2 %collective-permute-start.26 = (bf16[104,640]{1,0:T(8,128)(2,1)}, bf16[104,640]{1,0:T(8,128)(2,1)S(1)}, u32[]{:S(2)}, u32[]{:S(2)}) collective-permute-start(bf16[104,640]{1,0:T(8,128)(2,1)} %taylor.1), channel_id=1, source_target_pairs={{0,8},{8,16},{16,24},{24,0},{1,9},{9,17},{17,25},{25,1},{2,10},{10... | collective-permute-start | bytes 399368 | tf_op jit(solution)/shard_map/ppermute | solution.py:427
  167.3 1.1 collective-permute-start.33
  168.4 7.2 %collective-permute-start.36 = (f32[1,16]{1,0:T(1,128)S(1)}, f32[1,16]{1,0:T(1,128)S(1)}, u32[]{:S(2)}, u32[]{:S(2)}) collective-permute-start(f32[1,16]{1,0:T(1,128)S(1)} %add.134), channel_id=1, source_target_pairs={{0,6},{2,0},{4,2},{6,4},{1,7},{3,1},{5,3},{7,5},{8,14},{10,8},{12,... | collective-permute-start | bytes 200 | tf_op jit(solution)/shard_map/ppermute | solution.py:427
  169.8 5.8 %collective-permute-start.35 = (f32[1,16]{1,0:T(1,128)S(1)}, f32[1,16]{1,0:T(1,128)S(1)}, u32[]{:S(2)}, u32[]{:S(2)}) collective-permute-start(f32[1,16]{1,0:T(1,128)S(1)} %add.134), channel_id=1, source_target_pairs={{0,4},{2,6},{4,0},{6,2},{1,5},{3,7},{5,1},{7,3},{8,12},{10,14},{12... | collective-permute-start | bytes 200 | tf_op jit(solution)/shard_map/ppermute | solution.py:427
  172.8 4.8 %collective-permute-start.34 = (f32[1,16]{1,0:T(1,128)S(1)}, f32[1,16]{1,0:T(1,128)S(1)}, u32[]{:S(2)}, u32[]{:S(2)}) collective-permute-start(f32[1,16]{1,0:T(1,128)S(1)} %add.134), channel_id=1, source_target_pairs={{0,2},{2,4},{4,6},{6,0},{1,3},{3,5},{5,7},{7,1},{8,10},{10,12},{12... | collective-permute-start | bytes 200 | tf_op jit(solution)/shard_map/ppermute | solution.py:427
  175.5 11.5 %copy-start.2 = (bf16[4,104,640]{2,1,0:T(8,128)(2,1)}, bf16[4,104,640]{2,1,0:T(8,128)(2,1)S(1)}, u32[]{:S(2)}) copy-start(bf16[4,104,640]{2,1,0:T(8,128)(2,1)S(1)} %pad_maximum_fusion.mine) | copy-start | bytes 1597444
  175.5 11.5 %collective-permute-start.29 = (bf16[4,104,640]{2,1,0:T(8,128)(2,1)S(1)}, bf16[4,104,640]{2,1,0:T(8,128)(2,1)S(1)}, u32[]{:S(2)}, u32[]{:S(2)}) collective-permute-start(bf16[4,104,640]{2,1,0:T(8,128)(2,1)S(1)} %pad_maximum_fusion.mine), channel_id=1, source_target_pairs={{0,1},{1,0},{2,3},{3,2},{4,5},{5,4},{6,7},{7,6},{8,9},{9,8},{10,11... | collective-permute-start | bytes 1597448 | tf_op jit(solution)/shard_map/ppermute | solution.py:492
  177.6 5.4 %collective-permute-start.39 = (f32[1,16]{1,0:T(1,128)S(1)}, f32[1,16]{1,0:T(1,128)S(1)}, u32[]{:S(2)}, u32[]{:S(2)}) collective-permute-start(f32[1,16]{1,0:T(1,128)S(1)} %add_add_fusion.1), channel_id=1, source_target_pairs={{0,24},{8,0},{16,8},{24,16},{1,25},{9,1},{17,9},{25,17},{2,26},{10... | collective-permute-start | bytes 200 | tf_op jit(solution)/shard_map/ppermute | solution.py:427
  180.1 5.0 %collective-permute-start.38 = (f32[1,16]{1,0:T(1,128)S(1)}, f32[1,16]{1,0:T(1,128)S(1)}, u32[]{:S(2)}, u32[]{:S(2)}) collective-permute-start(f32[1,16]{1,0:T(1,128)S(1)} %add_add_fusion.1), channel_id=1, source_target_pairs={{0,16},{8,24},{16,0},{24,8},{1,17},{9,25},{17,1},{25,9},{2,18},{10... | collective-permute-start | bytes 200 | tf_op jit(solution)/shard_map/ppermute | solution.py:427
  181.7 4.8 %collective-permute-start.37 = (f32[1,16]{1,0:T(1,128)S(1)}, f32[1,16]{1,0:T(1,128)S(1)}, u32[]{:S(2)}, u32[]{:S(2)}) collective-permute-start(f32[1,16]{1,0:T(1,128)S(1)} %add_add_fusion.1), channel_id=1, source_target_pairs={{0,8},{8,16},{16,24},{24,0},{1,9},{9,17},{17,25},{25,1},{2,10},{10... | collective-permute-start | bytes 200 | tf_op jit(solution)/shard_map/ppermute | solution.py:427
  187.0 0.8 copy-start.8

commit v3 on v2

--- a/solution.py
+++ b/solution.py
@@ -34,7 +34,7 @@
     return [(q, (q + k) % n) for q in range(n)]
 
 
-def theta_kernel(n, quarter, place, wanted, trial, walkers, *rest):
+def theta_kernel(n, quarter, place, trial, walkers, *rest):
     own, (sent, c_ref, s_ref, y_ref, w_ref, h_ref, whole) = rest[:n], rest[n:]
     x_at, z_at, core = place[0], place[2], place[3]
     pair, rows = own[0].shape[:2]
@@ -100,10 +100,10 @@
     far = n_occ - count
     for j in range(n):
         sent[j, :quarter, :] = whole[pl.ds(pl.multiple_of(z_at * stride, stride), quarter), :]
-        sent[j, quarter:, :] = walkers[wanted[j], pl.ds(pl.multiple_of(core * far, far), count), :]
-
-
-def make_theta(place, wanted, trial, walkers, n, quarter, count):
+        sent[j, quarter:, :] = walkers[jnp.clip(place[4 + j] - 2 * pair * x_at, 0, 2 * pair - 1), pl.ds(pl.multiple_of(core * far, far), count), :]
+
+
+def make_theta(place, trial, walkers, n, quarter, count):
     _, n_occ, n_orb = walkers.shape
     pair = walkers.shape[0] // 2
     return pl.pallas_call(
@@ -112,7 +112,7 @@
         + [
             jax.ShapeDtypeStruct((n, quarter + count, n_orb), BF),
         ],
-        in_specs=[SMEM, SMEM, VMEM, VMEM],
+        in_specs=[SMEM, VMEM, VMEM],
         out_specs=[VMEM] * (n + 1),
         scratch_shapes=[pltpu.VMEM((pair, n_occ, n_occ), F32)] * 3
         + [
@@ -123,7 +123,7 @@
         compiler_params=params(),
         cost_estimate=taking(7.6),
         name="theta",
-    )(place, wanted, trial, walkers)
+    )(place, trial, walkers)
 
 
 def bias_kernel(n, place, mine, theirs, noise_mine, noise_theirs, *rest):
@@ -351,7 +351,7 @@
     )(place, before, *tables, halves)
 
 
-def taylor_kernel(n, place, chosen, walker, mine, theirs, out, v_ref):
+def taylor_kernel(n, place, walker, mine, theirs, out, v_ref):
     x_at, z_at, core = place[0], place[2], place[3]
     half = mine.shape[1]
     for k in range(n):
@@ -359,7 +359,7 @@
         v_ref[pl.ds(pl.multiple_of((2 * block + core) * half, half), half), :] = mine[k]
         v_ref[pl.ds(pl.multiple_of((2 * block + 1 - core) * half, half), half), :] = theirs[k]
 
-    term = walker[0, walker.shape[1] - out.shape[0] :, :]
+    term = walker[lax.div(place[4 + x_at], n), walker.shape[1] - out.shape[0] :, :]
     total = term.astype(F32)
     for k in range(1, TERMS + 1):
         term = (mm(term, v_ref[...], ((1,), (1,))) / k).astype(BF)
@@ -367,22 +367,18 @@
     out[...] = total.astype(BF)
 
 
-def make_taylor(place, chosen, walkers, mine, theirs, n, count):
-    _, rows, n_orb = walkers.shape
+def make_taylor(place, walkers, mine, theirs, n, count):
+    n_orb = walkers.shape[2]
     return pl.pallas_call(
         functools.partial(taylor_kernel, n),
         out_shape=jax.ShapeDtypeStruct((count, n_orb), BF),
-        grid_spec=pltpu.PrefetchScalarGridSpec(
-            num_scalar_prefetch=2,
-            grid=(1,),
-            in_specs=[pl.BlockSpec((1, rows, n_orb), lambda s, p, c: (c[0], 0, 0)), VMEM, VMEM],
-            out_specs=VMEM,
-            scratch_shapes=[pltpu.VMEM((n_orb, n_orb), BF)],
-        ),
+        in_specs=[SMEM] + [VMEM] * 3,
+        out_specs=VMEM,
+        scratch_shapes=[pltpu.VMEM((n_orb, n_orb), BF)],
         compiler_params=params(),
         cost_estimate=taking(0.01),
         name="taylor",
-    )(place, chosen, walkers, mine, theirs)
+    )(place, walkers, mine, theirs)
 
 
 def join_kernel(n, place, mine, theirs, out):
@@ -415,7 +411,6 @@
 def shards(walkers, trial, half_chol, chol_vectors, noise, copies):
     n = lax.axis_size("x")
     x, y, z, core = (lax.axis_index(a) for a in ("x", "y", "z", "core"))
-    place = jnp.stack([x, y, z, core]).astype(jnp.int32)
     w_grp, n_orb, n_occ = walkers.shape
     n_vec = half_chol.shape[0]
     slots = w_grp * n
@@ -426,16 +421,19 @@
     def along(v, axis, k):
         return lax.ppermute(v, axis, shift(n, k)) if k else v
 
+    numbers = jnp.arange(slots, dtype=jnp.int32)
+    ends = jnp.sum(jnp.where(numbers[None, :] <= numbers[:, None], copies[None, :], 0), axis=1)
     parent = jnp.sum(
-        (jnp.cumsum(copies)[None, :] <= jnp.arange(slots, dtype=jnp.int32)[:, None]).astype(jnp.int32),
+        (ends[None, :] <= numbers[:, None]).astype(jnp.int32),
         axis=1,
     )
 
     noise_theirs = other_core(noise)
     half_theirs = other_core(half_chol)
     quarter, count = 112, 104
-    wanted = jnp.clip(parent.reshape(n, w_grp)[:, y] - w_grp * x, 0, w_grp - 1)
-    *own, sent = make_theta(place, wanted, trial, walkers, n, quarter, count)
+    wanted = jnp.sum(jnp.where(jnp.arange(w_grp) == y, parent.reshape(n, w_grp), 0), axis=1)
+    place = jnp.concatenate([jnp.stack([x, y, z, core]), wanted]).astype(jnp.int32)
+    *own, sent = make_theta(place, trial, walkers, n, quarter, count)
     own = [own[0]] + [after(t, half_theirs, noise_theirs) for t in own[1:]]
     thetas = [along(own[k], "x", k) for k in range(n)]
     got = lax.all_to_all(after(sent, *thetas[1:]), "x", 0, 0, tiled=True)
@@ -448,12 +446,6 @@
     by_x = half_chol.reshape((n, n_vec // n) + half_chol.shape[1:])
     halves = lax.all_to_all(after(by_x, near), "x", 0, 0, tiled=True)
 
-    pieces = got[:, :quarter]
-    after_one, before_one = along(pieces, "z", 1), along(pieces, "z", 3)
-    opposite = jnp.concatenate(
-        [along(after_one[: n // 2], "z", 1), along(before_one[n // 2 :], "z", 3)], axis=0
-    )
-    tables = [pieces, after_one, opposite, before_one]
     order = jnp.array([[k, m] for k in range(n) for m in range(n)], jnp.int32)
     slot = w_grp * ((z + order[:, 1] - x) % n) + (y + order[:, 0]) % n
     pairs = jnp.array([w_grp * a + i for a in range(n) for i in range(w_grp // 2)], jnp.int32)
@@ -469,8 +461,13 @@
             total = total + p.astype(F32)
         return total.astype(BF)
 
-    moved = [along(partials[k], "y", k) for k in range(n)]
-    over_y = added([after(moved[0], *tables)] + moved[1:])
+    pieces = after(got[:, :quarter], partials[0])
+    after_one, before_one = along(pieces, "z", 1), along(pieces, "z", 3)
+    opposite = jnp.concatenate(
+        [along(after_one[: n // 2], "z", 1), along(before_one[n // 2 :], "z", 3)], axis=0
+    )
+    tables = [pieces, after_one, opposite, before_one]
+    over_y = added([along(partials[k], "y", k) for k in range(n)])
     piece = added([along(over_y[m], "z", m) for m in range(n)])
     plane = jnp.stack(
         [
@@ -486,16 +483,16 @@
     tables = tables + [other_core(t) for t in tables]
     running = make_cross(place, after(running, plane), tables, halves, n)
     plane = after(plane, running)
-    chosen = parent[x * w_grp + y].reshape(1) // w_grp
-    mine = make_taylor(place, chosen, got, plane, plane_theirs, n, count)
+    energy = running[:1]
+    over_x = [along(energy, "x", k) for k in range(n)]
+    mine = make_taylor(after(place, over_x[1]), got, plane, plane_theirs, n, count)
     spread = jnp.stack([along(mine, "y", k) for k in range(n)])
     new_walkers = join(place, spread, other_core(spread), n, n_occ)
 
-    energy = running[:1]
-    for axis in ("x", "z", "y"):
+    energy = sum(over_x)
+    energy = energy + other_core(energy)
+    for axis in ("z", "y"):
         energy = sum([along(energy, axis, k) for k in range(n)])
-        if axis == "x":
-            energy = energy + other_core(energy)
     n_all = n_vec * 2 * n * n
     energies = lax.dynamic_slice_in_dim(energy[0], w_grp * x, w_grp) / n_all
     return new_walkers.transpose(0, 2, 1), energies

time: 191 us -> 188 us (0.984)
  starting transfers between devices: 56.5 us -> 62.3 us
  waiting for transfers between devices: 44.5 us -> 41.3 us
  between operations: 3.59 us -> 0.97 us
    ppermute x25, starting transfers between devices: 40 us -> 46.2 us  [along(): return lax.ppermute(v, axis, shift(n, k)) if k else v]
    ppermute x4, waiting for transfers between devices: 7.76 us -> 3.36 us  [shards(): lax.ppermute(piece, ('x', 'z'), [(n * a + b, n * ((b - a) % n) + (b + k)...]
  transfers between devices with their start and end apart: 42 -> 42, of which waited for: 17 -> 18; matrix products, arithmetic and copies ran while one was open for 5% -> 4% of each run, Pallas kernels for 32% -> 32%
where the time goes in v3:
time: 188 us
  Pallas kernels  63.1 us (34%)
  starting transfers between devices  62.3 us (33%)
  waiting for transfers between devices  41.3 us (22%)
  blocking collectives  10.9 us (6%)
  other arithmetic  5.31 us (3%)
  local copies, waits for them, and re-layouts  3.7 us (2%)
    ppermute x25, starting transfers between devices, along(): return lax.ppermute(v, axis, shift(n, k)) if k else v  46.2 us
    ppermute x25, waiting for transfers between devices, along(): return lax.ppermute(v, axis, shift(n, k)) if k else v  34.9 us
    pallas_call x1, Pallas kernels, make_cross(): pl.pallas_call(functools.partial(cross_kernel, n, pair), out_shape=jax.Sh...  31.6 us
    psum x1, blocking collectives, shards(): near = lax.psum(share, 'x')  10.9 us
    pallas_call x1, Pallas kernels, make_potential(): pl.pallas_call(functools.partial(potential_kernel, n), out_shape=[jax.Sha...  10 us
    pallas_call x1, Pallas kernels, make_theta(): pl.pallas_call(functools.partial(theta_kernel, n, quarter), out_shape=[ja...  8.4 us
    pallas_call x1, Pallas kernels, make_bias(): pl.pallas_call(functools.partial(bias_kernel, n), out_shape=jax.ShapeDtyp...  7.49 us
    ppermute x4, starting transfers between devices, shards(): lax.ppermute(piece, ('x', 'z'), [(n * a + b, n * ((b - a) % n) + (b + k)...  5.19 us
  transfers between devices with their start and end apart: 42, of which 18 were waited for; matrix products, arithmetic and copies ran while one was open for 4% of the time, Pallas kernels for 32%

profile of v3, /device:TPU:0, one launch (start us, length us, event | category | flops | bytes accessed | tf_op | source)
XLA Modules:
  0.0 187.6 jit_solution(894492871781720401)
XLA Ops:
  0.7 0.5 collective-permute-start.1
  1.2 0.8 select_reduce_fusion
  2.3 0.6 concatenate.6.place
  3.0 8.4 %theta.1 = (bf16[2,160,200]{2,1,0:T(8,128)(2,1)}, bf16[2,160,200]{2,1,0:T(8,128)(2,1)}, bf16[2,160,200]{2,1,0:T(8,128)(2,1)}, bf16[2,160,200]{2,1,0:T(8,128)(2,1)}, bf16[4,216,640]{2,1,0:T(8,128)(2,1)}) custom-call(s32[8]{0:T(128)} %concatenate.6.place, bf16[200,640]{1,0:T(8,128)(2,1)} %bitcast.42, bf16[4,200,640]{2,1,0:T(8,128)(2,1)} %bitcast.41), custom_call_target="tpu_custom_call" | custom-call | flops 8739999744 | bytes 1 | tf_op jit(solution)/shard_map/theta/pallas_call | solution.py:109
  11.6 1.6 collective-permute-start.2
  13.1 2.7 %collective-permute-start.3 = (bf16[2,160,200]{2,1,0:T(8,128)(2,1)}, bf16[2,160,200]{2,1,0:T(8,128)(2,1)S(1)}, u32[]{:S(2)}, u32[]{:S(2)}) collective-permute-start(bf16[2,160,200]{2,1,0:T(8,128)(2,1)} %get-tuple-element.27), channel_id=1, source_target_pairs={{0,64},{32,96},{64,0},{96,32},{1,65},{33,97},{65,1},{97,33},{2,66}... | collective-permute-start | bytes 384008 | tf_op jit(solution)/shard_map/ppermute | solution.py:422
  15.9 1.4 collective-permute-start.4
  17.3 2.2 %collective-permute-done.2.rest_1_ = bf16[2,160,200]{2,1,0:T(8,128)(2,1)S(1)} collective-permute-done((bf16[2,160,200]{2,1,0:T(8,128)(2,1)}, bf16[2,160,200]{2,1,0:T(8,128)(2,1)S(1)}, u32[]{:S(2)}, u32[]{:S(2)}) %collective-permute-start.2) | collective-permute-done | bytes 128032 | tf_op jit(solution)/shard_map/ppermute | solution.py:422
  19.5 4.6 %collective-permute-done.3.rest_2_ = bf16[2,160,200]{2,1,0:T(8,128)(2,1)S(1)} collective-permute-done((bf16[2,160,200]{2,1,0:T(8,128)(2,1)}, bf16[2,160,200]{2,1,0:T(8,128)(2,1)S(1)}, u32[]{:S(2)}, u32[]{:S(2)}) %collective-permute-start.3) | collective-permute-done | bytes 128032 | tf_op jit(solution)/shard_map/ppermute | solution.py:422
  24.1 3.9 %all-to-all-start = ((bf16[4,216,640]{2,1,0:T(8,128)(2,1)}), bf16[4,216,640]{2,1,0:T(8,128)(2,1)S(1)}, u32[]{:S(2)}, u32[]{:S(2)}) async-start(bf16[4,216,640]{2,1,0:T(8,128)(2,1)} %get-tuple-element.38), calls=%async_computation | async-start | bytes 2211840 | tf_op jit(solution)/shard_map/all_to_all | solution.py:439
  28.0 7.5 %bias.1 = f32[8,112]{1,0:T(8,128)} custom-call(s32[8]{0:T(128)} %concatenate.6.place, bf16[56,160,200]{2,1,0:T(8,128)(2,1)} %mine.2, bf16[56,160,200]{2,1,0:T(8,128)(2,1)} %collective-permute-done.theirs, f32[4,56]{1,0:T(4,128)} %noise_mine.3, f32[4,56]{1,0:T(4,128)} %copy-done.13, bf16[2,160,200]{2,1,0:T(8,128)(2,1)} %get-tuple-element.23.rest_0_, ...), custom_call_target="tpu_custom_call" | custom-call | flops 11500000 | bytes 1 | tf_op jit(solution)/shard_map/bias/pallas_call | solution.py:193
  35.5 10.9 %psum.7.near = f32[8,112]{1,0:T(8,128)S(1)} all-reduce(f32[8,112]{1,0:T(8,128)} %bias.1), channel_id=1, replica_groups=mesh['x'=4,'y'=4,'z'=4,'core'=2] {'x'}, use_global_device_ids=true, to_apply=%region_3.4 | all-reduce | flops 896 | bytes 7168 | tf_op jit(solution)/shard_map/psum | solution.py:443
  46.5 5.0 %all-to-all-start.1 = ((bf16[4,14,160,200]{3,2,1,0:T(8,128)(2,1)}), bf16[4,14,160,200]{3,2,1,0:T(8,128)(2,1)}, u32[]{:S(2)}, u32[]{:S(2)}) async-start(bf16[4,14,160,200]{3,2,1,0:T(8,128)(2,1)} %bitcast.31), calls=%async_computation.1 | async-start | bytes 9175040 | tf_op jit(solution)/shard_map/all_to_all | solution.py:447
  51.6 0.7 gather_fusion
  52.4 0.7 compare_convert_fusion
  53.1 0.5 collective-permute-done.5.far
  53.6 0.6 copy-done.14
  54.1 10.0 %potential.1 = (bf16[4,80,640]{2,1,0:T(8,128)(2,1)}, bf16[4,80,640]{2,1,0:T(8,128)(2,1)}, bf16[4,80,640]{2,1,0:T(8,128)(2,1)}, bf16[4,80,640]{2,1,0:T(8,128)(2,1)}, f32[8,16]{1,0:T(8,128)}) custom-call(s32[8]{0:T(128)} %concatenate.6.place, f32[8,112]{1,0:T(8,128)} %copy-done.12, f32[8,112]{1,0:T(8,128)} %copy-done.14, f32[4,56]{1,0:T(4,128)} %noise_mine.3, ...), custom_call_target="tpu_custom_call" | custom-call | flops 11500000 | bytes 1 | tf_op jit(solution)/shard_map/potential/pallas_call | solution.py:261
  64.2 3.1 %collective-permute-start.9 = (bf16[4,80,640]{2,1,0:T(8,128)(2,1)}, bf16[4,80,640]{2,1,0:T(8,128)(2,1)S(1)}, u32[]{:S(2)}, u32[]{:S(2)}) collective-permute-start(bf16[4,80,640]{2,1,0:T(8,128)(2,1)} %get-tuple-element.35), channel_id=1, source_target_pairs={{0,24},{8,0},{16,8},{24,16},{1,25},{9,1},{17,9},{25,17},{2,26},{10... | collective-permute-start | bytes 1228808 | tf_op jit(solution)/shard_map/ppermute | solution.py:422
  67.2 0.6 collective-permute-start.8
  67.9 1.0 collective-permute-start.7
  68.9 2.0 %collective-permute-start.17 = (bf16[4,112,640]{2,1,0:T(8,128)(2,1)S(1)}, bf16[4,112,640]{2,1,0:T(8,128)(2,1)S(1)}, u32[]{:S(2)}, u32[]{:S(2)}) collective-permute-start(bf16[4,112,640]{2,1,0:T(8,128)(2,1)S(1)} %slice.36.rest_0_), channel_id=1, source_target_pairs={{0,2},{2,4},{4,6},{6,0},{1,3},{3,5},{5,7},{7,1},{8,10},{10,12},{12... | collective-permute-start | bytes 1720328 | tf_op jit(solution)/shard_map/ppermute | solution.py:422
  70.9 2.2 %collective-permute-start.19 = (bf16[4,112,640]{2,1,0:T(8,128)(2,1)S(1)}, bf16[4,112,640]{2,1,0:T(8,128)(2,1)S(1)}, u32[]{:S(2)}, u32[]{:S(2)}) collective-permute-start(bf16[4,112,640]{2,1,0:T(8,128)(2,1)S(1)} %slice.36.rest_0_), channel_id=1, source_target_pairs={{0,6},{2,0},{4,2},{6,4},{1,7},{3,1},{5,3},{7,5},{8,14},{10,8},{12,... | collective-permute-start | bytes 1720328 | tf_op jit(solution)/shard_map/ppermute | solution.py:422
  73.1 12.3 %collective-permute-done.9 = bf16[4,80,640]{2,1,0:T(8,128)(2,1)S(1)} collective-permute-done((bf16[4,80,640]{2,1,0:T(8,128)(2,1)}, bf16[4,80,640]{2,1,0:T(8,128)(2,1)S(1)}, u32[]{:S(2)}, u32[]{:S(2)}) %collective-permute-start.9) | collective-permute-done | bytes 409632 | tf_op jit(solution)/shard_map/ppermute | solution.py:422
  85.4 3.6 %collective-permute-done.7 = bf16[4,80,640]{2,1,0:T(8,128)(2,1)S(1)} collective-permute-done((bf16[4,80,640]{2,1,0:T(8,128)(2,1)}, bf16[4,80,640]{2,1,0:T(8,128)(2,1)S(1)}, u32[]{:S(2)}, u32[]{:S(2)}) %collective-permute-start.7) | collective-permute-done | bytes 409632 | tf_op jit(solution)/shard_map/ppermute | solution.py:422
  89.0 1.2 add_convert_fusion
  90.2 4.1 %collective-permute-start.12 = (bf16[80,640]{1,0:T(8,128)(2,1)S(1)}, bf16[80,640]{1,0:T(8,128)(2,1)S(1)}, u32[]{:S(2)}, u32[]{:S(2)}) collective-permute-start(bf16[80,640]{1,0:T(8,128)(2,1)S(1)} %get-tuple-element.45), channel_id=1, source_target_pairs={{0,6},{2,0},{4,2},{6,4},{1,7},{3,1},{5,3},{7,5},{8,14},{10,8},{12,... | collective-permute-start | bytes 307208 | tf_op jit(solution)/shard_map/ppermute | solution.py:422
  94.3 1.3 collective-permute-start.10
  95.6 2.3 %collective-permute-start.18 = (bf16[2,112,640]{2,1,0:T(8,128)(2,1)S(1)}, bf16[2,112,640]{2,1,0:T(8,128)(2,1)S(1)}, u32[]{:S(2)}, u32[]{:S(2)}) collective-permute-start(bf16[2,112,640]{2,1,0:T(8,128)(2,1)S(1)} %slice.46), channel_id=1, source_target_pairs={{0,2},{2,4},{4,6},{6,0},{1,3},{3,5},{5,7},{7,1},{8,10},{10,12},{12... | collective-permute-start | bytes 860168 | tf_op jit(solution)/shard_map/ppermute | solution.py:422
  98.0 1.0 collective-permute-done.12
  99.0 3.7 %collective-permute-start.20 = (bf16[2,112,640]{2,1,0:T(8,128)(2,1)S(1)}, bf16[2,112,640]{2,1,0:T(8,128)(2,1)S(1)}, u32[]{:S(2)}, u32[]{:S(2)}) collective-permute-start(bf16[2,112,640]{2,1,0:T(8,128)(2,1)S(1)} %slice.47), channel_id=1, source_target_pairs={{0,6},{2,0},{4,2},{6,4},{1,7},{3,1},{5,3},{7,5},{8,14},{10,8},{12,... | collective-permute-start | bytes 860168 | tf_op jit(solution)/shard_map/ppermute | solution.py:422
  102.8 1.7 collective-permute-start.16
  104.5 2.9 %collective-permute-start.15 = (bf16[80,640]{1,0:T(8,128)(2,1)S(1)}, bf16[80,640]{1,0:T(8,128)(2,1)S(1)}, u32[]{:S(2)}, u32[]{:S(2)}) collective-permute-start(bf16[80,640]{1,0:T(8,128)(2,1)S(1)} %fusion.2), channel_id=1, source_target_pairs={{0,4},{2,38},{4,64},{6,98},{32,100},{34,6},{36,32},{38,66},{64,68}... | collective-permute-start | bytes 307208 | tf_op jit(solution)/shard_map/ppermute | solution.py:474
  107.4 1.2 collective-permute-done.18
  108.5 3.4 %collective-permute-done.20 = bf16[2,112,640]{2,1,0:T(8,128)(2,1)S(1)} collective-permute-done((bf16[2,112,640]{2,1,0:T(8,128)(2,1)S(1)}, bf16[2,112,640]{2,1,0:T(8,128)(2,1)S(1)}, u32[]{:S(2)}, u32[]{:S(2)}) %collective-permute-start.20) | collective-permute-done | bytes 286752 | tf_op jit(solution)/shard_map/ppermute | solution.py:422
  111.9 0.7 collective-permute-start.13
  112.7 0.3 collective-permute-done.16
  113.1 0.5 collective-permute-start.24
  113.5 3.0 %collective-permute-done.14 = bf16[80,640]{1,0:T(8,128)(2,1)S(1)} collective-permute-done((bf16[80,640]{1,0:T(8,128)(2,1)S(1)}, bf16[80,640]{1,0:T(8,128)(2,1)S(1)}, u32[]{:S(2)}, u32[]{:S(2)}) %collective-permute-start.14) | collective-permute-done | bytes 102432 | tf_op jit(solution)/shard_map/ppermute | solution.py:474
  116.6 0.6 collective-permute-start.26
  117.2 1.4 collective-permute-done.23.rest_6_
  118.6 31.6 %cross.1 = f32[8,16]{1,0:T(8,128)} custom-call(s32[8]{0:T(128)} %concatenate.6.place, f32[8,16]{1,0:T(8,128)} %get-tuple-element.36.before, bf16[4,112,640]{2,1,0:T(8,128)(2,1)} %copy-done.1, bf16[4,112,640]{2,1,0:T(8,128)(2,1)} %copy-done.4, bf16[4,112,640]{2,1,0:T(8,128)(2,1)} %copy-done.6, bf16[4,112,640]{2,1,0:T(8,128)(2,1)} %copy-done.5, ...), custom_call_target="tpu_custom_call" | custom-call | flops 575000000 | bytes 1 | tf_op jit(solution)/shard_map/cross/pallas_call | solution.py:334
  150.2 0.7 slice.39
  150.9 5.1 %collective-permute-start.25 = (f32[1,16]{1,0:T(1,128)S(1)}, f32[1,16]{1,0:T(1,128)S(1)}, u32[]{:S(2)}, u32[]{:S(2)}) collective-permute-start(f32[1,16]{1,0:T(1,128)S(1)} %slice.39), channel_id=1, source_target_pairs={{0,32},{32,64},{64,96},{96,0},{1,33},{33,65},{65,97},{97,1},{2,34}... | collective-permute-start | bytes 200 | tf_op jit(solution)/shard_map/ppermute | solution.py:422
  156.0 1.4 collective-permute-start.32
  157.5 1.5 collective-permute-start.31
  159.0 3.3 %taylor.1 = bf16[104,640]{1,0:T(8,128)(2,1)} custom-call(s32[8]{0:T(128)} %concatenate.6.place, bf16[4,216,640]{2,1,0:T(8,128)(2,1)} %copy-done, bf16[4,80,640]{2,1,0:T(8,128)(2,1)} %copy-done.3, bf16[4,80,640]{2,1,0:T(8,128)(2,1)} %collective-permute-done.26.theirs), custom_call_target="tpu_custom_call" | custom-call | flops 11500000 | bytes 1 | tf_op jit(solution)/shard_map/taylor/pallas_call | solution.py:372
  162.3 0.6 collective-permute-start.28
  163.0 1.4 collective-permute-start.27
  164.4 0.7 add_add_fusion.2
  165.1 1.1 collective-permute-done.33
  166.2 3.7 %collective-permute-start.36 = (f32[1,16]{1,0:T(1,128)S(1)}, f32[1,16]{1,0:T(1,128)S(1)}, u32[]{:S(2)}, u32[]{:S(2)}) collective-permute-start(f32[1,16]{1,0:T(1,128)S(1)} %add.121), channel_id=1, source_target_pairs={{0,6},{2,0},{4,2},{6,4},{1,7},{3,1},{5,3},{7,5},{8,14},{10,8},{12,... | collective-permute-start | bytes 200 | tf_op jit(solution)/shard_map/ppermute | solution.py:422
  169.9 0.9 collective-permute-start.34
  170.8 1.4 collective-permute-done.27
  172.2 1.0 pad_maximum_fusion.mine
  173.3 1.7 collective-permute-done.35
  175.0 2.7 %collective-permute-start.39 = (f32[1,16]{1,0:T(1,128)S(1)}, f32[1,16]{1,0:T(1,128)S(1)}, u32[]{:S(2)}, u32[]{:S(2)}) collective-permute-start(f32[1,16]{1,0:T(1,128)S(1)} %add_add_fusion.1), channel_id=1, source_target_pairs={{0,24},{8,0},{16,8},{24,16},{1,25},{9,1},{17,9},{25,17},{2,26},{10... | collective-permute-start | bytes 200 | tf_op jit(solution)/shard_map/ppermute | solution.py:422
  177.7 1.5 collective-permute-start.38
  179.2 1.3 collective-permute-start.37
  180.6 2.2 %collective-permute-done.38 = f32[1,16]{1,0:T(1,128)S(1)} collective-permute-done((f32[1,16]{1,0:T(1,128)S(1)}, f32[1,16]{1,0:T(1,128)S(1)}, u32[]{:S(2)}, u32[]{:S(2)}) %collective-permute-start.38) | collective-permute-done | bytes 96 | tf_op jit(solution)/shard_map/ppermute | solution.py:422
  182.7 1.3 collective-permute-done.37
  184.0 0.6 multiply_bitcast_fusion
  184.6 0.8 copy-done.8
  185.4 2.3 %join.1 = bf16[4,200,640]{2,1,0:T(8,128)(2,1)} custom-call(s32[8]{0:T(128)} %concatenate.6.place, bf16[4,104,640]{2,1,0:T(8,128)(2,1)} %copy-done.2, bf16[4,104,640]{2,1,0:T(8,128)(2,1)} %copy-done.8), custom_call_target="tpu_custom_call" | custom-call | flops 11500000 | bytes 1 | tf_op jit(solution)/shard_map/join/pallas_call | solution.py:396
  (90 shorter events, 1.5 us)
Async XLA Ops:
  0.6 10.7 %collective-permute-start = (bf16[56,160,200]{2,1,0:T(8,128)(2,1)}, bf16[56,160,200]{2,1,0:T(8,128)(2,1)}, u32[]{:S(2)}, u32[]{:S(2)}) collective-permute-start(bf16[56,160,200]{2,1,0:T(8,128)(2,1)} %mine.2), channel_id=1, source_target_pairs={{0,1},{1,0},{2,3},{3,2},{4,5},{5,4},{6,7},{7,6},{8,9},{9,8},{10,11... | collective-permute-start | bytes 10752008 | tf_op jit(solution)/shard_map/ppermute | solution.py:432
  0.7 10.6 %collective-permute-start.1 = (f32[4,56]{1,0:T(4,128)}, f32[4,56]{1,0:T(4,128)S(1)}, u32[]{:S(2)}, u32[]{:S(2)}) collective-permute-start(f32[4,56]{1,0:T(4,128)} %noise_mine.3), channel_id=1, source_target_pairs={{0,1},{1,0},{2,3},{3,2},{4,5},{5,4},{6,7},{7,6},{8,9},{9,8},{10,11... | collective-permute-start | bytes 2696 | tf_op jit(solution)/shard_map/ppermute | solution.py:431
  11.4 16.7 %copy-start.13 = (f32[4,56]{1,0:T(4,128)}, f32[4,56]{1,0:T(4,128)S(1)}, u32[]{:S(2)}) copy-start(f32[4,56]{1,0:T(4,128)S(1)} %collective-permute-done.1.noise_theirs) | copy-start | bytes 2692
  11.4 42.2 %collective-permute-start.6 = (bf16[56,160,640]{2,1,0:T(8,128)(2,1)}, bf16[56,160,640]{2,1,0:T(8,128)(2,1)}, u32[]{:S(2)}, u32[]{:S(2)}) collective-permute-start(bf16[56,160,640]{2,1,0:T(8,128)(2,1)} %mine.3), channel_id=1, source_target_pairs={{0,1},{1,0},{2,3},{3,2},{4,5},{5,4},{6,7},{7,6},{8,9},{9,8},{10,11... | collective-permute-start | bytes 34406408 | tf_op jit(solution)/shard_map/ppermute | solution.py:440
  11.6 8.0 %collective-permute-start.2 = (bf16[2,160,200]{2,1,0:T(8,128)(2,1)}, bf16[2,160,200]{2,1,0:T(8,128)(2,1)S(1)}, u32[]{:S(2)}, u32[]{:S(2)}) collective-permute-start(bf16[2,160,200]{2,1,0:T(8,128)(2,1)} %get-tuple-element.25), channel_id=1, source_target_pairs={{0,32},{32,64},{64,96},{96,0},{1,33},{33,65},{65,97},{97,1},{2,34}... | collective-permute-start | bytes 384008 | tf_op jit(solution)/shard_map/ppermute | solution.py:422
  13.1 11.0 %collective-permute-start.3 = (bf16[2,160,200]{2,1,0:T(8,128)(2,1)}, bf16[2,160,200]{2,1,0:T(8,128)(2,1)S(1)}, u32[]{:S(2)}, u32[]{:S(2)}) collective-permute-start(bf16[2,160,200]{2,1,0:T(8,128)(2,1)} %get-tuple-element.27), channel_id=1, source_target_pairs={{0,64},{32,96},{64,0},{96,32},{1,65},{33,97},{65,1},{97,33},{2,66}... | collective-permute-start | bytes 384008 | tf_op jit(solution)/shard_map/ppermute | solution.py:422
  15.9 8.2 %collective-permute-start.4 = (bf16[2,160,200]{2,1,0:T(8,128)(2,1)}, bf16[2,160,200]{2,1,0:T(8,128)(2,1)S(1)}, u32[]{:S(2)}, u32[]{:S(2)}) collective-permute-start(bf16[2,160,200]{2,1,0:T(8,128)(2,1)} %get-tuple-element.29), channel_id=1, source_target_pairs={{0,96},{32,0},{64,32},{96,64},{1,97},{33,1},{65,33},{97,65},{2,98}... | collective-permute-start | bytes 384008 | tf_op jit(solution)/shard_map/ppermute | solution.py:422
  19.5 8.5 %copy-start.9 = (bf16[2,160,200]{2,1,0:T(8,128)(2,1)}, bf16[2,160,200]{2,1,0:T(8,128)(2,1)S(1)}, u32[]{:S(2)}) copy-start(bf16[2,160,200]{2,1,0:T(8,128)(2,1)S(1)} %collective-permute-done.2.rest_1_) | copy-start | bytes 384004
  24.1 3.9 %copy-start.10 = (bf16[2,160,200]{2,1,0:T(8,128)(2,1)}, bf16[2,160,200]{2,1,0:T(8,128)(2,1)S(1)}, u32[]{:S(2)}) copy-start(bf16[2,160,200]{2,1,0:T(8,128)(2,1)S(1)} %collective-permute-done.3.rest_2_) | copy-start | bytes 384004
  24.1 3.9 %copy-start.11 = (bf16[2,160,200]{2,1,0:T(8,128)(2,1)}, bf16[2,160,200]{2,1,0:T(8,128)(2,1)S(1)}, u32[]{:S(2)}) copy-start(bf16[2,160,200]{2,1,0:T(8,128)(2,1)S(1)} %collective-permute-done.4.rest_3_) | copy-start | bytes 384004
  24.1 22.4 %all-to-all-start = ((bf16[4,216,640]{2,1,0:T(8,128)(2,1)}), bf16[4,216,640]{2,1,0:T(8,128)(2,1)S(1)}, u32[]{:S(2)}, u32[]{:S(2)}) async-start(bf16[4,216,640]{2,1,0:T(8,128)(2,1)} %get-tuple-element.38), calls=%async_computation | async-start | bytes 2211840 | tf_op jit(solution)/shard_map/all_to_all | solution.py:439
  46.5 5.8 %copy-start.12 = (f32[8,112]{1,0:T(8,128)}, f32[8,112]{1,0:T(8,128)S(1)}, u32[]{:S(2)}) copy-start(f32[8,112]{1,0:T(8,128)S(1)} %psum.7.near) | copy-start | bytes 10756
  46.5 5.1 %copy-start.16 = (s32[16,1]{0,1:T(1,128)S(1)}, s32[16,1]{0,1:T(1,128)}, u32[]{:S(2)}) copy-start(s32[16,1]{0,1:T(1,128)} %constant.59) | copy-start | bytes 196
  46.5 5.1 %copy-start.17 = (s32[16,1]{0,1:T(1,128)S(1)}, s32[16,1]{0,1:T(1,128)}, u32[]{:S(2)}) copy-start(s32[16,1]{0,1:T(1,128)} %constant.58) | copy-start | bytes 196
  46.5 5.8 %copy-start.15 = (s32[8]{0:T(128)S(1)}, s32[8]{0:T(128)}, u32[]{:S(2)}) copy-start(s32[8]{0:T(128)} %constant.54.clone) | copy-start | bytes 100
  46.5 22.3 %copy-start = (bf16[4,216,640]{2,1,0:T(8,128)(2,1)}, bf16[4,216,640]{2,1,0:T(8,128)(2,1)S(1)}, u32[]{:S(2)}) copy-start(bf16[4,216,640]{2,1,0:T(8,128)(2,1)S(1)} %all-to-all-done.walker) | copy-start | bytes 3317764
  46.5 70.6 %all-to-all-start.1 = ((bf16[4,14,160,200]{3,2,1,0:T(8,128)(2,1)}), bf16[4,14,160,200]{3,2,1,0:T(8,128)(2,1)}, u32[]{:S(2)}, u32[]{:S(2)}) async-start(bf16[4,14,160,200]{3,2,1,0:T(8,128)(2,1)} %bitcast.31), calls=%async_computation.1 | async-start | bytes 9175040 | tf_op jit(solution)/shard_map/all_to_all | solution.py:447
  52.3 1.2 collective-permute-start.5
  53.5 0.6 copy-start.14
  64.2 21.2 %collective-permute-start.9 = (bf16[4,80,640]{2,1,0:T(8,128)(2,1)}, bf16[4,80,640]{2,1,0:T(8,128)(2,1)S(1)}, u32[]{:S(2)}, u32[]{:S(2)}) collective-permute-start(bf16[4,80,640]{2,1,0:T(8,128)(2,1)} %get-tuple-element.35), channel_id=1, source_target_pairs={{0,24},{8,0},{16,8},{24,16},{1,25},{9,1},{17,9},{25,17},{2,26},{10... | collective-permute-start | bytes 1228808 | tf_op jit(solution)/shard_map/ppermute | solution.py:422
  67.2 18.2 %collective-permute-start.8 = (bf16[4,80,640]{2,1,0:T(8,128)(2,1)}, bf16[4,80,640]{2,1,0:T(8,128)(2,1)S(1)}, u32[]{:S(2)}, u32[]{:S(2)}) collective-permute-start(bf16[4,80,640]{2,1,0:T(8,128)(2,1)} %get-tuple-element.34), channel_id=1, source_target_pairs={{0,16},{8,24},{16,0},{24,8},{1,17},{9,25},{17,1},{25,9},{2,18},{10... | collective-permute-start | bytes 1228808 | tf_op jit(solution)/shard_map/ppermute | solution.py:422
  67.9 21.1 %collective-permute-start.7 = (bf16[4,80,640]{2,1,0:T(8,128)(2,1)}, bf16[4,80,640]{2,1,0:T(8,128)(2,1)S(1)}, u32[]{:S(2)}, u32[]{:S(2)}) collective-permute-start(bf16[4,80,640]{2,1,0:T(8,128)(2,1)} %get-tuple-element.33), channel_id=1, source_target_pairs={{0,8},{8,16},{16,24},{24,0},{1,9},{9,17},{17,25},{25,1},{2,10},{10... | collective-permute-start | bytes 1228808 | tf_op jit(solution)/shard_map/ppermute | solution.py:422
  68.9 49.7 %copy-start.1 = (bf16[4,112,640]{2,1,0:T(8,128)(2,1)}, bf16[4,112,640]{2,1,0:T(8,128)(2,1)S(1)}, u32[]{:S(2)}) copy-start(bf16[4,112,640]{2,1,0:T(8,128)(2,1)S(1)} %slice.36.rest_0_) | copy-start | bytes 1720324
  68.9 26.7 %collective-permute-start.17 = (bf16[4,112,640]{2,1,0:T(8,128)(2,1)S(1)}, bf16[4,112,640]{2,1,0:T(8,128)(2,1)S(1)}, u32[]{:S(2)}, u32[]{:S(2)}) collective-permute-start(bf16[4,112,640]{2,1,0:T(8,128)(2,1)S(1)} %slice.36.rest_0_), channel_id=1, source_target_pairs={{0,2},{2,4},{4,6},{6,0},{1,3},{3,5},{5,7},{7,1},{8,10},{10,12},{12... | collective-permute-start | bytes 1720328 | tf_op jit(solution)/shard_map/ppermute | solution.py:422
  70.9 27.0 %collective-permute-start.19 = (bf16[4,112,640]{2,1,0:T(8,128)(2,1)S(1)}, bf16[4,112,640]{2,1,0:T(8,128)(2,1)S(1)}, u32[]{:S(2)}, u32[]{:S(2)}) collective-permute-start(bf16[4,112,640]{2,1,0:T(8,128)(2,1)S(1)} %slice.36.rest_0_), channel_id=1, source_target_pairs={{0,6},{2,0},{4,2},{6,4},{1,7},{3,1},{5,3},{7,5},{8,14},{10,8},{12,... | collective-permute-start | bytes 1720328 | tf_op jit(solution)/shard_map/ppermute | solution.py:422
  90.2 8.7 %collective-permute-start.12 = (bf16[80,640]{1,0:T(8,128)(2,1)S(1)}, bf16[80,640]{1,0:T(8,128)(2,1)S(1)}, u32[]{:S(2)}, u32[]{:S(2)}) collective-permute-start(bf16[80,640]{1,0:T(8,128)(2,1)S(1)} %get-tuple-element.45), channel_id=1, source_target_pairs={{0,6},{2,0},{4,2},{6,4},{1,7},{3,1},{5,3},{7,5},{8,14},{10,8},{12,... | collective-permute-start | bytes 307208 | tf_op jit(solution)/shard_map/ppermute | solution.py:422
  94.3 8.3 %collective-permute-start.11 = (bf16[80,640]{1,0:T(8,128)(2,1)S(1)}, bf16[80,640]{1,0:T(8,128)(2,1)S(1)}, u32[]{:S(2)}, u32[]{:S(2)}) collective-permute-start(bf16[80,640]{1,0:T(8,128)(2,1)S(1)} %get-tuple-element.46), channel_id=1, source_target_pairs={{0,4},{2,6},{4,0},{6,2},{1,5},{3,7},{5,1},{7,3},{8,12},{10,14},{12... | collective-permute-start | bytes 307208 | tf_op jit(solution)/shard_map/ppermute | solution.py:422
  94.3 8.4 %collective-permute-start.10 = (bf16[80,640]{1,0:T(8,128)(2,1)S(1)}, bf16[80,640]{1,0:T(8,128)(2,1)S(1)}, u32[]{:S(2)}, u32[]{:S(2)}) collective-permute-start(bf16[80,640]{1,0:T(8,128)(2,1)S(1)} %get-tuple-element.44), channel_id=1, source_target_pairs={{0,2},{2,4},{4,6},{6,0},{1,3},{3,5},{5,7},{7,1},{8,10},{10,12},{12... | collective-permute-start | bytes 307208 | tf_op jit(solution)/shard_map/ppermute | solution.py:422
  95.6 23.0 %copy-start.4 = (bf16[4,112,640]{2,1,0:T(8,128)(2,1)}, bf16[4,112,640]{2,1,0:T(8,128)(2,1)S(1)}, u32[]{:S(2)}) copy-start(bf16[4,112,640]{2,1,0:T(8,128)(2,1)S(1)} %collective-permute-done.17.rest_1_) | copy-start | bytes 1720324
  95.6 12.9 %collective-permute-start.18 = (bf16[2,112,640]{2,1,0:T(8,128)(2,1)S(1)}, bf16[2,112,640]{2,1,0:T(8,128)(2,1)S(1)}, u32[]{:S(2)}, u32[]{:S(2)}) collective-permute-start(bf16[2,112,640]{2,1,0:T(8,128)(2,1)S(1)} %slice.46), channel_id=1, source_target_pairs={{0,2},{2,4},{4,6},{6,0},{1,3},{3,5},{5,7},{7,1},{8,10},{10,12},{12... | collective-permute-start | bytes 860168 | tf_op jit(solution)/shard_map/ppermute | solution.py:422
  97.9 20.7 %copy-start.5 = (bf16[4,112,640]{2,1,0:T(8,128)(2,1)}, bf16[4,112,640]{2,1,0:T(8,128)(2,1)S(1)}, u32[]{:S(2)}) copy-start(bf16[4,112,640]{2,1,0:T(8,128)(2,1)S(1)} %collective-permute-done.19.rest_3_) | copy-start | bytes 1720324
  97.9 19.2 %collective-permute-start.21 = (bf16[4,112,640]{2,1,0:T(8,128)(2,1)S(1)}, bf16[4,112,640]{2,1,0:T(8,128)(2,1)S(1)}, u32[]{:S(2)}, u32[]{:S(2)}) collective-permute-start(bf16[4,112,640]{2,1,0:T(8,128)(2,1)S(1)} %slice.36.rest_0_), channel_id=1, source_target_pairs={{0,1},{1,0},{2,3},{3,2},{4,5},{5,4},{6,7},{7,6},{8,9},{9,8},{10,11... | collective-permute-start | bytes 1720328 | tf_op jit(solution)/shard_map/ppermute | solution.py:483
  99.0 13.0 %collective-permute-start.20 = (bf16[2,112,640]{2,1,0:T(8,128)(2,1)S(1)}, bf16[2,112,640]{2,1,0:T(8,128)(2,1)S(1)}, u32[]{:S(2)}, u32[]{:S(2)}) collective-permute-start(bf16[2,112,640]{2,1,0:T(8,128)(2,1)S(1)} %slice.47), channel_id=1, source_target_pairs={{0,6},{2,0},{4,2},{6,4},{1,7},{3,1},{5,3},{7,5},{8,14},{10,8},{12,... | collective-permute-start | bytes 860168 | tf_op jit(solution)/shard_map/ppermute | solution.py:422
  102.8 10.2 %collective-permute-start.16 = (bf16[80,640]{1,0:T(8,128)(2,1)S(1)}, bf16[80,640]{1,0:T(8,128)(2,1)S(1)}, u32[]{:S(2)}, u32[]{:S(2)}) collective-permute-start(bf16[80,640]{1,0:T(8,128)(2,1)S(1)} %fusion.2), channel_id=1, source_target_pairs={{0,6},{2,32},{4,66},{6,100},{32,102},{34,0},{36,34},{38,68},{64,70... | collective-permute-start | bytes 307208 | tf_op jit(solution)/shard_map/ppermute | solution.py:474
  104.5 8.6 %collective-permute-start.15 = (bf16[80,640]{1,0:T(8,128)(2,1)S(1)}, bf16[80,640]{1,0:T(8,128)(2,1)S(1)}, u32[]{:S(2)}, u32[]{:S(2)}) collective-permute-start(bf16[80,640]{1,0:T(8,128)(2,1)S(1)} %fusion.2), channel_id=1, source_target_pairs={{0,4},{2,38},{4,64},{6,98},{32,100},{34,6},{36,32},{38,66},{64,68}... | collective-permute-start | bytes 307208 | tf_op jit(solution)/shard_map/ppermute | solution.py:474
  108.5 8.0 %collective-permute-start.14 = (bf16[80,640]{1,0:T(8,128)(2,1)S(1)}, bf16[80,640]{1,0:T(8,128)(2,1)S(1)}, u32[]{:S(2)}, u32[]{:S(2)}) collective-permute-start(bf16[80,640]{1,0:T(8,128)(2,1)S(1)} %fusion.2), channel_id=1, source_target_pairs={{0,2},{2,36},{4,70},{6,96},{32,98},{34,4},{36,38},{38,64},{64,66},... | collective-permute-start | bytes 307208 | tf_op jit(solution)/shard_map/ppermute | solution.py:474
  111.9 4.6 %collective-permute-start.13 = (bf16[80,640]{1,0:T(8,128)(2,1)S(1)}, bf16[80,640]{1,0:T(8,128)(2,1)S(1)}, u32[]{:S(2)}, u32[]{:S(2)}) collective-permute-start(bf16[80,640]{1,0:T(8,128)(2,1)S(1)} %fusion.2), channel_id=1, source_target_pairs={{0,0},{2,34},{4,68},{6,102},{32,96},{34,2},{36,36},{38,70},{64,64}... | collective-permute-start | bytes 307208 | tf_op jit(solution)/shard_map/ppermute | solution.py:474
  112.7 6.0 %copy-start.6 = (bf16[4,112,640]{2,1,0:T(8,128)(2,1)}, bf16[4,112,640]{2,1,0:T(8,128)(2,1)S(1)}, u32[]{:S(2)}) copy-start(bf16[4,112,640]{2,1,0:T(8,128)(2,1)S(1)} %constant_dynamic-update-slice_fusion.rest_2_) | copy-start | bytes 1720324
  113.0 4.2 %collective-permute-start.22 = (bf16[4,112,640]{2,1,0:T(8,128)(2,1)S(1)}, bf16[4,112,640]{2,1,0:T(8,128)(2,1)}, u32[]{:S(2)}, u32[]{:S(2)}) collective-permute-start(bf16[4,112,640]{2,1,0:T(8,128)(2,1)S(1)} %collective-permute-done.17.rest_1_), channel_id=1, source_target_pairs={{0,1},{1,0},{2,3},{3,2},{4,5},{5,4},{6,7},{7,6},{8,9},{9,8},{10,11... | collective-permute-start | bytes 1720328 | tf_op jit(solution)/shard_map/ppermute | solution.py:483
  113.1 4.1 %collective-permute-start.24 = (bf16[4,112,640]{2,1,0:T(8,128)(2,1)S(1)}, bf16[4,112,640]{2,1,0:T(8,128)(2,1)}, u32[]{:S(2)}, u32[]{:S(2)}) collective-permute-start(bf16[4,112,640]{2,1,0:T(8,128)(2,1)S(1)} %collective-permute-done.19.rest_3_), channel_id=1, source_target_pairs={{0,1},{1,0},{2,3},{3,2},{4,5},{5,4},{6,7},{7,6},{8,9},{9,8},{10,11... | collective-permute-start | bytes 1720328 | tf_op jit(solution)/shard_map/ppermute | solution.py:483
  116.5 2.1 %collective-permute-start.23 = (bf16[4,112,640]{2,1,0:T(8,128)(2,1)S(1)}, bf16[4,112,640]{2,1,0:T(8,128)(2,1)}, u32[]{:S(2)}, u32[]{:S(2)}) collective-permute-start(bf16[4,112,640]{2,1,0:T(8,128)(2,1)S(1)} %constant_dynamic-update-slice_fusion.rest_2_), channel_id=1, source_target_pairs={{0,1},{1,0},{2,3},{3,2},{4,5},{5,4},{6,7},{7,6},{8,9},{9,8},{10,11... | collective-permute-start | bytes 1720328 | tf_op jit(solution)/shard_map/ppermute | solution.py:483
  116.6 33.6 %copy-start.3 = (bf16[4,80,640]{2,1,0:T(8,128)(2,1)}, bf16[4,80,640]{2,1,0:T(8,128)(2,1)S(1)}, u32[]{:S(2)}) copy-start(bf16[4,80,640]{2,1,0:T(8,128)(2,1)S(1)} %pad_maximum_fusion.1.mine) | copy-start | bytes 1228804
  116.6 42.4 %collective-permute-start.26 = (bf16[4,80,640]{2,1,0:T(8,128)(2,1)S(1)}, bf16[4,80,640]{2,1,0:T(8,128)(2,1)}, u32[]{:S(2)}, u32[]{:S(2)}) collective-permute-start(bf16[4,80,640]{2,1,0:T(8,128)(2,1)S(1)} %pad_maximum_fusion.1.mine), channel_id=1, source_target_pairs={{0,1},{1,0},{2,3},{3,2},{4,5},{5,4},{6,7},{7,6},{8,9},{9,8},{10,11... | collective-permute-start | bytes 1228808 | tf_op jit(solution)/shard_map/ppermute | solution.py:482
  117.2 1.5 copy-start.7
  150.9 8.1 %collective-permute-start.25 = (f32[1,16]{1,0:T(1,128)S(1)}, f32[1,16]{1,0:T(1,128)S(1)}, u32[]{:S(2)}, u32[]{:S(2)}) collective-permute-start(f32[1,16]{1,0:T(1,128)S(1)} %slice.39), channel_id=1, source_target_pairs={{0,32},{32,64},{64,96},{96,0},{1,33},{33,65},{65,97},{97,1},{2,34}... | collective-permute-start | bytes 200 | tf_op jit(solution)/shard_map/ppermute | solution.py:422
  156.0 8.4 %collective-permute-start.32 = (f32[1,16]{1,0:T(1,128)S(1)}, f32[1,16]{1,0:T(1,128)S(1)}, u32[]{:S(2)}, u32[]{:S(2)}) collective-permute-start(f32[1,16]{1,0:T(1,128)S(1)} %slice.39), channel_id=1, source_target_pairs={{0,96},{32,0},{64,32},{96,64},{1,97},{33,1},{65,33},{97,65},{2,98}... | collective-permute-start | bytes 200 | tf_op jit(solution)/shard_map/ppermute | solution.py:422
  157.5 6.9 %collective-permute-start.31 = (f32[1,16]{1,0:T(1,128)S(1)}, f32[1,16]{1,0:T(1,128)S(1)}, u32[]{:S(2)}, u32[]{:S(2)}) collective-permute-start(f32[1,16]{1,0:T(1,128)S(1)} %slice.39), channel_id=1, source_target_pairs={{0,64},{32,96},{64,0},{96,32},{1,65},{33,97},{65,1},{97,33},{2,66}... | collective-permute-start | bytes 200 | tf_op jit(solution)/shard_map/ppermute | solution.py:422
  162.3 7.6 %collective-permute-start.29 = (bf16[104,640]{1,0:T(8,128)(2,1)}, bf16[104,640]{1,0:T(8,128)(2,1)S(1)}, u32[]{:S(2)}, u32[]{:S(2)}) collective-permute-start(bf16[104,640]{1,0:T(8,128)(2,1)} %taylor.1), channel_id=1, source_target_pairs={{0,24},{8,0},{16,8},{24,16},{1,25},{9,1},{17,9},{25,17},{2,26},{10... | collective-permute-start | bytes 399368 | tf_op jit(solution)/shard_map/ppermute | solution.py:422
  162.3 8.4 %collective-permute-start.28 = (bf16[104,640]{1,0:T(8,128)(2,1)}, bf16[104,640]{1,0:T(8,128)(2,1)S(1)}, u32[]{:S(2)}, u32[]{:S(2)}) collective-permute-start(bf16[104,640]{1,0:T(8,128)(2,1)} %taylor.1), channel_id=1, source_target_pairs={{0,16},{8,24},{16,0},{24,8},{1,17},{9,25},{17,1},{25,9},{2,18},{10... | collective-permute-start | bytes 399368 | tf_op jit(solution)/shard_map/ppermute | solution.py:422
  163.0 9.2 %collective-permute-start.27 = (bf16[104,640]{1,0:T(8,128)(2,1)}, bf16[104,640]{1,0:T(8,128)(2,1)S(1)}, u32[]{:S(2)}, u32[]{:S(2)}) collective-permute-start(bf16[104,640]{1,0:T(8,128)(2,1)} %taylor.1), channel_id=1, source_target_pairs={{0,8},{8,16},{16,24},{24,0},{1,9},{9,17},{17,25},{25,1},{2,10},{10... | collective-permute-start | bytes 399368 | tf_op jit(solution)/shard_map/ppermute | solution.py:422
  165.1 1.1 collective-permute-start.33
  166.2 7.1 %collective-permute-start.36 = (f32[1,16]{1,0:T(1,128)S(1)}, f32[1,16]{1,0:T(1,128)S(1)}, u32[]{:S(2)}, u32[]{:S(2)}) collective-permute-start(f32[1,16]{1,0:T(1,128)S(1)} %add.121), channel_id=1, source_target_pairs={{0,6},{2,0},{4,2},{6,4},{1,7},{3,1},{5,3},{7,5},{8,14},{10,8},{12,... | collective-permute-start | bytes 200 | tf_op jit(solution)/shard_map/ppermute | solution.py:422
  169.9 5.0 %collective-permute-start.35 = (f32[1,16]{1,0:T(1,128)S(1)}, f32[1,16]{1,0:T(1,128)S(1)}, u32[]{:S(2)}, u32[]{:S(2)}) collective-permute-start(f32[1,16]{1,0:T(1,128)S(1)} %add.121), channel_id=1, source_target_pairs={{0,4},{2,6},{4,0},{6,2},{1,5},{3,7},{5,1},{7,3},{8,12},{10,14},{12... | collective-permute-start | bytes 200 | tf_op jit(solution)/shard_map/ppermute | solution.py:422
  169.9 5.0 %collective-permute-start.34 = (f32[1,16]{1,0:T(1,128)S(1)}, f32[1,16]{1,0:T(1,128)S(1)}, u32[]{:S(2)}, u32[]{:S(2)}) collective-permute-start(f32[1,16]{1,0:T(1,128)S(1)} %add.121), channel_id=1, source_target_pairs={{0,2},{2,4},{4,6},{6,0},{1,3},{3,5},{5,7},{7,1},{8,10},{10,12},{12... | collective-permute-start | bytes 200 | tf_op jit(solution)/shard_map/ppermute | solution.py:422
  173.2 11.4 %copy-start.2 = (bf16[4,104,640]{2,1,0:T(8,128)(2,1)}, bf16[4,104,640]{2,1,0:T(8,128)(2,1)S(1)}, u32[]{:S(2)}) copy-start(bf16[4,104,640]{2,1,0:T(8,128)(2,1)S(1)} %pad_maximum_fusion.mine) | copy-start | bytes 1597444
  173.2 11.4 %collective-permute-start.30 = (bf16[4,104,640]{2,1,0:T(8,128)(2,1)S(1)}, bf16[4,104,640]{2,1,0:T(8,128)(2,1)S(1)}, u32[]{:S(2)}, u32[]{:S(2)}) collective-permute-start(bf16[4,104,640]{2,1,0:T(8,128)(2,1)S(1)} %pad_maximum_fusion.mine), channel_id=1, source_target_pairs={{0,1},{1,0},{2,3},{3,2},{4,5},{5,4},{6,7},{7,6},{8,9},{9,8},{10,11... | collective-permute-start | bytes 1597448 | tf_op jit(solution)/shard_map/ppermute | solution.py:490
  175.0 5.6 %collective-permute-start.39 = (f32[1,16]{1,0:T(1,128)S(1)}, f32[1,16]{1,0:T(1,128)S(1)}, u32[]{:S(2)}, u32[]{:S(2)}) collective-permute-start(f32[1,16]{1,0:T(1,128)S(1)} %add_add_fusion.1), channel_id=1, source_target_pairs={{0,24},{8,0},{16,8},{24,16},{1,25},{9,1},{17,9},{25,17},{2,26},{10... | collective-permute-start | bytes 200 | tf_op jit(solution)/shard_map/ppermute | solution.py:422
  177.7 5.0 %collective-permute-start.38 = (f32[1,16]{1,0:T(1,128)S(1)}, f32[1,16]{1,0:T(1,128)S(1)}, u32[]{:S(2)}, u32[]{:S(2)}) collective-permute-start(f32[1,16]{1,0:T(1,128)S(1)} %add_add_fusion.1), channel_id=1, source_target_pairs={{0,16},{8,24},{16,0},{24,8},{1,17},{9,25},{17,1},{25,9},{2,18},{10... | collective-permute-start | bytes 200 | tf_op jit(solution)/shard_map/ppermute | solution.py:422
  179.2 4.8 %collective-permute-start.37 = (f32[1,16]{1,0:T(1,128)S(1)}, f32[1,16]{1,0:T(1,128)S(1)}, u32[]{:S(2)}, u32[]{:S(2)}) collective-permute-start(f32[1,16]{1,0:T(1,128)S(1)} %add_add_fusion.1), channel_id=1, source_target_pairs={{0,8},{8,16},{16,24},{24,0},{1,9},{9,17},{17,25},{25,1},{2,10},{10... | collective-permute-start | bytes 200 | tf_op jit(solution)/shard_map/ppermute | solution.py:422
  184.6 0.8 copy-start.8

commit v4 on v3

--- a/solution.py
+++ b/solution.py
@@ -189,7 +189,7 @@
     pair = thetas[0].shape[0]
     walkers = n * pair
     lanes = 32
-    block = 14
+    block = 28
     return pl.pallas_call(
         functools.partial(bias_kernel, n),
         out_shape=jax.ShapeDtypeStruct((walkers, 2 * n_vec), F32),

time: 188 us -> 188 us (level)
  no operation moved by 1% of the time
where the time goes in v4:
time: 188 us; the launch traced here: 187 us
  starting transfers between devices  62.4 us (33%)
  Pallas kernels  62.3 us (33%)
  waiting for transfers between devices  41.3 us (22%)
  blocking collectives  11.3 us (6%)
  other arithmetic  5.31 us (3%)
  local copies, waits for them, and re-layouts  3.7 us (2%)
    ppermute x25, starting transfers between devices, along(): return lax.ppermute(v, axis, shift(n, k)) if k else v  46.3 us
    ppermute x25, waiting for transfers between devices, along(): return lax.ppermute(v, axis, shift(n, k)) if k else v  34.9 us
    pallas_call x1, Pallas kernels, make_cross(): pl.pallas_call(functools.partial(cross_kernel, n, pair), out_shape=jax.Sh...  31.6 us
    psum x1, blocking collectives, shards(): near = lax.psum(share, 'x')  11.3 us
    pallas_call x1, Pallas kernels, make_potential(): pl.pallas_call(functools.partial(potential_kernel, n), out_shape=[jax.Sha...  10 us
    pallas_call x1, Pallas kernels, make_theta(): pl.pallas_call(functools.partial(theta_kernel, n, quarter), out_shape=[ja...  8.4 us
    pallas_call x1, Pallas kernels, make_bias(): pl.pallas_call(functools.partial(bias_kernel, n), out_shape=jax.ShapeDtyp...  6.76 us
    ppermute x4, starting transfers between devices, shards(): lax.ppermute(piece, ('x', 'z'), [(n * a + b, n * ((b - a) % n) + (b + k)...  5.19 us
  transfers between devices with their start and end apart: 42, of which 18 were waited for; matrix products, arithmetic and copies ran while one was open for 4% of the time, Pallas kernels for 32%

profile of v4, /device:TPU:0, one launch (start us, length us, event | category | flops | bytes accessed | tf_op | source)
XLA Modules:
  0.0 187.3 jit_solution(10340932430040704736)
XLA Ops:
  0.7 0.5 collective-permute-start.1
  1.2 0.8 select_reduce_fusion
  2.3 0.6 concatenate.6.place
  3.0 8.4 %theta.1 = (bf16[2,160,200]{2,1,0:T(8,128)(2,1)}, bf16[2,160,200]{2,1,0:T(8,128)(2,1)}, bf16[2,160,200]{2,1,0:T(8,128)(2,1)}, bf16[2,160,200]{2,1,0:T(8,128)(2,1)}, bf16[4,216,640]{2,1,0:T(8,128)(2,1)}) custom-call(s32[8]{0:T(128)} %concatenate.6.place, bf16[200,640]{1,0:T(8,128)(2,1)} %bitcast.42, bf16[4,200,640]{2,1,0:T(8,128)(2,1)} %bitcast.41), custom_call_target="tpu_custom_call" | custom-call | flops 8739999744 | bytes 1 | tf_op jit(solution)/shard_map/theta/pallas_call | solution.py:109
  11.6 1.6 collective-permute-start.2
  13.1 2.7 %collective-permute-start.3 = (bf16[2,160,200]{2,1,0:T(8,128)(2,1)}, bf16[2,160,200]{2,1,0:T(8,128)(2,1)S(1)}, u32[]{:S(2)}, u32[]{:S(2)}) collective-permute-start(bf16[2,160,200]{2,1,0:T(8,128)(2,1)} %get-tuple-element.27), channel_id=1, source_target_pairs={{0,64},{32,96},{64,0},{96,32},{1,65},{33,97},{65,1},{97,33},{2,66}... | collective-permute-start | bytes 384008 | tf_op jit(solution)/shard_map/ppermute | solution.py:422
  15.9 1.4 collective-permute-start.4
  17.3 2.2 %collective-permute-done.2.rest_1_ = bf16[2,160,200]{2,1,0:T(8,128)(2,1)S(1)} collective-permute-done((bf16[2,160,200]{2,1,0:T(8,128)(2,1)}, bf16[2,160,200]{2,1,0:T(8,128)(2,1)S(1)}, u32[]{:S(2)}, u32[]{:S(2)}) %collective-permute-start.2) | collective-permute-done | bytes 128032 | tf_op jit(solution)/shard_map/ppermute | solution.py:422
  19.5 4.6 %collective-permute-done.3.rest_2_ = bf16[2,160,200]{2,1,0:T(8,128)(2,1)S(1)} collective-permute-done((bf16[2,160,200]{2,1,0:T(8,128)(2,1)}, bf16[2,160,200]{2,1,0:T(8,128)(2,1)S(1)}, u32[]{:S(2)}, u32[]{:S(2)}) %collective-permute-start.3) | collective-permute-done | bytes 128032 | tf_op jit(solution)/shard_map/ppermute | solution.py:422
  24.1 3.9 %all-to-all-start = ((bf16[4,216,640]{2,1,0:T(8,128)(2,1)}), bf16[4,216,640]{2,1,0:T(8,128)(2,1)S(1)}, u32[]{:S(2)}, u32[]{:S(2)}) async-start(bf16[4,216,640]{2,1,0:T(8,128)(2,1)} %get-tuple-element.38), calls=%async_computation | async-start | bytes 2211840 | tf_op jit(solution)/shard_map/all_to_all | solution.py:439
  28.0 6.8 %bias.1 = f32[8,112]{1,0:T(8,128)} custom-call(s32[8]{0:T(128)} %concatenate.6.place, bf16[56,160,200]{2,1,0:T(8,128)(2,1)} %mine.2, bf16[56,160,200]{2,1,0:T(8,128)(2,1)} %collective-permute-done.theirs, f32[4,56]{1,0:T(4,128)} %noise_mine.3, f32[4,56]{1,0:T(4,128)} %copy-done.13, bf16[2,160,200]{2,1,0:T(8,128)(2,1)} %get-tuple-element.23.rest_0_, ...), custom_call_target="tpu_custom_call" | custom-call | flops 11500000 | bytes 1 | tf_op jit(solution)/shard_map/bias/pallas_call | solution.py:193
  34.8 11.3 %psum.7.near = f32[8,112]{1,0:T(8,128)S(1)} all-reduce(f32[8,112]{1,0:T(8,128)} %bias.1), channel_id=1, replica_groups=mesh['x'=4,'y'=4,'z'=4,'core'=2] {'x'}, use_global_device_ids=true, to_apply=%region_3.4 | all-reduce | flops 896 | bytes 7168 | tf_op jit(solution)/shard_map/psum | solution.py:443
  46.2 5.0 %all-to-all-start.1 = ((bf16[4,14,160,200]{3,2,1,0:T(8,128)(2,1)}), bf16[4,14,160,200]{3,2,1,0:T(8,128)(2,1)}, u32[]{:S(2)}, u32[]{:S(2)}) async-start(bf16[4,14,160,200]{3,2,1,0:T(8,128)(2,1)} %bitcast.31), calls=%async_computation.1 | async-start | bytes 9175040 | tf_op jit(solution)/shard_map/all_to_all | solution.py:447
  51.2 0.7 gather_fusion
  52.0 0.7 compare_convert_fusion
  52.7 0.5 collective-permute-done.5.far
  53.2 0.6 copy-done.14
  53.8 10.0 %potential.1 = (bf16[4,80,640]{2,1,0:T(8,128)(2,1)}, bf16[4,80,640]{2,1,0:T(8,128)(2,1)}, bf16[4,80,640]{2,1,0:T(8,128)(2,1)}, bf16[4,80,640]{2,1,0:T(8,128)(2,1)}, f32[8,16]{1,0:T(8,128)}) custom-call(s32[8]{0:T(128)} %concatenate.6.place, f32[8,112]{1,0:T(8,128)} %copy-done.12, f32[8,112]{1,0:T(8,128)} %copy-done.14, f32[4,56]{1,0:T(4,128)} %noise_mine.3, ...), custom_call_target="tpu_custom_call" | custom-call | flops 11500000 | bytes 1 | tf_op jit(solution)/shard_map/potential/pallas_call | solution.py:261
  63.8 3.1 %collective-permute-start.9 = (bf16[4,80,640]{2,1,0:T(8,128)(2,1)}, bf16[4,80,640]{2,1,0:T(8,128)(2,1)S(1)}, u32[]{:S(2)}, u32[]{:S(2)}) collective-permute-start(bf16[4,80,640]{2,1,0:T(8,128)(2,1)} %get-tuple-element.35), channel_id=1, source_target_pairs={{0,24},{8,0},{16,8},{24,16},{1,25},{9,1},{17,9},{25,17},{2,26},{10... | collective-permute-start | bytes 1228808 | tf_op jit(solution)/shard_map/ppermute | solution.py:422
  66.9 0.6 collective-permute-start.8
  67.5 1.0 collective-permute-start.7
  68.5 2.0 %collective-permute-start.17 = (bf16[4,112,640]{2,1,0:T(8,128)(2,1)S(1)}, bf16[4,112,640]{2,1,0:T(8,128)(2,1)S(1)}, u32[]{:S(2)}, u32[]{:S(2)}) collective-permute-start(bf16[4,112,640]{2,1,0:T(8,128)(2,1)S(1)} %slice.36.rest_0_), channel_id=1, source_target_pairs={{0,2},{2,4},{4,6},{6,0},{1,3},{3,5},{5,7},{7,1},{8,10},{10,12},{12... | collective-permute-start | bytes 1720328 | tf_op jit(solution)/shard_map/ppermute | solution.py:422
  70.5 2.2 %collective-permute-start.19 = (bf16[4,112,640]{2,1,0:T(8,128)(2,1)S(1)}, bf16[4,112,640]{2,1,0:T(8,128)(2,1)S(1)}, u32[]{:S(2)}, u32[]{:S(2)}) collective-permute-start(bf16[4,112,640]{2,1,0:T(8,128)(2,1)S(1)} %slice.36.rest_0_), channel_id=1, source_target_pairs={{0,6},{2,0},{4,2},{6,4},{1,7},{3,1},{5,3},{7,5},{8,14},{10,8},{12,... | collective-permute-start | bytes 1720328 | tf_op jit(solution)/shard_map/ppermute | solution.py:422
  72.7 12.3 %collective-permute-done.9 = bf16[4,80,640]{2,1,0:T(8,128)(2,1)S(1)} collective-permute-done((bf16[4,80,640]{2,1,0:T(8,128)(2,1)}, bf16[4,80,640]{2,1,0:T(8,128)(2,1)S(1)}, u32[]{:S(2)}, u32[]{:S(2)}) %collective-permute-start.9) | collective-permute-done | bytes 409632 | tf_op jit(solution)/shard_map/ppermute | solution.py:422
  85.0 3.6 %collective-permute-done.7 = bf16[4,80,640]{2,1,0:T(8,128)(2,1)S(1)} collective-permute-done((bf16[4,80,640]{2,1,0:T(8,128)(2,1)}, bf16[4,80,640]{2,1,0:T(8,128)(2,1)S(1)}, u32[]{:S(2)}, u32[]{:S(2)}) %collective-permute-start.7) | collective-permute-done | bytes 409632 | tf_op jit(solution)/shard_map/ppermute | solution.py:422
  88.6 1.2 add_convert_fusion
  89.9 4.1 %collective-permute-start.12 = (bf16[80,640]{1,0:T(8,128)(2,1)S(1)}, bf16[80,640]{1,0:T(8,128)(2,1)S(1)}, u32[]{:S(2)}, u32[]{:S(2)}) collective-permute-start(bf16[80,640]{1,0:T(8,128)(2,1)S(1)} %get-tuple-element.45), channel_id=1, source_target_pairs={{0,6},{2,0},{4,2},{6,4},{1,7},{3,1},{5,3},{7,5},{8,14},{10,8},{12,... | collective-permute-start | bytes 307208 | tf_op jit(solution)/shard_map/ppermute | solution.py:422
  94.0 1.2 collective-permute-start.10
  95.3 2.3 %collective-permute-start.18 = (bf16[2,112,640]{2,1,0:T(8,128)(2,1)S(1)}, bf16[2,112,640]{2,1,0:T(8,128)(2,1)S(1)}, u32[]{:S(2)}, u32[]{:S(2)}) collective-permute-start(bf16[2,112,640]{2,1,0:T(8,128)(2,1)S(1)} %slice.46), channel_id=1, source_target_pairs={{0,2},{2,4},{4,6},{6,0},{1,3},{3,5},{5,7},{7,1},{8,10},{10,12},{12... | collective-permute-start | bytes 860168 | tf_op jit(solution)/shard_map/ppermute | solution.py:422
  97.6 1.0 collective-permute-done.12
  98.6 3.7 %collective-permute-start.20 = (bf16[2,112,640]{2,1,0:T(8,128)(2,1)S(1)}, bf16[2,112,640]{2,1,0:T(8,128)(2,1)S(1)}, u32[]{:S(2)}, u32[]{:S(2)}) collective-permute-start(bf16[2,112,640]{2,1,0:T(8,128)(2,1)S(1)} %slice.47), channel_id=1, source_target_pairs={{0,6},{2,0},{4,2},{6,4},{1,7},{3,1},{5,3},{7,5},{8,14},{10,8},{12,... | collective-permute-start | bytes 860168 | tf_op jit(solution)/shard_map/ppermute | solution.py:422
  102.5 1.7 collective-permute-start.16
  104.1 2.9 %collective-permute-start.15 = (bf16[80,640]{1,0:T(8,128)(2,1)S(1)}, bf16[80,640]{1,0:T(8,128)(2,1)S(1)}, u32[]{:S(2)}, u32[]{:S(2)}) collective-permute-start(bf16[80,640]{1,0:T(8,128)(2,1)S(1)} %fusion.2), channel_id=1, source_target_pairs={{0,4},{2,38},{4,64},{6,98},{32,100},{34,6},{36,32},{38,66},{64,68}... | collective-permute-start | bytes 307208 | tf_op jit(solution)/shard_map/ppermute | solution.py:474
  107.0 1.1 collective-permute-done.18
  108.2 3.4 %collective-permute-done.20 = bf16[2,112,640]{2,1,0:T(8,128)(2,1)S(1)} collective-permute-done((bf16[2,112,640]{2,1,0:T(8,128)(2,1)S(1)}, bf16[2,112,640]{2,1,0:T(8,128)(2,1)S(1)}, u32[]{:S(2)}, u32[]{:S(2)}) %collective-permute-start.20) | collective-permute-done | bytes 286752 | tf_op jit(solution)/shard_map/ppermute | solution.py:422
  111.6 0.7 collective-permute-start.13
  112.3 0.3 collective-permute-done.16
  112.7 0.5 collective-permute-start.24
  113.2 3.0 %collective-permute-done.14 = bf16[80,640]{1,0:T(8,128)(2,1)S(1)} collective-permute-done((bf16[80,640]{1,0:T(8,128)(2,1)S(1)}, bf16[80,640]{1,0:T(8,128)(2,1)S(1)}, u32[]{:S(2)}, u32[]{:S(2)}) %collective-permute-start.14) | collective-permute-done | bytes 102432 | tf_op jit(solution)/shard_map/ppermute | solution.py:474
  116.2 0.6 collective-permute-start.26
  116.8 1.4 collective-permute-done.23.rest_6_
  118.3 31.6 %cross.1 = f32[8,16]{1,0:T(8,128)} custom-call(s32[8]{0:T(128)} %concatenate.6.place, f32[8,16]{1,0:T(8,128)} %get-tuple-element.36.before, bf16[4,112,640]{2,1,0:T(8,128)(2,1)} %copy-done.1, bf16[4,112,640]{2,1,0:T(8,128)(2,1)} %copy-done.4, bf16[4,112,640]{2,1,0:T(8,128)(2,1)} %copy-done.6, bf16[4,112,640]{2,1,0:T(8,128)(2,1)} %copy-done.5, ...), custom_call_target="tpu_custom_call" | custom-call | flops 575000000 | bytes 1 | tf_op jit(solution)/shard_map/cross/pallas_call | solution.py:334
  149.9 0.7 slice.39
  150.5 5.2 %collective-permute-start.25 = (f32[1,16]{1,0:T(1,128)S(1)}, f32[1,16]{1,0:T(1,128)S(1)}, u32[]{:S(2)}, u32[]{:S(2)}) collective-permute-start(f32[1,16]{1,0:T(1,128)S(1)} %slice.39), channel_id=1, source_target_pairs={{0,32},{32,64},{64,96},{96,0},{1,33},{33,65},{65,97},{97,1},{2,34}... | collective-permute-start | bytes 200 | tf_op jit(solution)/shard_map/ppermute | solution.py:422
  155.7 1.4 collective-permute-start.32
  157.1 1.5 collective-permute-start.31
  158.6 3.3 %taylor.1 = bf16[104,640]{1,0:T(8,128)(2,1)} custom-call(s32[8]{0:T(128)} %concatenate.6.place, bf16[4,216,640]{2,1,0:T(8,128)(2,1)} %copy-done, bf16[4,80,640]{2,1,0:T(8,128)(2,1)} %copy-done.3, bf16[4,80,640]{2,1,0:T(8,128)(2,1)} %collective-permute-done.26.theirs), custom_call_target="tpu_custom_call" | custom-call | flops 11500000 | bytes 1 | tf_op jit(solution)/shard_map/taylor/pallas_call | solution.py:372
  162.0 0.6 collective-permute-start.28
  162.6 1.4 collective-permute-start.27
  164.0 0.7 add_add_fusion.2
  164.7 1.1 collective-permute-done.33
  165.8 3.7 %collective-permute-start.36 = (f32[1,16]{1,0:T(1,128)S(1)}, f32[1,16]{1,0:T(1,128)S(1)}, u32[]{:S(2)}, u32[]{:S(2)}) collective-permute-start(f32[1,16]{1,0:T(1,128)S(1)} %add.121), channel_id=1, source_target_pairs={{0,6},{2,0},{4,2},{6,4},{1,7},{3,1},{5,3},{7,5},{8,14},{10,8},{12,... | collective-permute-start | bytes 200 | tf_op jit(solution)/shard_map/ppermute | solution.py:422
  169.5 0.9 collective-permute-start.34
  170.4 1.4 collective-permute-done.27
  171.8 1.0 pad_maximum_fusion.mine
  172.9 1.6 collective-permute-done.35
  174.6 2.7 %collective-permute-start.39 = (f32[1,16]{1,0:T(1,128)S(1)}, f32[1,16]{1,0:T(1,128)S(1)}, u32[]{:S(2)}, u32[]{:S(2)}) collective-permute-start(f32[1,16]{1,0:T(1,128)S(1)} %add_add_fusion.1), channel_id=1, source_target_pairs={{0,24},{8,0},{16,8},{24,16},{1,25},{9,1},{17,9},{25,17},{2,26},{10... | collective-permute-start | bytes 200 | tf_op jit(solution)/shard_map/ppermute | solution.py:422
  177.3 1.5 collective-permute-start.38
  178.9 1.3 collective-permute-start.37
  180.2 2.2 %collective-permute-done.38 = f32[1,16]{1,0:T(1,128)S(1)} collective-permute-done((f32[1,16]{1,0:T(1,128)S(1)}, f32[1,16]{1,0:T(1,128)S(1)}, u32[]{:S(2)}, u32[]{:S(2)}) %collective-permute-start.38) | collective-permute-done | bytes 96 | tf_op jit(solution)/shard_map/ppermute | solution.py:422
  182.4 1.3 collective-permute-done.37
  183.6 0.6 multiply_bitcast_fusion
  184.2 0.8 copy-done.8
  185.0 2.3 %join.1 = bf16[4,200,640]{2,1,0:T(8,128)(2,1)} custom-call(s32[8]{0:T(128)} %concatenate.6.place, bf16[4,104,640]{2,1,0:T(8,128)(2,1)} %copy-done.2, bf16[4,104,640]{2,1,0:T(8,128)(2,1)} %copy-done.8), custom_call_target="tpu_custom_call" | custom-call | flops 11500000 | bytes 1 | tf_op jit(solution)/shard_map/join/pallas_call | solution.py:396
  (90 shorter events, 1.5 us)
Async XLA Ops:
  0.6 10.7 %collective-permute-start = (bf16[56,160,200]{2,1,0:T(8,128)(2,1)}, bf16[56,160,200]{2,1,0:T(8,128)(2,1)}, u32[]{:S(2)}, u32[]{:S(2)}) collective-permute-start(bf16[56,160,200]{2,1,0:T(8,128)(2,1)} %mine.2), channel_id=1, source_target_pairs={{0,1},{1,0},{2,3},{3,2},{4,5},{5,4},{6,7},{7,6},{8,9},{9,8},{10,11... | collective-permute-start | bytes 10752008 | tf_op jit(solution)/shard_map/ppermute | solution.py:432
  0.7 10.6 %collective-permute-start.1 = (f32[4,56]{1,0:T(4,128)}, f32[4,56]{1,0:T(4,128)S(1)}, u32[]{:S(2)}, u32[]{:S(2)}) collective-permute-start(f32[4,56]{1,0:T(4,128)} %noise_mine.3), channel_id=1, source_target_pairs={{0,1},{1,0},{2,3},{3,2},{4,5},{5,4},{6,7},{7,6},{8,9},{9,8},{10,11... | collective-permute-start | bytes 2696 | tf_op jit(solution)/shard_map/ppermute | solution.py:431
  11.4 16.7 %copy-start.13 = (f32[4,56]{1,0:T(4,128)}, f32[4,56]{1,0:T(4,128)S(1)}, u32[]{:S(2)}) copy-start(f32[4,56]{1,0:T(4,128)S(1)} %collective-permute-done.1.noise_theirs) | copy-start | bytes 2692
  11.4 41.8 %collective-permute-start.6 = (bf16[56,160,640]{2,1,0:T(8,128)(2,1)}, bf16[56,160,640]{2,1,0:T(8,128)(2,1)}, u32[]{:S(2)}, u32[]{:S(2)}) collective-permute-start(bf16[56,160,640]{2,1,0:T(8,128)(2,1)} %mine.3), channel_id=1, source_target_pairs={{0,1},{1,0},{2,3},{3,2},{4,5},{5,4},{6,7},{7,6},{8,9},{9,8},{10,11... | collective-permute-start | bytes 34406408 | tf_op jit(solution)/shard_map/ppermute | solution.py:440
  11.6 8.0 %collective-permute-start.2 = (bf16[2,160,200]{2,1,0:T(8,128)(2,1)}, bf16[2,160,200]{2,1,0:T(8,128)(2,1)S(1)}, u32[]{:S(2)}, u32[]{:S(2)}) collective-permute-start(bf16[2,160,200]{2,1,0:T(8,128)(2,1)} %get-tuple-element.25), channel_id=1, source_target_pairs={{0,32},{32,64},{64,96},{96,0},{1,33},{33,65},{65,97},{97,1},{2,34}... | collective-permute-start | bytes 384008 | tf_op jit(solution)/shard_map/ppermute | solution.py:422
  13.1 11.0 %collective-permute-start.3 = (bf16[2,160,200]{2,1,0:T(8,128)(2,1)}, bf16[2,160,200]{2,1,0:T(8,128)(2,1)S(1)}, u32[]{:S(2)}, u32[]{:S(2)}) collective-permute-start(bf16[2,160,200]{2,1,0:T(8,128)(2,1)} %get-tuple-element.27), channel_id=1, source_target_pairs={{0,64},{32,96},{64,0},{96,32},{1,65},{33,97},{65,1},{97,33},{2,66}... | collective-permute-start | bytes 384008 | tf_op jit(solution)/shard_map/ppermute | solution.py:422
  15.9 8.2 %collective-permute-start.4 = (bf16[2,160,200]{2,1,0:T(8,128)(2,1)}, bf16[2,160,200]{2,1,0:T(8,128)(2,1)S(1)}, u32[]{:S(2)}, u32[]{:S(2)}) collective-permute-start(bf16[2,160,200]{2,1,0:T(8,128)(2,1)} %get-tuple-element.29), channel_id=1, source_target_pairs={{0,96},{32,0},{64,32},{96,64},{1,97},{33,1},{65,33},{97,65},{2,98}... | collective-permute-start | bytes 384008 | tf_op jit(solution)/shard_map/ppermute | solution.py:422
  19.5 8.5 %copy-start.9 = (bf16[2,160,200]{2,1,0:T(8,128)(2,1)}, bf16[2,160,200]{2,1,0:T(8,128)(2,1)S(1)}, u32[]{:S(2)}) copy-start(bf16[2,160,200]{2,1,0:T(8,128)(2,1)S(1)} %collective-permute-done.2.rest_1_) | copy-start | bytes 384004
  24.1 3.9 %copy-start.10 = (bf16[2,160,200]{2,1,0:T(8,128)(2,1)}, bf16[2,160,200]{2,1,0:T(8,128)(2,1)S(1)}, u32[]{:S(2)}) copy-start(bf16[2,160,200]{2,1,0:T(8,128)(2,1)S(1)} %collective-permute-done.3.rest_2_) | copy-start | bytes 384004
  24.1 3.9 %copy-start.11 = (bf16[2,160,200]{2,1,0:T(8,128)(2,1)}, bf16[2,160,200]{2,1,0:T(8,128)(2,1)S(1)}, u32[]{:S(2)}) copy-start(bf16[2,160,200]{2,1,0:T(8,128)(2,1)S(1)} %collective-permute-done.4.rest_3_) | copy-start | bytes 384004
  24.1 22.0 %all-to-all-start = ((bf16[4,216,640]{2,1,0:T(8,128)(2,1)}), bf16[4,216,640]{2,1,0:T(8,128)(2,1)S(1)}, u32[]{:S(2)}, u32[]{:S(2)}) async-start(bf16[4,216,640]{2,1,0:T(8,128)(2,1)} %get-tuple-element.38), calls=%async_computation | async-start | bytes 2211840 | tf_op jit(solution)/shard_map/all_to_all | solution.py:439
  46.1 5.8 %copy-start.12 = (f32[8,112]{1,0:T(8,128)}, f32[8,112]{1,0:T(8,128)S(1)}, u32[]{:S(2)}) copy-start(f32[8,112]{1,0:T(8,128)S(1)} %psum.7.near) | copy-start | bytes 10756
  46.1 5.1 %copy-start.16 = (s32[16,1]{0,1:T(1,128)S(1)}, s32[16,1]{0,1:T(1,128)}, u32[]{:S(2)}) copy-start(s32[16,1]{0,1:T(1,128)} %constant.59) | copy-start | bytes 196
  46.1 5.1 %copy-start.17 = (s32[16,1]{0,1:T(1,128)S(1)}, s32[16,1]{0,1:T(1,128)}, u32[]{:S(2)}) copy-start(s32[16,1]{0,1:T(1,128)} %constant.58) | copy-start | bytes 196
  46.1 5.8 %copy-start.15 = (s32[8]{0:T(128)S(1)}, s32[8]{0:T(128)}, u32[]{:S(2)}) copy-start(s32[8]{0:T(128)} %constant.54.clone) | copy-start | bytes 100
  46.2 22.3 %copy-start = (bf16[4,216,640]{2,1,0:T(8,128)(2,1)}, bf16[4,216,640]{2,1,0:T(8,128)(2,1)S(1)}, u32[]{:S(2)}) copy-start(bf16[4,216,640]{2,1,0:T(8,128)(2,1)S(1)} %all-to-all-done.walker) | copy-start | bytes 3317764
  46.2 70.7 %all-to-all-start.1 = ((bf16[4,14,160,200]{3,2,1,0:T(8,128)(2,1)}), bf16[4,14,160,200]{3,2,1,0:T(8,128)(2,1)}, u32[]{:S(2)}, u32[]{:S(2)}) async-start(bf16[4,14,160,200]{3,2,1,0:T(8,128)(2,1)} %bitcast.31), calls=%async_computation.1 | async-start | bytes 9175040 | tf_op jit(solution)/shard_map/all_to_all | solution.py:447
  51.9 1.2 collective-permute-start.5
  53.2 0.6 copy-start.14
  63.8 21.2 %collective-permute-start.9 = (bf16[4,80,640]{2,1,0:T(8,128)(2,1)}, bf16[4,80,640]{2,1,0:T(8,128)(2,1)S(1)}, u32[]{:S(2)}, u32[]{:S(2)}) collective-permute-start(bf16[4,80,640]{2,1,0:T(8,128)(2,1)} %get-tuple-element.35), channel_id=1, source_target_pairs={{0,24},{8,0},{16,8},{24,16},{1,25},{9,1},{17,9},{25,17},{2,26},{10... | collective-permute-start | bytes 1228808 | tf_op jit(solution)/shard_map/ppermute | solution.py:422
  66.9 18.1 %collective-permute-start.8 = (bf16[4,80,640]{2,1,0:T(8,128)(2,1)}, bf16[4,80,640]{2,1,0:T(8,128)(2,1)S(1)}, u32[]{:S(2)}, u32[]{:S(2)}) collective-permute-start(bf16[4,80,640]{2,1,0:T(8,128)(2,1)} %get-tuple-element.34), channel_id=1, source_target_pairs={{0,16},{8,24},{16,0},{24,8},{1,17},{9,25},{17,1},{25,9},{2,18},{10... | collective-permute-start | bytes 1228808 | tf_op jit(solution)/shard_map/ppermute | solution.py:422
  67.5 21.1 %collective-permute-start.7 = (bf16[4,80,640]{2,1,0:T(8,128)(2,1)}, bf16[4,80,640]{2,1,0:T(8,128)(2,1)S(1)}, u32[]{:S(2)}, u32[]{:S(2)}) collective-permute-start(bf16[4,80,640]{2,1,0:T(8,128)(2,1)} %get-tuple-element.33), channel_id=1, source_target_pairs={{0,8},{8,16},{16,24},{24,0},{1,9},{9,17},{17,25},{25,1},{2,10},{10... | collective-permute-start | bytes 1228808 | tf_op jit(solution)/shard_map/ppermute | solution.py:422
  68.5 49.7 %copy-start.1 = (bf16[4,112,640]{2,1,0:T(8,128)(2,1)}, bf16[4,112,640]{2,1,0:T(8,128)(2,1)S(1)}, u32[]{:S(2)}) copy-start(bf16[4,112,640]{2,1,0:T(8,128)(2,1)S(1)} %slice.36.rest_0_) | copy-start | bytes 1720324
  68.5 26.7 %collective-permute-start.17 = (bf16[4,112,640]{2,1,0:T(8,128)(2,1)S(1)}, bf16[4,112,640]{2,1,0:T(8,128)(2,1)S(1)}, u32[]{:S(2)}, u32[]{:S(2)}) collective-permute-start(bf16[4,112,640]{2,1,0:T(8,128)(2,1)S(1)} %slice.36.rest_0_), channel_id=1, source_target_pairs={{0,2},{2,4},{4,6},{6,0},{1,3},{3,5},{5,7},{7,1},{8,10},{10,12},{12... | collective-permute-start | bytes 1720328 | tf_op jit(solution)/shard_map/ppermute | solution.py:422
  70.5 27.1 %collective-permute-start.19 = (bf16[4,112,640]{2,1,0:T(8,128)(2,1)S(1)}, bf16[4,112,640]{2,1,0:T(8,128)(2,1)S(1)}, u32[]{:S(2)}, u32[]{:S(2)}) collective-permute-start(bf16[4,112,640]{2,1,0:T(8,128)(2,1)S(1)} %slice.36.rest_0_), channel_id=1, source_target_pairs={{0,6},{2,0},{4,2},{6,4},{1,7},{3,1},{5,3},{7,5},{8,14},{10,8},{12,... | collective-permute-start | bytes 1720328 | tf_op jit(solution)/shard_map/ppermute | solution.py:422
  89.9 8.7 %collective-permute-start.12 = (bf16[80,640]{1,0:T(8,128)(2,1)S(1)}, bf16[80,640]{1,0:T(8,128)(2,1)S(1)}, u32[]{:S(2)}, u32[]{:S(2)}) collective-permute-start(bf16[80,640]{1,0:T(8,128)(2,1)S(1)} %get-tuple-element.45), channel_id=1, source_target_pairs={{0,6},{2,0},{4,2},{6,4},{1,7},{3,1},{5,3},{7,5},{8,14},{10,8},{12,... | collective-permute-start | bytes 307208 | tf_op jit(solution)/shard_map/ppermute | solution.py:422
  94.0 8.3 %collective-permute-start.11 = (bf16[80,640]{1,0:T(8,128)(2,1)S(1)}, bf16[80,640]{1,0:T(8,128)(2,1)S(1)}, u32[]{:S(2)}, u32[]{:S(2)}) collective-permute-start(bf16[80,640]{1,0:T(8,128)(2,1)S(1)} %get-tuple-element.46), channel_id=1, source_target_pairs={{0,4},{2,6},{4,0},{6,2},{1,5},{3,7},{5,1},{7,3},{8,12},{10,14},{12... | collective-permute-start | bytes 307208 | tf_op jit(solution)/shard_map/ppermute | solution.py:422
  94.0 8.4 %collective-permute-start.10 = (bf16[80,640]{1,0:T(8,128)(2,1)S(1)}, bf16[80,640]{1,0:T(8,128)(2,1)S(1)}, u32[]{:S(2)}, u32[]{:S(2)}) collective-permute-start(bf16[80,640]{1,0:T(8,128)(2,1)S(1)} %get-tuple-element.44), channel_id=1, source_target_pairs={{0,2},{2,4},{4,6},{6,0},{1,3},{3,5},{5,7},{7,1},{8,10},{10,12},{12... | collective-permute-start | bytes 307208 | tf_op jit(solution)/shard_map/ppermute | solution.py:422
  95.2 23.0 %copy-start.4 = (bf16[4,112,640]{2,1,0:T(8,128)(2,1)}, bf16[4,112,640]{2,1,0:T(8,128)(2,1)S(1)}, u32[]{:S(2)}) copy-start(bf16[4,112,640]{2,1,0:T(8,128)(2,1)S(1)} %collective-permute-done.17.rest_1_) | copy-start | bytes 1720324
  95.3 12.9 %collective-permute-start.18 = (bf16[2,112,640]{2,1,0:T(8,128)(2,1)S(1)}, bf16[2,112,640]{2,1,0:T(8,128)(2,1)S(1)}, u32[]{:S(2)}, u32[]{:S(2)}) collective-permute-start(bf16[2,112,640]{2,1,0:T(8,128)(2,1)S(1)} %slice.46), channel_id=1, source_target_pairs={{0,2},{2,4},{4,6},{6,0},{1,3},{3,5},{5,7},{7,1},{8,10},{10,12},{12... | collective-permute-start | bytes 860168 | tf_op jit(solution)/shard_map/ppermute | solution.py:422
  97.6 20.7 %copy-start.5 = (bf16[4,112,640]{2,1,0:T(8,128)(2,1)}, bf16[4,112,640]{2,1,0:T(8,128)(2,1)S(1)}, u32[]{:S(2)}) copy-start(bf16[4,112,640]{2,1,0:T(8,128)(2,1)S(1)} %collective-permute-done.19.rest_3_) | copy-start | bytes 1720324
  97.6 19.2 %collective-permute-start.21 = (bf16[4,112,640]{2,1,0:T(8,128)(2,1)S(1)}, bf16[4,112,640]{2,1,0:T(8,128)(2,1)S(1)}, u32[]{:S(2)}, u32[]{:S(2)}) collective-permute-start(bf16[4,112,640]{2,1,0:T(8,128)(2,1)S(1)} %slice.36.rest_0_), channel_id=1, source_target_pairs={{0,1},{1,0},{2,3},{3,2},{4,5},{5,4},{6,7},{7,6},{8,9},{9,8},{10,11... | collective-permute-start | bytes 1720328 | tf_op jit(solution)/shard_map/ppermute | solution.py:483
  98.6 13.0 %collective-permute-start.20 = (bf16[2,112,640]{2,1,0:T(8,128)(2,1)S(1)}, bf16[2,112,640]{2,1,0:T(8,128)(2,1)S(1)}, u32[]{:S(2)}, u32[]{:S(2)}) collective-permute-start(bf16[2,112,640]{2,1,0:T(8,128)(2,1)S(1)} %slice.47), channel_id=1, source_target_pairs={{0,6},{2,0},{4,2},{6,4},{1,7},{3,1},{5,3},{7,5},{8,14},{10,8},{12,... | collective-permute-start | bytes 860168 | tf_op jit(solution)/shard_map/ppermute | solution.py:422
  102.5 10.2 %collective-permute-start.16 = (bf16[80,640]{1,0:T(8,128)(2,1)S(1)}, bf16[80,640]{1,0:T(8,128)(2,1)S(1)}, u32[]{:S(2)}, u32[]{:S(2)}) collective-permute-start(bf16[80,640]{1,0:T(8,128)(2,1)S(1)} %fusion.2), channel_id=1, source_target_pairs={{0,6},{2,32},{4,66},{6,100},{32,102},{34,0},{36,34},{38,68},{64,70... | collective-permute-start | bytes 307208 | tf_op jit(solution)/shard_map/ppermute | solution.py:474
  104.1 8.6 %collective-permute-start.15 = (bf16[80,640]{1,0:T(8,128)(2,1)S(1)}, bf16[80,640]{1,0:T(8,128)(2,1)S(1)}, u32[]{:S(2)}, u32[]{:S(2)}) collective-permute-start(bf16[80,640]{1,0:T(8,128)(2,1)S(1)} %fusion.2), channel_id=1, source_target_pairs={{0,4},{2,38},{4,64},{6,98},{32,100},{34,6},{36,32},{38,66},{64,68}... | collective-permute-start | bytes 307208 | tf_op jit(solution)/shard_map/ppermute | solution.py:474
  108.2 8.0 %collective-permute-start.14 = (bf16[80,640]{1,0:T(8,128)(2,1)S(1)}, bf16[80,640]{1,0:T(8,128)(2,1)S(1)}, u32[]{:S(2)}, u32[]{:S(2)}) collective-permute-start(bf16[80,640]{1,0:T(8,128)(2,1)S(1)} %fusion.2), channel_id=1, source_target_pairs={{0,2},{2,36},{4,70},{6,96},{32,98},{34,4},{36,38},{38,64},{64,66},... | collective-permute-start | bytes 307208 | tf_op jit(solution)/shard_map/ppermute | solution.py:474
  111.6 4.5 %collective-permute-start.13 = (bf16[80,640]{1,0:T(8,128)(2,1)S(1)}, bf16[80,640]{1,0:T(8,128)(2,1)S(1)}, u32[]{:S(2)}, u32[]{:S(2)}) collective-permute-start(bf16[80,640]{1,0:T(8,128)(2,1)S(1)} %fusion.2), channel_id=1, source_target_pairs={{0,0},{2,34},{4,68},{6,102},{32,96},{34,2},{36,36},{38,70},{64,64}... | collective-permute-start | bytes 307208 | tf_op jit(solution)/shard_map/ppermute | solution.py:474
  112.3 5.9 %copy-start.6 = (bf16[4,112,640]{2,1,0:T(8,128)(2,1)}, bf16[4,112,640]{2,1,0:T(8,128)(2,1)S(1)}, u32[]{:S(2)}) copy-start(bf16[4,112,640]{2,1,0:T(8,128)(2,1)S(1)} %constant_dynamic-update-slice_fusion.rest_2_) | copy-start | bytes 1720324
  112.7 4.2 %collective-permute-start.22 = (bf16[4,112,640]{2,1,0:T(8,128)(2,1)S(1)}, bf16[4,112,640]{2,1,0:T(8,128)(2,1)}, u32[]{:S(2)}, u32[]{:S(2)}) collective-permute-start(bf16[4,112,640]{2,1,0:T(8,128)(2,1)S(1)} %collective-permute-done.17.rest_1_), channel_id=1, source_target_pairs={{0,1},{1,0},{2,3},{3,2},{4,5},{5,4},{6,7},{7,6},{8,9},{9,8},{10,11... | collective-permute-start | bytes 1720328 | tf_op jit(solution)/shard_map/ppermute | solution.py:483
  112.7 4.1 %collective-permute-start.24 = (bf16[4,112,640]{2,1,0:T(8,128)(2,1)S(1)}, bf16[4,112,640]{2,1,0:T(8,128)(2,1)}, u32[]{:S(2)}, u32[]{:S(2)}) collective-permute-start(bf16[4,112,640]{2,1,0:T(8,128)(2,1)S(1)} %collective-permute-done.19.rest_3_), channel_id=1, source_target_pairs={{0,1},{1,0},{2,3},{3,2},{4,5},{5,4},{6,7},{7,6},{8,9},{9,8},{10,11... | collective-permute-start | bytes 1720328 | tf_op jit(solution)/shard_map/ppermute | solution.py:483
  116.1 2.1 %collective-permute-start.23 = (bf16[4,112,640]{2,1,0:T(8,128)(2,1)S(1)}, bf16[4,112,640]{2,1,0:T(8,128)(2,1)}, u32[]{:S(2)}, u32[]{:S(2)}) collective-permute-start(bf16[4,112,640]{2,1,0:T(8,128)(2,1)S(1)} %constant_dynamic-update-slice_fusion.rest_2_), channel_id=1, source_target_pairs={{0,1},{1,0},{2,3},{3,2},{4,5},{5,4},{6,7},{7,6},{8,9},{9,8},{10,11... | collective-permute-start | bytes 1720328 | tf_op jit(solution)/shard_map/ppermute | solution.py:483
  116.2 33.6 %copy-start.3 = (bf16[4,80,640]{2,1,0:T(8,128)(2,1)}, bf16[4,80,640]{2,1,0:T(8,128)(2,1)S(1)}, u32[]{:S(2)}) copy-start(bf16[4,80,640]{2,1,0:T(8,128)(2,1)S(1)} %pad_maximum_fusion.1.mine) | copy-start | bytes 1228804
  116.2 42.4 %collective-permute-start.26 = (bf16[4,80,640]{2,1,0:T(8,128)(2,1)S(1)}, bf16[4,80,640]{2,1,0:T(8,128)(2,1)}, u32[]{:S(2)}, u32[]{:S(2)}) collective-permute-start(bf16[4,80,640]{2,1,0:T(8,128)(2,1)S(1)} %pad_maximum_fusion.1.mine), channel_id=1, source_target_pairs={{0,1},{1,0},{2,3},{3,2},{4,5},{5,4},{6,7},{7,6},{8,9},{9,8},{10,11... | collective-permute-start | bytes 1228808 | tf_op jit(solution)/shard_map/ppermute | solution.py:482
  116.8 1.5 copy-start.7
  150.5 8.1 %collective-permute-start.25 = (f32[1,16]{1,0:T(1,128)S(1)}, f32[1,16]{1,0:T(1,128)S(1)}, u32[]{:S(2)}, u32[]{:S(2)}) collective-permute-start(f32[1,16]{1,0:T(1,128)S(1)} %slice.39), channel_id=1, source_target_pairs={{0,32},{32,64},{64,96},{96,0},{1,33},{33,65},{65,97},{97,1},{2,34}... | collective-permute-start | bytes 200 | tf_op jit(solution)/shard_map/ppermute | solution.py:422
  155.7 8.3 %collective-permute-start.32 = (f32[1,16]{1,0:T(1,128)S(1)}, f32[1,16]{1,0:T(1,128)S(1)}, u32[]{:S(2)}, u32[]{:S(2)}) collective-permute-start(f32[1,16]{1,0:T(1,128)S(1)} %slice.39), channel_id=1, source_target_pairs={{0,96},{32,0},{64,32},{96,64},{1,97},{33,1},{65,33},{97,65},{2,98}... | collective-permute-start | bytes 200 | tf_op jit(solution)/shard_map/ppermute | solution.py:422
  157.1 6.9 %collective-permute-start.31 = (f32[1,16]{1,0:T(1,128)S(1)}, f32[1,16]{1,0:T(1,128)S(1)}, u32[]{:S(2)}, u32[]{:S(2)}) collective-permute-start(f32[1,16]{1,0:T(1,128)S(1)} %slice.39), channel_id=1, source_target_pairs={{0,64},{32,96},{64,0},{96,32},{1,65},{33,97},{65,1},{97,33},{2,66}... | collective-permute-start | bytes 200 | tf_op jit(solution)/shard_map/ppermute | solution.py:422
  162.0 7.6 %collective-permute-start.29 = (bf16[104,640]{1,0:T(8,128)(2,1)}, bf16[104,640]{1,0:T(8,128)(2,1)S(1)}, u32[]{:S(2)}, u32[]{:S(2)}) collective-permute-start(bf16[104,640]{1,0:T(8,128)(2,1)} %taylor.1), channel_id=1, source_target_pairs={{0,24},{8,0},{16,8},{24,16},{1,25},{9,1},{17,9},{25,17},{2,26},{10... | collective-permute-start | bytes 399368 | tf_op jit(solution)/shard_map/ppermute | solution.py:422
  162.0 8.4 %collective-permute-start.28 = (bf16[104,640]{1,0:T(8,128)(2,1)}, bf16[104,640]{1,0:T(8,128)(2,1)S(1)}, u32[]{:S(2)}, u32[]{:S(2)}) collective-permute-start(bf16[104,640]{1,0:T(8,128)(2,1)} %taylor.1), channel_id=1, source_target_pairs={{0,16},{8,24},{16,0},{24,8},{1,17},{9,25},{17,1},{25,9},{2,18},{10... | collective-permute-start | bytes 399368 | tf_op jit(solution)/shard_map/ppermute | solution.py:422
  162.6 9.3 %collective-permute-start.27 = (bf16[104,640]{1,0:T(8,128)(2,1)}, bf16[104,640]{1,0:T(8,128)(2,1)S(1)}, u32[]{:S(2)}, u32[]{:S(2)}) collective-permute-start(bf16[104,640]{1,0:T(8,128)(2,1)} %taylor.1), channel_id=1, source_target_pairs={{0,8},{8,16},{16,24},{24,0},{1,9},{9,17},{17,25},{25,1},{2,10},{10... | collective-permute-start | bytes 399368 | tf_op jit(solution)/shard_map/ppermute | solution.py:422
  164.7 1.1 collective-permute-start.33
  165.8 7.1 %collective-permute-start.36 = (f32[1,16]{1,0:T(1,128)S(1)}, f32[1,16]{1,0:T(1,128)S(1)}, u32[]{:S(2)}, u32[]{:S(2)}) collective-permute-start(f32[1,16]{1,0:T(1,128)S(1)} %add.121), channel_id=1, source_target_pairs={{0,6},{2,0},{4,2},{6,4},{1,7},{3,1},{5,3},{7,5},{8,14},{10,8},{12,... | collective-permute-start | bytes 200 | tf_op jit(solution)/shard_map/ppermute | solution.py:422
  169.5 5.0 %collective-permute-start.35 = (f32[1,16]{1,0:T(1,128)S(1)}, f32[1,16]{1,0:T(1,128)S(1)}, u32[]{:S(2)}, u32[]{:S(2)}) collective-permute-start(f32[1,16]{1,0:T(1,128)S(1)} %add.121), channel_id=1, source_target_pairs={{0,4},{2,6},{4,0},{6,2},{1,5},{3,7},{5,1},{7,3},{8,12},{10,14},{12... | collective-permute-start | bytes 200 | tf_op jit(solution)/shard_map/ppermute | solution.py:422
  169.5 5.0 %collective-permute-start.34 = (f32[1,16]{1,0:T(1,128)S(1)}, f32[1,16]{1,0:T(1,128)S(1)}, u32[]{:S(2)}, u32[]{:S(2)}) collective-permute-start(f32[1,16]{1,0:T(1,128)S(1)} %add.121), channel_id=1, source_target_pairs={{0,2},{2,4},{4,6},{6,0},{1,3},{3,5},{5,7},{7,1},{8,10},{10,12},{12... | collective-permute-start | bytes 200 | tf_op jit(solution)/shard_map/ppermute | solution.py:422
  172.8 11.4 %copy-start.2 = (bf16[4,104,640]{2,1,0:T(8,128)(2,1)}, bf16[4,104,640]{2,1,0:T(8,128)(2,1)S(1)}, u32[]{:S(2)}) copy-start(bf16[4,104,640]{2,1,0:T(8,128)(2,1)S(1)} %pad_maximum_fusion.mine) | copy-start | bytes 1597444
  172.8 11.4 %collective-permute-start.30 = (bf16[4,104,640]{2,1,0:T(8,128)(2,1)S(1)}, bf16[4,104,640]{2,1,0:T(8,128)(2,1)S(1)}, u32[]{:S(2)}, u32[]{:S(2)}) collective-permute-start(bf16[4,104,640]{2,1,0:T(8,128)(2,1)S(1)} %pad_maximum_fusion.mine), channel_id=1, source_target_pairs={{0,1},{1,0},{2,3},{3,2},{4,5},{5,4},{6,7},{7,6},{8,9},{9,8},{10,11... | collective-permute-start | bytes 1597448 | tf_op jit(solution)/shard_map/ppermute | solution.py:490
  174.6 5.6 %collective-permute-start.39 = (f32[1,16]{1,0:T(1,128)S(1)}, f32[1,16]{1,0:T(1,128)S(1)}, u32[]{:S(2)}, u32[]{:S(2)}) collective-permute-start(f32[1,16]{1,0:T(1,128)S(1)} %add_add_fusion.1), channel_id=1, source_target_pairs={{0,24},{8,0},{16,8},{24,16},{1,25},{9,1},{17,9},{25,17},{2,26},{10... | collective-permute-start | bytes 200 | tf_op jit(solution)/shard_map/ppermute | solution.py:422
  177.3 5.0 %collective-permute-start.38 = (f32[1,16]{1,0:T(1,128)S(1)}, f32[1,16]{1,0:T(1,128)S(1)}, u32[]{:S(2)}, u32[]{:S(2)}) collective-permute-start(f32[1,16]{1,0:T(1,128)S(1)} %add_add_fusion.1), channel_id=1, source_target_pairs={{0,16},{8,24},{16,0},{24,8},{1,17},{9,25},{17,1},{25,9},{2,18},{10... | collective-permute-start | bytes 200 | tf_op jit(solution)/shard_map/ppermute | solution.py:422
  178.9 4.8 %collective-permute-start.37 = (f32[1,16]{1,0:T(1,128)S(1)}, f32[1,16]{1,0:T(1,128)S(1)}, u32[]{:S(2)}, u32[]{:S(2)}) collective-permute-start(f32[1,16]{1,0:T(1,128)S(1)} %add_add_fusion.1), channel_id=1, source_target_pairs={{0,8},{8,16},{16,24},{24,0},{1,9},{9,17},{17,25},{25,1},{2,10},{10... | collective-permute-start | bytes 200 | tf_op jit(solution)/shard_map/ppermute | solution.py:422
  184.2 0.8 copy-start.8
